TPU v7x, 32 devices: a whole 2x2x4 slice. The times are simulated.
32 devices in a mesh: space: 8 (over y, x, core), vel: 4 (over z).
Axes of the slice: x: 2, y: 2, z: 4, core: 2. Of those that a mesh axis runs over, the one named last changes fastest.
Arguments:
- dist: float32 [512, 64, 4096], P('space', None, 'vel'), as said below
- cell_kind: int32 [512, 64], P('space'), may hold values from 0 to 2, as said below
- normal_code: int32 [512, 64], P('space'), may hold values from 0 to 3
- wall_temp: float32 [512, 64], P('space'), may hold values from 0.8 to 1.25
Outputs:
- evolved: float32 [512, 64, 4096], P('space', None, 'vel')
- wall_flux: float32 [512, 64], P('space', 'vel')
Inputs may be any that keep to these rules, and one draw needn't show every extreme that they name: `cell_kind`: 0 is a gas cell, 1 a solid wall cell, 2 an evaporating meniscus cell. `normal_code`: normal into the gas: 0 rising rows, 1 falling rows, 2 rising columns, 3 falling columns; used only where cell_kind is not 0. `dist`: every population is positive.
All inputs are finite; a program needn't handle non-finite values.
Results may differ from a plain program's by a relative error of at most 0.0003.
Values sent between devices are 32-bit elements; how exact they have to be, the bound alone decides.
No kernel may reach another device: no remote copies, remote signals or barrier semaphores. Data moves between devices by JAX's collectives and lax.ppermute only.
A program may use at most 128 MiB of HBM per device.

v0:
```python
import math

import jax
import jax.numpy as jnp
from jax import lax
from jax.sharding import PartitionSpec as P

NQ = 16
STEPS = 4


LIMIT = 5.0
TIME_STEP = 0.05
SIGMA = 0.8
LATENT = 5.0
PRANDTL = 2.0 / 3.0
SHEAR_EXPONENT = 0.1


def extended_2(value, sides, width):
    for axis, dim in sides:
        size, length = (lax.axis_size(axis), value.shape[dim])
        up = [(i, (i + 1) % size) for i in range(size - 1)]
        down = [(j, i) for i, j in up]
        last = lax.slice_in_dim(value, length - width, length, axis=dim)
        leading = lax.slice_in_dim(value, 0, width, axis=dim)
        before = lax.ppermute(last, axis, up)
        after = lax.ppermute(leading, axis, down)
        value = jnp.concatenate([before, value, after], axis=dim)
    return value


def velocity_grid(points, levels):
    spacing = 2.0 * LIMIT / levels
    first = points % levels
    second = points // levels % levels
    third = points // (levels * levels)
    picks = ((first + third) % levels, (second + third) % levels, (first + second + third) % levels)
    return tuple((-LIMIT + (pick.astype(jnp.float32) + 0.5) * spacing for pick in picks))


def quad_weight(levels):
    return (2.0 * LIMIT / levels) ** 3 / (2.0 * math.pi) ** 1.5


def moment_table(speeds, weight):
    along_x, along_y, along_z = speeds
    self_product = along_x * along_x + along_y * along_y + along_z * along_z
    listed = [
        jnp.ones_like(along_x),
        along_x,
        along_y,
        along_z,
        self_product,
        along_x * along_x,
        along_y * along_y,
        along_z * along_z,
        along_x * along_y,
        along_x * along_z,
        along_y * along_z,
        along_x * self_product,
        along_y * self_product,
        along_z * self_product,
    ]
    return jnp.stack(listed) * weight


def project_moments(values, table):
    return jnp.einsum("kv,nv->kn", table, values, precision=lax.Precision.HIGHEST)


def beam_warming(padded, drift, length, axis):
    centre = lax.slice_in_dim(padded, 2, 2 + length, axis=axis)
    below = lax.slice_in_dim(padded, 1, 1 + length, axis=axis)
    below_far = lax.slice_in_dim(padded, 0, length, axis=axis)
    above = lax.slice_in_dim(padded, 3, 3 + length, axis=axis)
    above_far = lax.slice_in_dim(padded, 4, 4 + length, axis=axis)
    ahead = drift > 0
    courant = jnp.abs(drift)
    near = jnp.where(ahead, below, above)
    distant = jnp.where(ahead, below_far, above_far)
    return (
        centre
        - 0.5 * courant * (3.0 * centre - 4.0 * near + distant)
        + 0.5 * courant * courant * (centre - 2.0 * near + distant)
    )


def normal_speed(codes, speeds):
    column = codes[:, None]
    along_x = speeds[0][None, :]
    along_y = speeds[1][None, :]
    return jnp.where(
        column == 0,
        along_x,
        jnp.where(column == 1, -along_x, jnp.where(column == 2, along_y, -along_y)),
    )


def wall_mass(incident, norm, kinds, saturated):
    evaporating = jnp.where(kinds == 2.0, 1.0, 0.0)
    boundary = jnp.where(kinds > 0.0, 1.0, 0.0)
    emitted = evaporating * SIGMA * saturated + (1.0 - evaporating * SIGMA) * incident / norm
    return (emitted, boundary * (emitted * norm - incident))


def gas_state(hydrodynamic_fields):
    particle_count_field = hydrodynamic_fields[0]
    mean_drift = [
        hydrodynamic_fields[1] / particle_count_field,
        hydrodynamic_fields[2] / particle_count_field,
        hydrodynamic_fields[3] / particle_count_field,
    ]
    mean_drift_norm = (
        mean_drift[0] * mean_drift[0]
        + mean_drift[1] * mean_drift[1]
        + mean_drift[2] * mean_drift[2]
    )
    cellwise_warmth = (hydrodynamic_fields[4] / particle_count_field - mean_drift_norm) / 3.0
    flow_dot = (
        mean_drift[0] * hydrodynamic_fields[1]
        + mean_drift[1] * hydrodynamic_fields[2]
        + mean_drift[2] * hydrodynamic_fields[3]
    )
    second = [
        [hydrodynamic_fields[5], hydrodynamic_fields[8], hydrodynamic_fields[9]],
        [hydrodynamic_fields[8], hydrodynamic_fields[6], hydrodynamic_fields[10]],
        [hydrodynamic_fields[9], hydrodynamic_fields[10], hydrodynamic_fields[7]],
    ]
    thermal_current = []
    for comp in range(3):
        value = (
            hydrodynamic_fields[11 + comp]
            - 2.0
            * (
                mean_drift[0] * second[comp][0]
                + mean_drift[1] * second[comp][1]
                + mean_drift[2] * second[comp][2]
            )
            + mean_drift_norm * hydrodynamic_fields[1 + comp]
            - mean_drift[comp] * hydrodynamic_fields[4]
            + 2.0 * mean_drift[comp] * flow_dot
            - mean_drift[comp] * mean_drift_norm * particle_count_field
        )
        thermal_current.append(0.5 * value)
    return jnp.stack([particle_count_field] + mean_drift + [cellwise_warmth] + thermal_current)


def relax_shakhov(values, steam_distribution, speeds):
    (
        particle_count_field,
        mean_drift_first,
        mean_drift_second,
        mean_drift_third,
        cellwise_warmth,
        thermal_current_first,
        thermal_current_second,
        thermal_current_third,
    ) = [steam_distribution[placement_offset][:, None] for placement_offset in range(8)]
    peculiar_x = speeds[0][None, :] - mean_drift_first
    peculiar_y = speeds[1][None, :] - mean_drift_second
    peculiar_z = speeds[2][None, :] - mean_drift_third
    thermal_motion_norm = (
        peculiar_x * peculiar_x + peculiar_y * peculiar_y + peculiar_z * peculiar_z
    )
    isotropic_stress = particle_count_field * cellwise_warmth
    target_gaussian = (
        particle_count_field
        * cellwise_warmth ** (-1.5)
        * jnp.exp(-thermal_motion_norm / (2.0 * cellwise_warmth))
    )
    factor = 1.0 + (1.0 - PRANDTL) * (
        peculiar_x * thermal_current_first
        + peculiar_y * thermal_current_second
        + peculiar_z * thermal_current_third
    ) / (5.0 * isotropic_stress * cellwise_warmth) * (thermal_motion_norm / cellwise_warmth - 5.0)
    target = target_gaussian * factor
    collision_interval = SHEAR_EXPONENT * cellwise_warmth**0.72 / isotropic_stress
    return target + (values - target) * jnp.exp(-TIME_STEP / collision_interval)


def settle_state(parts):
    return gas_state(parts)


def reduce_stats(parts):
    total = lax.psum(parts, "vel")
    return settle_state(total)


def shards(dist, cell_kind, normal_code, wall_temp):
    nrows, ncols, span = dist.shape
    cell_count = nrows * ncols
    weight = quad_weight(NQ)
    points = lax.axis_index("vel") * span + jnp.arange(span, dtype=jnp.int32)
    speeds = velocity_grid(points, NQ)
    table = moment_table(speeds, weight)
    kinds = cell_kind.reshape(cell_count).astype(jnp.float32)
    facing = normal_speed(normal_code.reshape(cell_count), speeds)
    emit = (kinds[:, None] > 0.0) & (facing > 0.0)
    wall_flat = wall_temp.reshape(cell_count)
    saturated = jnp.exp(LATENT * (1.0 - 1.0 / wall_flat)) / wall_flat
    self_product = speeds[0] * speeds[0] + speeds[1] * speeds[1] + speeds[2] * speeds[2]
    wall_maxwell = wall_flat[:, None] ** (-1.5) * jnp.exp(
        -self_product[None, :] / (2.0 * wall_flat[:, None])
    )
    incoming = jnp.maximum(-facing, 0.0) * weight
    norm_part = jnp.sum(jnp.maximum(facing, 0.0) * wall_maxwell, axis=1) * weight
    emitted_part = project_moments(jnp.where(emit, wall_maxwell, 0.0), table)
    fixed_total = lax.psum(jnp.concatenate([norm_part[None, :], emitted_part], axis=0), "vel")
    current = dist
    flux = jnp.zeros((cell_count,), jnp.float32)
    for repeat in range(STEPS):
        extended = extended_2(current, (("space", 0),), 2)
        rowwise = beam_warming(extended, speeds[0] * TIME_STEP, nrows, 0)
        padded = jnp.pad(rowwise, ((0, 0), (2, 2), (0, 0)))
        flat = beam_warming(padded, speeds[1] * TIME_STEP, ncols, 1).reshape(cell_count, span)
        incident_part = jnp.sum(incoming * flat, axis=1)
        incident = lax.psum(incident_part, "vel")
        emitted, flux = wall_mass(incident, fixed_total[0], kinds, saturated)
        bounded = jnp.where(emit, emitted[:, None] * wall_maxwell, flat)
        steam_distribution = reduce_stats(project_moments(bounded, table))
        current = relax_shakhov(bounded, steam_distribution, speeds).reshape(nrows, ncols, span)
    flux_grid = flux.reshape(nrows, ncols)
    columns = ncols // lax.axis_size("vel")
    own_flux = lax.dynamic_slice_in_dim(flux_grid, lax.axis_index("vel") * columns, columns, 1)
    return (current, own_flux)


def solution(mesh):
    placed = (P("space", None, "vel"), P("space", None), P("space", None), P("space", None))
    return jax.shard_map(
        shards,
        mesh=mesh,
        in_specs=placed,
        out_specs=(P("space", None, "vel"), P("space", "vel")),
        check_vma=False,
    )
```

profile of v0, /device:TPU:4, one launch (start us, length us, event | category | flops | bytes accessed | tf_op | source)
XLA Modules:
  0.0 1123.1 jit_solution(6653378924992345718)
XLA Ops:
  7.2 1.3 fusion.210
  8.5 1.9 collective-permute-start
  10.4 4.5 collective-permute-start.1
  15.9 0.8 broadcast_compare_fusion.2
  16.7 0.8 reshape.3025
  17.8 0.8 convert_compare_fusion.1
  18.6 9.5 multiply_reduce_fusion.3
  28.3 20.8 %fusion.127 = f32[14,4096]{1,0:T(8,128)S(1)} fusion(f32[4096]{0:T(1024)S(1)} %get-tuple-element.233, f32[1024]{0:T(1024)S(1)} %get-tuple-element.237, f32[4096]{0:T(1024)S(1)} %get-tuple-element.232, f32[14,1024]{1,0:T(8,128)S(1)} %stack.2, f32[1024]{0:T(1024)S(1)} %get-tuple-element.249, f32[1024]{0:T(1024)S(1)} %get-tuple-element.235, ...), kind=kOutput, calls=%fused_computation.227 | convolution fusion | flops 738211840 | bytes 356352 | tf_op jit(solution)/shard_map/kv,nv->kn/dot_general | solution.py:69
  49.2 0.7 pad_maximum_fusion.6
  50.5 35.3 %all-reduce.10.cloned.1.call-done = f32[15,4096]{1,0:T(8,128)} async-done(((f32[15,4096]{1,0:T(8,128)}), f32[15,4096]{1,0:T(8,128)}) %all-reduce.10.cloned.1.call-update) | async-done | bytes 245776 | tf_op jit(solution)/shard_map/psum | solution.py:210
  85.7 0.9 slice.487
  86.7 0.8 constant_dynamic-update-slice_fusion.1
  87.5 17.6 %constant_dynamic-update-slice_fusion = (f32[66,64,1024]{2,1,0:T(8,128)}, f32[66,64,1024]{2,1,0:T(8,128)}) fusion(f32[66,64,1024]{2,1,0:T(8,128)} %constant_dynamic-update-slice_fusion.1, f32[64,64,1024]{2,1,0:T(8,128)} %param.4), kind=kLoop, calls=%fused_computation.363 | loop fusion | bytes 50331648 | tf_op jit(solution)/shard_map/concatenate | solution.py:29
  105.1 0.8 constant_dynamic-update-slice_fusion.2
  106.0 35.0 %multiply_add_fusion.14 = f32[64,64,1024]{2,1,0:T(8,128)} fusion(f32[64,64,1024]{2,1,0:T(8,128)} %param.4, f32[66,64,1024]{2,1,0:T(8,128)} %constant_dynamic-update-slice_fusion.2, f32[66,64,1024]{2,1,0:T(8,128)} %get-tuple-element.111, f32[1024]{0:T(1024)S(1)} %get-tuple-element.244, f32[1024]{0:T(1024)S(1)} %get-tuple-element.245, ...), kind=kLoop, calls=%fused_computation.232 | loop fusion | flops 54525952 | bytes 100672512 | tf_op jit(solution)/shard_map/add | solution.py:83
  140.9 44.6 %multiply_reduce_fusion.4 = (f32[64,64]{1,0:T(8,128)S(1)}, f32[64,64,1024]{2,1,0:T(8,128)}) fusion(f32[1024]{0:T(1024)S(1)} %get-tuple-element.249, f32[1024]{0:T(1024)S(1)} %get-tuple-element.235, f32[1024]{0:T(1024)S(1)} %get-tuple-element.248, f32[1024]{0:T(1024)S(1)} %get-tuple-element.234, pred[64,64]{1,0:T(8,128)(4,1)S(1)} %get-tuple-element.215, ...), kind=kLoop, calls=%fused_computation.230 | loop fusion | flops 88076288 | bytes 33608704 | tf_op jit(solution)/shard_map/reduce_sum | solution.py:218
  185.6 17.5 %psum.63 = f32[4096]{0:T(1024)S(1)} all-reduce(f32[4096]{0:T(1024)S(1)} %reduce_sum.54), channel_id=1, replica_groups=mesh['space'=8,'vel'=4] {'vel'}, use_global_device_ids=true, to_apply=%region_1.2 | all-reduce | flops 4096 | bytes 32768 | tf_op jit(solution)/shard_map/psum | solution.py:219
  203.2 22.6 %bitcast_select_fusion.3 = f32[4096,1024]{1,0:T(8,128)S(1)} fusion(f32[64,64,1024]{2,1,0:T(8,128)} %get-tuple-element.104, f32[4096]{0:T(1024)S(1)} %divide_add_fusion.3, f32[4096]{0:T(1024)S(1)} %get-tuple-element.233, f32[1024]{0:T(1024)S(1)} %get-tuple-element.237, f32[4096]{0:T(1024)S(1)} %get-tuple-element.232, f32[1024]{0:T(1024)S(1)} %get-tuple-element.249, ...), kind=kLoop, calls=%fused_computation.210 | loop fusion | flops 37748736 | bytes 33640448 | tf_op jit(solution)/shard_map/jit(_where)/select_n | solution.py:221
  225.8 14.7 %fusion.141 = f32[14,4096]{1,0:T(8,128)} fusion(f32[4096,1024]{1,0:T(8,128)S(1)} %bitcast_select_fusion.3, f32[14,1024]{1,0:T(8,128)S(1)} %stack.2), kind=kOutput, calls=%fused_computation.248 | convolution fusion | flops 704657408 | bytes 17063936 | tf_op jit(solution)/shard_map/kv,nv->kn/dot_general | solution.py:69
  240.6 33.5 %all-reduce.12.cloned.1.call-done = f32[14,4096]{1,0:T(8,128)} async-done(((f32[14,4096]{1,0:T(8,128)}), f32[14,4096]{1,0:T(8,128)}) %all-reduce.12.cloned.1.call-update) | async-done | bytes 229392 | tf_op jit(solution)/shard_map/psum | solution.py:187
  274.1 2.6 slice_reduce_fusion.49
  277.7 1.8 fusion.213
  279.6 48.8 %multiply_add_fusion.11 = f32[4096,1024]{1,0:T(8,128)} fusion(f32[4096]{0:T(1024)S(1)} %get-tuple-element.206, f32[4096]{0:T(1024)S(1)} %get-tuple-element.231, f32[4096]{0:T(1024)S(1)} %get-tuple-element.205, f32[4096]{0:T(1024)S(1)} %get-tuple-element.228, f32[4096]{0:T(1024)S(1)} %get-tuple-element.229, f32[4096]{0:T(1024)S(1)} %get-tuple-element.230, ...), kind=kLoop, calls=%fused_computation.225 | loop fusion | flops 146800640 | bytes 33824768 | tf_op jit(solution)/shard_map/add | solution.py:179
  328.4 1.3 fusion.209
  329.7 1.9 collective-permute-start.3
  331.7 2.8 collective-permute-start.2
  334.7 47.3 %multiply_add_fusion.12 = f32[64,64,1024]{2,1,0:T(8,128)} fusion(f32[64,64,1024]{2,1,0:T(8,128)S(1)} %bitcast.69, f32[64,64]{1,0:T(8,128)S(1)} %get-tuple-element.185, f32[64,64]{1,0:T(8,128)S(1)} %get-tuple-element.213, f32[1024]{0:T(1024)S(1)} %get-tuple-element.237, f32[64,64]{1,0:T(8,128)S(1)} %get-tuple-element.212, f32[64,64]{1,0:T(8,128)S(1)} %mul.3357, ...), kind=kLoop, calls=%fused_computation.226 | loop fusion | flops 146800640 | bytes 33824768 | tf_op jit(solution)/shard_map/add | solution.py:179
  382.0 33.6 %multiply_add_fusion.10 = f32[64,64,1024]{2,1,0:T(8,128)} fusion(f32[64,64,1024]{2,1,0:T(8,128)} %multiply_add_fusion.12, f32[2,64,1024]{2,1,0:T(8,128)S(1)} %collective-permute-done.3, f32[2,64,1024]{2,1,0:T(8,128)S(1)} %collective-permute-done.2, f32[1024]{0:T(1024)S(1)} %get-tuple-element.244, f32[1024]{0:T(1024)S(1)} %get-tuple-element.245, ...), kind=kLoop, calls=%fused_computation.224 | loop fusion | flops 71303168 | bytes 34612224 | tf_op jit(solution)/shard_map/add | solution.py:83
  415.6 44.6 %multiply_reduce_fusion.2 = (f32[64,64]{1,0:T(8,128)S(1)}, f32[64,64,1024]{2,1,0:T(8,128)}) fusion(f32[1024]{0:T(1024)S(1)} %get-tuple-element.249, f32[1024]{0:T(1024)S(1)} %get-tuple-element.235, f32[1024]{0:T(1024)S(1)} %get-tuple-element.248, f32[1024]{0:T(1024)S(1)} %get-tuple-element.234, pred[64,64]{1,0:T(8,128)(4,1)S(1)} %get-tuple-element.215, ...), kind=kLoop, calls=%fused_computation.222 | loop fusion | flops 88076288 | bytes 33608704 | tf_op jit(solution)/shard_map/reduce_sum | solution.py:218
  460.3 17.5 %psum.66 = f32[4096]{0:T(1024)S(1)} all-reduce(f32[4096]{0:T(1024)S(1)} %reduce_sum.57), channel_id=1, replica_groups=mesh['space'=8,'vel'=4] {'vel'}, use_global_device_ids=true, to_apply=%region_6.7 | all-reduce | flops 4096 | bytes 32768 | tf_op jit(solution)/shard_map/psum | solution.py:219
  477.8 11.5 %bitcast_select_fusion.2 = f32[4096,1024]{1,0:T(8,128)S(1)} fusion(f32[64,64,1024]{2,1,0:T(8,128)} %get-tuple-element.92, f32[4096]{0:T(1024)S(1)} %divide_add_fusion.2, f32[4096]{0:T(1024)S(1)} %get-tuple-element.233, f32[1024]{0:T(1024)S(1)} %get-tuple-element.237, f32[4096]{0:T(1024)S(1)} %get-tuple-element.232, f32[1024]{0:T(1024)S(1)} %get-tuple-element.249, ...), kind=kLoop, calls=%fused_computation.209 | loop fusion | flops 37748736 | bytes 33640448 | tf_op jit(solution)/shard_map/jit(_where)/select_n | solution.py:221
  489.3 14.7 %fusion.139 = f32[14,4096]{1,0:T(8,128)} fusion(f32[4096,1024]{1,0:T(8,128)S(1)} %bitcast_select_fusion.2, f32[14,1024]{1,0:T(8,128)S(1)} %stack.2), kind=kOutput, calls=%fused_computation.246 | convolution fusion | flops 704657408 | bytes 17063936 | tf_op jit(solution)/shard_map/kv,nv->kn/dot_general | solution.py:69
  504.0 0.4 all-reduce.16.cloned.1.call-start
  504.5 33.1 %all-reduce.14.cloned.1.call-done = f32[14,4096]{1,0:T(8,128)} async-done(((f32[14,4096]{1,0:T(8,128)}), f32[14,4096]{1,0:T(8,128)}) %all-reduce.14.cloned.1.call-update) | async-done | bytes 229392 | tf_op jit(solution)/shard_map/psum | solution.py:187
  537.7 2.5 slice_reduce_fusion.35
  541.2 1.7 fusion.212
  543.0 48.8 %multiply_add_fusion.7 = f32[4096,1024]{1,0:T(8,128)} fusion(f32[4096]{0:T(1024)S(1)} %get-tuple-element.199, f32[4096]{0:T(1024)S(1)} %get-tuple-element.226, f32[4096]{0:T(1024)S(1)} %get-tuple-element.198, f32[4096]{0:T(1024)S(1)} %get-tuple-element.223, f32[4096]{0:T(1024)S(1)} %get-tuple-element.224, f32[4096]{0:T(1024)S(1)} %get-tuple-element.225, ...), kind=kLoop, calls=%fused_computation.220 | loop fusion | flops 146800640 | bytes 33824768 | tf_op jit(solution)/shard_map/add | solution.py:179
  591.9 1.3 fusion.208
  593.2 1.9 collective-permute-start.5
  595.1 2.4 collective-permute-start.4
  597.7 47.3 %multiply_add_fusion.8 = f32[64,64,1024]{2,1,0:T(8,128)} fusion(f32[64,64,1024]{2,1,0:T(8,128)S(1)} %bitcast.71, f32[64,64]{1,0:T(8,128)S(1)} %get-tuple-element.183, f32[64,64]{1,0:T(8,128)S(1)} %mul.3500, f32[64,64]{1,0:T(8,128)S(1)} %get-tuple-element.204, f32[64,64]{1,0:T(8,128)S(1)} %get-tuple-element.182, f32[64,64]{1,0:T(8,128)S(1)} %get-tuple-element.201, ...), kind=kLoop, calls=%fused_computation.221 | loop fusion | flops 146800640 | bytes 33824768 | tf_op jit(solution)/shard_map/add | solution.py:179
  645.1 33.6 %multiply_add_fusion.6 = f32[64,64,1024]{2,1,0:T(8,128)} fusion(f32[64,64,1024]{2,1,0:T(8,128)} %multiply_add_fusion.8, f32[2,64,1024]{2,1,0:T(8,128)S(1)} %collective-permute-done.5, f32[2,64,1024]{2,1,0:T(8,128)S(1)} %collective-permute-done.4, f32[1024]{0:T(1024)S(1)} %get-tuple-element.244, f32[1024]{0:T(1024)S(1)} %get-tuple-element.245, ...), kind=kLoop, calls=%fused_computation.219 | loop fusion | flops 71303168 | bytes 34612224 | tf_op jit(solution)/shard_map/add | solution.py:83
  678.7 44.6 %multiply_reduce_fusion.1 = (f32[64,64]{1,0:T(8,128)S(1)}, f32[64,64,1024]{2,1,0:T(8,128)}) fusion(f32[1024]{0:T(1024)S(1)} %get-tuple-element.249, f32[1024]{0:T(1024)S(1)} %get-tuple-element.235, f32[1024]{0:T(1024)S(1)} %get-tuple-element.248, f32[1024]{0:T(1024)S(1)} %get-tuple-element.234, pred[64,64]{1,0:T(8,128)(4,1)S(1)} %get-tuple-element.215, ...), kind=kLoop, calls=%fused_computation.217 | loop fusion | flops 88076288 | bytes 33608704 | tf_op jit(solution)/shard_map/reduce_sum | solution.py:218
  723.3 17.5 %psum.68 = f32[4096]{0:T(1024)S(1)} all-reduce(f32[4096]{0:T(1024)S(1)} %reduce_sum.59), channel_id=1, replica_groups=mesh['space'=8,'vel'=4] {'vel'}, use_global_device_ids=true, to_apply=%region_9.10 | all-reduce | flops 4096 | bytes 32768 | tf_op jit(solution)/shard_map/psum | solution.py:219
  740.9 11.5 %bitcast_select_fusion.1 = f32[4096,1024]{1,0:T(8,128)S(1)} fusion(f32[64,64,1024]{2,1,0:T(8,128)} %get-tuple-element.80, f32[4096]{0:T(1024)S(1)} %divide_add_fusion.1, f32[4096]{0:T(1024)S(1)} %get-tuple-element.233, f32[1024]{0:T(1024)S(1)} %get-tuple-element.237, f32[4096]{0:T(1024)S(1)} %get-tuple-element.232, f32[1024]{0:T(1024)S(1)} %get-tuple-element.249, ...), kind=kLoop, calls=%fused_computation.208 | loop fusion | flops 37748736 | bytes 33640448 | tf_op jit(solution)/shard_map/jit(_where)/select_n | solution.py:221
  752.4 14.7 %fusion.137 = f32[14,4096]{1,0:T(8,128)} fusion(f32[4096,1024]{1,0:T(8,128)S(1)} %bitcast_select_fusion.1, f32[14,1024]{1,0:T(8,128)S(1)} %stack.2), kind=kOutput, calls=%fused_computation.244 | convolution fusion | flops 704657408 | bytes 17063936 | tf_op jit(solution)/shard_map/kv,nv->kn/dot_general | solution.py:69
  767.0 0.4 all-reduce.18.cloned.1.call-start
  767.6 33.1 %all-reduce.16.cloned.1.call-done = f32[14,4096]{1,0:T(8,128)} async-done(((f32[14,4096]{1,0:T(8,128)}), f32[14,4096]{1,0:T(8,128)}) %all-reduce.16.cloned.1.call-update) | async-done | bytes 229392 | tf_op jit(solution)/shard_map/psum | solution.py:187
  800.7 2.5 slice_reduce_fusion.21
  804.2 1.7 fusion.211
  806.1 48.8 %multiply_add_fusion.3 = f32[4096,1024]{1,0:T(8,128)} fusion(f32[4096]{0:T(1024)S(1)} %get-tuple-element.192, f32[4096]{0:T(1024)S(1)} %get-tuple-element.221, f32[4096]{0:T(1024)S(1)} %get-tuple-element.191, f32[4096]{0:T(1024)S(1)} %get-tuple-element.218, f32[4096]{0:T(1024)S(1)} %get-tuple-element.219, f32[4096]{0:T(1024)S(1)} %get-tuple-element.220, ...), kind=kLoop, calls=%fused_computation.215 | loop fusion | flops 146800640 | bytes 33824768 | tf_op jit(solution)/shard_map/add | solution.py:179
  854.9 1.3 fusion.207
  856.2 1.9 collective-permute-start.7
  858.1 2.4 collective-permute-start.6
  860.8 47.3 %multiply_add_fusion.4 = f32[64,64,1024]{2,1,0:T(8,128)} fusion(f32[64,64,1024]{2,1,0:T(8,128)S(1)} %bitcast.73, f32[64,64]{1,0:T(8,128)S(1)} %get-tuple-element.181, f32[64,64]{1,0:T(8,128)S(1)} %mul.3639, f32[64,64]{1,0:T(8,128)S(1)} %get-tuple-element.197, f32[64,64]{1,0:T(8,128)S(1)} %get-tuple-element.180, f32[64,64]{1,0:T(8,128)S(1)} %get-tuple-element.194, ...), kind=kLoop, calls=%fused_computation.216 | loop fusion | flops 146800640 | bytes 33824768 | tf_op jit(solution)/shard_map/add | solution.py:179
  908.1 33.6 %multiply_add_fusion.2 = f32[64,64,1024]{2,1,0:T(8,128)} fusion(f32[64,64,1024]{2,1,0:T(8,128)} %multiply_add_fusion.4, f32[2,64,1024]{2,1,0:T(8,128)S(1)} %collective-permute-done.7, f32[2,64,1024]{2,1,0:T(8,128)S(1)} %collective-permute-done.6, f32[1024]{0:T(1024)S(1)} %get-tuple-element.244, f32[1024]{0:T(1024)S(1)} %get-tuple-element.245, ...), kind=kLoop, calls=%fused_computation.214 | loop fusion | flops 71303168 | bytes 34612224 | tf_op jit(solution)/shard_map/add | solution.py:83
  941.7 44.6 %multiply_reduce_fusion = (f32[64,64]{1,0:T(8,128)S(1)}, f32[64,64,1024]{2,1,0:T(8,128)}) fusion(f32[1024]{0:T(1024)S(1)} %get-tuple-element.249, f32[1024]{0:T(1024)S(1)} %get-tuple-element.235, f32[1024]{0:T(1024)S(1)} %get-tuple-element.248, f32[1024]{0:T(1024)S(1)} %get-tuple-element.234, pred[64,64]{1,0:T(8,128)(4,1)S(1)} %get-tuple-element.215, ...), kind=kLoop, calls=%fused_computation.212 | loop fusion | flops 88076288 | bytes 33608704 | tf_op jit(solution)/shard_map/reduce_sum | solution.py:218
  986.4 17.5 %psum.70 = f32[4096]{0:T(1024)S(1)} all-reduce(f32[4096]{0:T(1024)S(1)} %reduce_sum.61), channel_id=1, replica_groups=mesh['space'=8,'vel'=4] {'vel'}, use_global_device_ids=true, to_apply=%region_12.13 | all-reduce | flops 4096 | bytes 32768 | tf_op jit(solution)/shard_map/psum | solution.py:219
  1003.9 11.5 %bitcast_select_fusion = f32[4096,1024]{1,0:T(8,128)S(1)} fusion(f32[64,64,1024]{2,1,0:T(8,128)} %get-tuple-element.68, f32[4096]{0:T(1024)S(1)} %get-tuple-element.61, f32[4096]{0:T(1024)S(1)} %get-tuple-element.233, f32[1024]{0:T(1024)S(1)} %get-tuple-element.237, f32[4096]{0:T(1024)S(1)} %get-tuple-element.232, f32[1024]{0:T(1024)S(1)} %get-tuple-element.249, ...), kind=kLoop, calls=%fused_computation.207 | loop fusion | flops 37748736 | bytes 33640448 | tf_op jit(solution)/shard_map/jit(_where)/select_n | solution.py:221
  1015.4 14.7 %fusion.135 = f32[14,4096]{1,0:T(8,128)} fusion(f32[4096,1024]{1,0:T(8,128)S(1)} %bitcast_select_fusion, f32[14,1024]{1,0:T(8,128)S(1)} %stack.2), kind=kOutput, calls=%fused_computation.242 | convolution fusion | flops 704657408 | bytes 17063936 | tf_op jit(solution)/shard_map/kv,nv->kn/dot_general | solution.py:69
  1030.3 0.7 copy.6
  1031.0 32.8 %all-reduce.18.cloned.1.call-done = f32[14,4096]{1,0:T(8,128)} async-done(((f32[14,4096]{1,0:T(8,128)}), f32[14,4096]{1,0:T(8,128)}) %all-reduce.18.cloned.1.call-update) | async-done | bytes 229392 | tf_op jit(solution)/shard_map/psum | solution.py:187
  1063.7 2.7 slice_reduce_fusion.7
  1067.6 48.7 %multiply_add_fusion = f32[64,64,1024]{2,1,0:T(8,128)} fusion(f32[64,64,1024]{2,1,0:T(8,128)} %get-tuple-element.68, f32[64,64]{1,0:T(8,128)S(1)} %get-tuple-element.179, f32[64,64]{1,0:T(8,128)S(1)} %mul.3778, f32[64,64]{1,0:T(8,128)S(1)} %get-tuple-element.190, f32[64,64]{1,0:T(8,128)S(1)} %get-tuple-element.178, f32[64,64]{1,0:T(8,128)S(1)} %get-tuple-element.187, ...), kind=kLoop, calls=%fused_computation.211 | loop fusion | flops 146800640 | bytes 33824768 | tf_op jit(solution)/shard_map/add | solution.py:179
  (155 shorter events, 7.8 us)
Async XLA Ops:
  7.2 78.6 %all-reduce.10.cloned.1.call-start = ((), (), s32[]{:S(2)}) async-start(), calls=%async_computation | async-start | bytes 524288 | tf_op jit(solution)/shard_map/psum | solution.py:210
  8.5 78.2 %collective-permute-start = (f32[2,64,1024]{2,1,0:T(8,128)S(1)}, f32[2,64,1024]{2,1,0:T(8,128)S(1)}, u32[]{:S(2)}, u32[]{:S(2)}) collective-permute-start(f32[2,64,1024]{2,1,0:T(8,128)S(1)} %get-tuple-element.113), channel_id=1, source_target_pairs={{0,4},{4,8},{8,12},{12,16},{16,20},{20,24},{24,28},{1,5},{5,9},{9,... | collective-permute-start | bytes 1572872 | tf_op jit(solution)/shard_map/ppermute | solution.py:27
  10.4 94.7 %collective-permute-start.1 = (f32[2,64,1024]{2,1,0:T(8,128)S(1)}, f32[2,64,1024]{2,1,0:T(8,128)S(1)}, u32[]{:S(2)}, u32[]{:S(2)}) collective-permute-start(f32[2,64,1024]{2,1,0:T(8,128)S(1)} %get-tuple-element.114), channel_id=1, source_target_pairs={{4,0},{8,4},{12,8},{16,12},{20,16},{24,20},{28,24},{5,1},{9,5},{13... | collective-permute-start | bytes 1572872 | tf_op jit(solution)/shard_map/ppermute | solution.py:28
  28.3 21.9 %copy-start.1 = (s32[64,64]{1,0:T(8,128)S(1)}, s32[64,64]{1,0:T(8,128)}, u32[]{:S(2)}) copy-start(s32[64,64]{1,0:T(8,128)} %param.5) | copy-start | bytes 49156
  50.0 224.1 %all-reduce.12.cloned.1.call-start = ((), (), s32[]{:S(2)}) async-start(), calls=%async_computation.1 | async-start | bytes 524288 | tf_op jit(solution)/shard_map/psum | solution.py:187
  225.8 14.8 %copy-start = (f32[64,64]{1,0:T(8,128)S(1)}, f32[64,64]{1,0:T(8,128)}, u32[]{:S(2)}) copy-start(f32[64,64]{1,0:T(8,128)} %param.7) | copy-start | bytes 49156
  240.5 297.2 %all-reduce.14.cloned.1.call-start = ((), (), s32[]{:S(2)}) async-start(), calls=%async_computation.2 | async-start | bytes 524288 | tf_op jit(solution)/shard_map/psum | solution.py:187
  277.7 56.9 %slice-start = ((s8[16777216]{0:T(1024)(128)(4,1)}), s8[4194304]{0:T(1024)(128)(4,1)S(1)}, s32[]{:S(2)}) async-start(s8[16777216]{0:T(1024)(128)(4,1)} %bitcast.68), calls=%async_computation.5 | async-start | bytes 8388608
  279.6 55.1 %slice-start.1 = ((s8[16777216]{0:T(1024)(128)(4,1)}), s8[4194304]{0:T(1024)(128)(4,1)S(1)}, s32[]{:S(2)}) async-start(s8[16777216]{0:T(1024)(128)(4,1)} %bitcast.68), calls=%async_computation.6 | async-start | bytes 8388608
  279.6 55.1 %slice-start.2 = ((s8[16777216]{0:T(1024)(128)(4,1)}), s8[4194304]{0:T(1024)(128)(4,1)S(1)}, s32[]{:S(2)}) async-start(s8[16777216]{0:T(1024)(128)(4,1)} %bitcast.68), calls=%async_computation.7 | async-start | bytes 8388608
  279.6 55.1 %slice-start.3 = ((s8[16777216]{0:T(1024)(128)(4,1)}), s8[4194304]{0:T(1024)(128)(4,1)S(1)}, s32[]{:S(2)}) async-start(s8[16777216]{0:T(1024)(128)(4,1)} %bitcast.68), calls=%async_computation.8 | async-start | bytes 8388608
  329.7 52.3 %collective-permute-start.3 = (f32[2,64,1024]{2,1,0:T(8,128)S(1)}, f32[2,64,1024]{2,1,0:T(8,128)S(1)}, u32[]{:S(2)}, u32[]{:S(2)}) collective-permute-start(f32[2,64,1024]{2,1,0:T(8,128)S(1)} %bitcast.77), channel_id=1, source_target_pairs={{4,0},{8,4},{12,8},{16,12},{20,16},{24,20},{28,24},{5,1},{9,5},{13... | collective-permute-start | bytes 1572872 | tf_op jit(solution)/shard_map/ppermute | solution.py:28
  331.7 50.4 %collective-permute-start.2 = (f32[2,64,1024]{2,1,0:T(8,128)S(1)}, f32[2,64,1024]{2,1,0:T(8,128)S(1)}, u32[]{:S(2)}, u32[]{:S(2)}) collective-permute-start(f32[2,64,1024]{2,1,0:T(8,128)S(1)} %bitcast.74), channel_id=1, source_target_pairs={{0,4},{4,8},{8,12},{12,16},{16,20},{20,24},{24,28},{1,5},{5,9},{9,... | collective-permute-start | bytes 1572872 | tf_op jit(solution)/shard_map/ppermute | solution.py:27
  504.0 296.7 %all-reduce.16.cloned.1.call-start = ((), (), s32[]{:S(2)}) async-start(), calls=%async_computation.3 | async-start | bytes 524288 | tf_op jit(solution)/shard_map/psum | solution.py:187
  541.2 56.5 %slice-start.4 = ((s8[16777216]{0:T(1024)(128)(4,1)}), s8[4194304]{0:T(1024)(128)(4,1)S(1)}, s32[]{:S(2)}) async-start(s8[16777216]{0:T(1024)(128)(4,1)} %bitcast.70), calls=%async_computation.9 | async-start | bytes 8388608
  543.0 54.7 %slice-start.5 = ((s8[16777216]{0:T(1024)(128)(4,1)}), s8[4194304]{0:T(1024)(128)(4,1)S(1)}, s32[]{:S(2)}) async-start(s8[16777216]{0:T(1024)(128)(4,1)} %bitcast.70), calls=%async_computation.10 | async-start | bytes 8388608
  543.0 54.7 %slice-start.6 = ((s8[16777216]{0:T(1024)(128)(4,1)}), s8[4194304]{0:T(1024)(128)(4,1)S(1)}, s32[]{:S(2)}) async-start(s8[16777216]{0:T(1024)(128)(4,1)} %bitcast.70), calls=%async_computation.11 | async-start | bytes 8388608
  543.0 54.7 %slice-start.7 = ((s8[16777216]{0:T(1024)(128)(4,1)}), s8[4194304]{0:T(1024)(128)(4,1)S(1)}, s32[]{:S(2)}) async-start(s8[16777216]{0:T(1024)(128)(4,1)} %bitcast.70), calls=%async_computation.12 | async-start | bytes 8388608
  593.2 51.9 %collective-permute-start.5 = (f32[2,64,1024]{2,1,0:T(8,128)S(1)}, f32[2,64,1024]{2,1,0:T(8,128)S(1)}, u32[]{:S(2)}, u32[]{:S(2)}) collective-permute-start(f32[2,64,1024]{2,1,0:T(8,128)S(1)} %bitcast.78), channel_id=1, source_target_pairs={{4,0},{8,4},{12,8},{16,12},{20,16},{24,20},{28,24},{5,1},{9,5},{13... | collective-permute-start | bytes 1572872 | tf_op jit(solution)/shard_map/ppermute | solution.py:28
  595.1 50.0 %collective-permute-start.4 = (f32[2,64,1024]{2,1,0:T(8,128)S(1)}, f32[2,64,1024]{2,1,0:T(8,128)S(1)}, u32[]{:S(2)}, u32[]{:S(2)}) collective-permute-start(f32[2,64,1024]{2,1,0:T(8,128)S(1)} %bitcast.75), channel_id=1, source_target_pairs={{0,4},{4,8},{8,12},{12,16},{16,20},{20,24},{24,28},{1,5},{5,9},{9,... | collective-permute-start | bytes 1572872 | tf_op jit(solution)/shard_map/ppermute | solution.py:27
  767.0 296.7 %all-reduce.18.cloned.1.call-start = ((), (), s32[]{:S(2)}) async-start(), calls=%async_computation.4 | async-start | bytes 524288 | tf_op jit(solution)/shard_map/psum | solution.py:187
  804.2 56.5 %slice-start.8 = ((s8[16777216]{0:T(1024)(128)(4,1)}), s8[4194304]{0:T(1024)(128)(4,1)S(1)}, s32[]{:S(2)}) async-start(s8[16777216]{0:T(1024)(128)(4,1)} %bitcast.72), calls=%async_computation.13 | async-start | bytes 8388608
  806.0 54.7 %slice-start.9 = ((s8[16777216]{0:T(1024)(128)(4,1)}), s8[4194304]{0:T(1024)(128)(4,1)S(1)}, s32[]{:S(2)}) async-start(s8[16777216]{0:T(1024)(128)(4,1)} %bitcast.72), calls=%async_computation.14 | async-start | bytes 8388608
  806.1 54.7 %slice-start.10 = ((s8[16777216]{0:T(1024)(128)(4,1)}), s8[4194304]{0:T(1024)(128)(4,1)S(1)}, s32[]{:S(2)}) async-start(s8[16777216]{0:T(1024)(128)(4,1)} %bitcast.72), calls=%async_computation.15 | async-start | bytes 8388608
  806.1 54.7 %slice-start.11 = ((s8[16777216]{0:T(1024)(128)(4,1)}), s8[4194304]{0:T(1024)(128)(4,1)S(1)}, s32[]{:S(2)}) async-start(s8[16777216]{0:T(1024)(128)(4,1)} %bitcast.72), calls=%async_computation.16 | async-start | bytes 8388608
  856.2 51.9 %collective-permute-start.7 = (f32[2,64,1024]{2,1,0:T(8,128)S(1)}, f32[2,64,1024]{2,1,0:T(8,128)S(1)}, u32[]{:S(2)}, u32[]{:S(2)}) collective-permute-start(f32[2,64,1024]{2,1,0:T(8,128)S(1)} %bitcast.79), channel_id=1, source_target_pairs={{4,0},{8,4},{12,8},{16,12},{20,16},{24,20},{28,24},{5,1},{9,5},{13... | collective-permute-start | bytes 1572872 | tf_op jit(solution)/shard_map/ppermute | solution.py:28
  858.1 50.0 %collective-permute-start.6 = (f32[2,64,1024]{2,1,0:T(8,128)S(1)}, f32[2,64,1024]{2,1,0:T(8,128)S(1)}, u32[]{:S(2)}, u32[]{:S(2)}) collective-permute-start(f32[2,64,1024]{2,1,0:T(8,128)S(1)} %bitcast.76), channel_id=1, source_target_pairs={{0,4},{4,8},{8,12},{12,16},{16,20},{20,24},{24,28},{1,5},{5,9},{9,... | collective-permute-start | bytes 1572872 | tf_op jit(solution)/shard_map/ppermute | solution.py:27
Sparse Core Ops, SparseCore 0:
  50.1 35.6 all-reduce.9
  240.6 33.4 all-reduce.11
  504.1 33.4 all-reduce.13
  767.2 33.4 all-reduce.15
  1030.2 33.4 all-reduce.17
where the time goes:
time: 1130 us; the launch traced here: 1120 us
  other arithmetic  722 us (64%)
  waiting for transfers between devices  168 us (15%)
  matrix products  79.5 us (7%)
  blocking collectives  70 us (6%)
  local copies, waits for them, and re-layouts  47.8 us (4%)
  starting transfers between devices  21.1 us (2%)
  between operations  14.7 us (1%)
    add x7, other arithmetic, relax_shakhov(): return target + (values - target) * jnp.exp(-TIME_STEP / collision_interval)  337 us
    reduce_sum x4, other arithmetic, shards(): incident_part = jnp.sum(incoming * flat, axis=1)  178 us
    add x4, other arithmetic, beam_warming(): centre - 0.5 * courant * (3.0 * centre - 4.0 * near + distant)  136 us
    psum x4, waiting for transfers between devices, reduce_stats(): total = lax.psum(parts, 'vel')  132 us
    dot_general x5, matrix products, project_moments(): jnp.einsum('kv,nv->kn', table, values, precision=lax.Precision.HIGHEST)  79.5 us
    psum x4, blocking collectives, shards(): incident = lax.psum(incident_part, 'vel')  70 us
    select_n x4, other arithmetic, shards(): bounded = jnp.where(emit, emitted[:, None] * wall_maxwell, flat)  57 us
    psum x1, waiting for transfers between devices, shards(): lax.psum(jnp.concatenate([norm_part[None, :], emitted_part], axis=0), 'vel')  35.3 us
  transfers between devices with their start and end apart: 13, of which 5 were waited for; matrix products, arithmetic and copies ran while one was open for 18% of the time, Pallas kernels for 0%

commit v1 on v0

v1 whole, which is shorter than its diff:
```python
import functools
import math

import jax
import jax.numpy as jnp
from jax import lax
from jax.experimental import pallas as pl
from jax.experimental.pallas import tpu as pltpu
from jax.sharding import PartitionSpec as P

NQ = 16
STEPS = 4
LIMIT = 5.0
TIME_STEP = 0.05
SIGMA = 0.8
LATENT = 5.0
PRANDTL = 2.0 / 3.0
SHEAR_EXPONENT = 0.1

SPACING = 2.0 * LIMIT / NQ
HALF = 0.5 * SPACING
WEIGHT = SPACING**3 / (2.0 * math.pi) ** 1.5
LOG2E = math.log2(math.e)
LANES = 128
ROWS = 16
OFF = 1024.0

T_SQ_HI, T_SQ_LO, T_X, T_Y, T_Z, T_ONE = range(6)
P_ONE, P_X, P_Y, P_Z, P_XX, P_YY, P_ZZ, P_XY, P_XZ, P_YZ = range(6, 16)
P_XS, P_YS, P_ZS, P_XSL, P_YSL, P_ZSL = range(16, 22)
W_SQ_HI, W_SQ_LO, W_ONE, W_XP, W_XN, W_YP, W_YN = range(22, 29)
B_E, B_W = 29, 30
PART = 32
COEF = 128

VMEM_LIMIT = 60 * 1024 * 1024


def setup_kernel(span, target_ref, factor_ref, wall_ref, sums_ref, stencil_ref, spread_ref,
                 feature_ref, moment_ref):
    shape = (8, span)
    place = lax.broadcasted_iota(jnp.int32, shape, 1)
    third = lax.axis_index("vel") * (span // WIDE) + place // WIDE
    first = place % NQ
    middle = place // NQ % NQ

    def odd(pick):
        return (2 * (pick % NQ) - (NQ - 1)).astype(jnp.float32)

    x, y, z = odd(first + third), odd(middle), odd(first + middle)
    one = jnp.ones(shape, jnp.float32)
    square = x * x + y * y + z * z
    square_hi = jnp.floor(square * (1.0 / 16.0)) * 16.0
    square_lo = square - square_hi

    def split(v):
        hi = jnp.floor(v * (1.0 / 128.0)) * 128.0
        return hi, v - hi

    xs, xsl = split(x * square)
    ys, ysl = split(y * square)
    zs, zsl = split(z * square)
    xp = jnp.where(x > 0, 1.0, 0.0)
    yp = jnp.where(y > 0, 1.0, 0.0)
    features = [square_hi, square_lo, x, y, z, one,
                one, x, y, z, x * x, y * y, z * z, x * y, x * z, y * z, xs, ys, zs, xsl, ysl, zsl,
                square_hi, square_lo, one, xp, one - xp, yp, one - yp]
    feature_ref[...] = jnp.zeros_like(feature_ref)
    for k, feature in enumerate(features):
        feature_ref[k:k + 1, :] = feature[0:1]
    row = lax.broadcasted_iota(jnp.int32, (PART, span), 0)
    blank = jnp.zeros((COEF - 3 * PART, span), jnp.float32)
    for ref, low, high in ((target_ref, T_SQ_HI, P_ONE), (factor_ref, P_ONE, W_SQ_HI),
                           (wall_ref, W_SQ_HI, B_E)):
        chosen = jnp.where((row >= low) & (row < high), feature_ref[...], 0.0)
        ref[...] = jnp.concatenate([chosen, chosen, chosen, blank], axis=0).astype(jnp.bfloat16)
    quadrants = (xp * yp, xp * (one - yp), (one - xp) * yp, (one - xp) * (one - yp))
    moment = feature_ref[P_ONE:W_SQ_HI, :]
    moment_ref[...] = jnp.zeros_like(moment_ref)
    for k, quadrant in enumerate(quadrants):
        moment_ref[ROWS * k:ROWS * (k + 1), :] = moment * quadrant[0:1]
    for k, speed in enumerate((-x, x, -y, y)):
        moment_ref[4 * ROWS + k:4 * ROWS + k + 1, :] = jnp.maximum(speed, 0.0)[0:1]
    for l in range(span // LANES):
        cut = slice(l * LANES, (l + 1) * LANES)
        sums_ref[cut, :] = moment_ref[:, cut].T.astype(jnp.bfloat16)
    for k, v in enumerate((x, y)):
        courant = jnp.abs(v) * (HALF * TIME_STEP)
        half_square = 0.5 * courant * courant
        for n, value in enumerate((1.0 - 1.5 * courant + half_square, 2.0 * courant - 2.0 * half_square,
                                   half_square - 0.5 * courant, v)):
            stencil_ref[8 * (4 * k + n):8 * (4 * k + n + 1), :] = value
    row = lax.broadcasted_iota(jnp.int32, (COEF, 2 * LANES), 0)
    column = lax.broadcasted_iota(jnp.int32, (COEF, 2 * LANES), 1)
    want = jnp.where(column < LANES, B_E, B_W)
    hit = (row % PART == want) & (row < 3 * PART)
    spread_ref[...] = jnp.where(hit, 1.0, 0.0).astype(jnp.bfloat16)


def setup(span):
    table = jax.ShapeDtypeStruct((COEF, span), jnp.bfloat16)
    return pl.pallas_call(
        functools.partial(setup_kernel, span),
        out_shape=(table, table, table,
                   jax.ShapeDtypeStruct((span, LANES), jnp.bfloat16),
                   jax.ShapeDtypeStruct((64, span), jnp.float32),
                   jax.ShapeDtypeStruct((COEF, 2 * LANES), jnp.bfloat16)),
        out_specs=(pl.BlockSpec(memory_space=pltpu.VMEM),) * 6,
        scratch_shapes=[pltpu.VMEM((PART, span), jnp.float32), pltpu.VMEM((LANES, span), jnp.float32)],
        name="setup",
    )()


def turned(values, l, span, back=False):
    third = lax.axis_index("vel") * (span // WIDE) + l
    shift = NQ * (third % NQ)
    return pltpu.roll(values, (WIDE - shift) % WIDE if back else shift, 1)


def dot(a, b):
    return jnp.dot(a, b, preferred_element_type=jnp.float32)


def state_kernel(groups, with_edges, sums_ref, kind_ref, code_ref, temp_ref, first_ref, last_ref, spread_ref,
                 target_ref, factor_ref, wall_ref, coef_ref, flux_ref, *outer):
    stack_ref = outer[-1]

    def read(k, scale):
        return sums_ref[pl.ds(k, groups, stride=ROWS), :] * (WEIGHT * scale)

    kind = kind_ref[...]
    code = code_ref[...]
    wall = temp_ref[...]
    s0 = s1 = s2 = s3 = jnp.zeros_like(wall)
    inverse = 1.0 / wall
    for j in range(NQ // 2):
        speed = HALF * (2 * j + 1)
        e = jnp.exp(inverse * (-0.5 * speed * speed))
        s0, s1, s2, s3 = s0 + e, s1 + speed * e, s2 + speed**2 * e, s3 + speed**3 * e
    scale = (WEIGHT * 2.0) * inverse * lax.rsqrt(wall)
    norm = 2.0 * scale * s1 * s0 * s0
    f_one = 2.0 * scale * s0 * s0 * s0
    f_nn = 2.0 * scale * s2 * s0 * s0
    f_tt = f_nn
    f_ns = 2.0 * scale * (s3 * s0 * s0 + 2.0 * s1 * s2 * s0)
    saturated = jnp.exp(LATENT * (1.0 - inverse)) * inverse
    incident = read(13, HALF)
    share = jnp.where(kind == 2, SIGMA, 0.0)
    emitted = share * saturated + (1.0 - share) * incident / norm
    boundary = kind > 0
    flux_ref[...] = jnp.where(boundary, emitted * norm - incident, 0.0)
    em = jnp.where(boundary, emitted, 0.0)
    along_x = code < 2
    sign = jnp.where((code == 0) | (code == 2), 1.0, -1.0)
    sx = jnp.where(along_x, sign, 0.0)
    sy = jnp.where(along_x, 0.0, sign)

    rho = read(0, 1.0) + em * f_one
    em_n = em * norm
    em_s = em * f_ns
    mx = read(1, HALF) + sx * em_n
    my = read(2, HALF) + sy * em_n
    mz = read(3, HALF)
    mxx = read(4, HALF**2) + em * f_nn
    myy = read(5, HALF**2) + em * f_tt
    mzz = read(6, HALF**2) + em * f_tt
    mxy = read(7, HALF**2)
    mxz = read(8, HALF**2)
    myz = read(9, HALF**2)
    mxs = read(10, HALF**3) + sx * em_s
    mys = read(11, HALF**3) + sy * em_s
    mzs = read(12, HALF**3)
    msq = mxx + myy + mzz
    per = 1.0 / rho
    ux, uy, uz = mx * per, my * per, mz * per
    uu = ux * ux + uy * uy + uz * uz
    temp = (msq * per - uu) * (1.0 / 3.0)
    dotted = ux * mx + uy * my + uz * mz

    def heat(third, u, m, second):
        return 0.5 * (third - 2.0 * (ux * second[0] + uy * second[1] + uz * second[2]) + uu * m
                      - u * msq + 2.0 * u * dotted - u * uu * rho)

    qx = heat(mxs, ux, mx, (mxx, mxy, mxz))
    qy = heat(mys, uy, my, (mxy, myy, myz))
    qz = heat(mzs, uz, mz, (mxz, myz, mzz))
    pressure = rho * temp
    per_t = 1.0 / temp
    decay = jnp.exp((-TIME_STEP / SHEAR_EXPONENT) * pressure * jnp.exp(-0.72 * jnp.log(temp)))
    amount = (1.0 - decay) * rho * per_t * lax.rsqrt(temp)
    bend = amount * ((1.0 - PRANDTL) / 5.0) * per_t * per_t / pressure
    kappa = (0.5 * LOG2E) * per_t
    qu = qx * ux + qy * uy + qz * uz
    rest = uu - 5.0 * temp
    twice = -2.0 * bend * HALF**2
    kappa_sq = -kappa * HALF**2
    kappa_u = (2.0 * HALF) * kappa
    wall_sq = (-0.5 * LOG2E * HALF**2) * inverse
    bqu = bend * qu * HALF**2
    solid = jnp.where(boundary, OFF, 0.0)
    rows = {
        T_SQ_HI: kappa_sq, T_SQ_LO: kappa_sq,
        T_X: kappa_u * ux, T_Y: kappa_u * uy, T_Z: kappa_u * uz, T_ONE: -kappa * uu,
        P_ONE: amount - bend * qu * rest,
        P_X: bend * HALF * (qx * rest + 2.0 * qu * ux),
        P_Y: bend * HALF * (qy * rest + 2.0 * qu * uy),
        P_Z: bend * HALF * (qz * rest + 2.0 * qu * uz),
        P_XX: twice * qx * ux - bqu, P_YY: twice * qy * uy - bqu, P_ZZ: twice * qz * uz - bqu,
        P_XY: twice * (qx * uy + qy * ux), P_XZ: twice * (qx * uz + qz * ux),
        P_YZ: twice * (qy * uz + qz * uy),
        P_XS: bend * HALF**3 * qx, P_YS: bend * HALF**3 * qy, P_ZS: bend * HALF**3 * qz,
        W_SQ_HI: wall_sq, W_SQ_LO: wall_sq,
        W_ONE: jnp.where(boundary, 0.0, OFF),
        W_XP: jnp.where(code == 1, solid, 0.0), W_XN: jnp.where(code == 0, solid, 0.0),
        W_YP: jnp.where(code == 3, solid, 0.0), W_YN: jnp.where(code == 2, solid, 0.0),
        B_E: decay, B_W: em * decay * inverse * lax.rsqrt(wall),
    }
    rows[P_XSL], rows[P_YSL], rows[P_ZSL] = rows[P_XS], rows[P_YS], rows[P_ZS]
    zero = jnp.zeros_like(wall)
    for k in range(PART):
        value = rows.get(k)
        for part in range(3):
            if value is None:
                stack_ref[pl.ds(part * PART + k, groups, stride=COEF), :] = zero
                continue
            hi = value.astype(jnp.bfloat16).astype(jnp.float32)
            stack_ref[pl.ds(part * PART + k, groups, stride=COEF), :] = hi
            value = value - hi
    blank = jnp.zeros((COEF - 3 * PART, LANES), jnp.float32)

    def turn(g, carry):
        start = pl.multiple_of(g * COEF, COEF)
        block = jnp.concatenate([stack_ref[pl.ds(start, 3 * PART), :], blank], axis=0)
        coef_ref[pl.ds(start, LANES), :] = block.T.astype(jnp.bfloat16)
        return carry

    lax.fori_loop(0, groups, turn, 0, unroll=4)
    if not with_edges:
        return
    low_ref, high_ref = outer[:2]
    size = low_ref.shape[0]
    for flat_ref, start, out_ref in ((first_ref, 0, low_ref), (last_ref, groups * LANES - size, high_ref)):
        coef = coef_ref[start:start + size, :]
        even = dot(coef, spread_ref[...])
        for l in range(flat_ref.shape[1] // WIDE):
            columns = slice(l * WIDE, (l + 1) * WIDE)
            out_ref[:, columns] = relaxed(coef, even, flat_ref[:, columns], target_ref[:, columns],
                                          factor_ref[:, columns], wall_ref[:, columns])


def state(with_edges, sums, kind, code, temp, flat, spread, tables, ncols):
    groups = kind.shape[0]
    cells, span = flat.shape
    size = 2 * ncols
    last = cells // size - 1
    whole = pl.BlockSpec(memory_space=pltpu.VMEM)
    out_shape = (jax.ShapeDtypeStruct((cells, COEF), jnp.bfloat16),
                 jax.ShapeDtypeStruct((groups, LANES), jnp.float32))
    if with_edges:
        out_shape += (jax.ShapeDtypeStruct((size, span), jnp.float32),) * 2
    return pl.pallas_call(
        functools.partial(state_kernel, groups, with_edges),
        grid=(1,),
        out_shape=out_shape,
        in_specs=[whole] * 4 + [pl.BlockSpec((size, span), lambda i: (0, 0)),
                                pl.BlockSpec((size, span), lambda i: (last, 0))] + [whole] * 4,
        out_specs=(whole,) * len(out_shape),
        scratch_shapes=[pltpu.VMEM((groups * COEF, LANES), jnp.float32)],
        compiler_params=pltpu.CompilerParams(vmem_limit_bytes=VMEM_LIMIT),
        name="state",
    )(sums, kind, code, temp, flat, flat, spread, *tables)


CELLS = 256
WIDE = 256


def relaxed(coef, even, flat, target, factor, wall):
    exponent = dot(coef, target)
    factor = dot(coef, factor)
    wall = dot(coef, wall)
    decay, amount = even[:, :LANES], even[:, LANES:]
    parts = []
    for h in range(WIDE // LANES):
        cut = slice(h * LANES, (h + 1) * LANES)
        bounded = jnp.where(wall[:, cut] > 0.0, flat[:, cut] * decay, amount * jnp.exp2(wall[:, cut]))
        parts.append(bounded + jnp.exp2(exponent[:, cut]) * factor[:, cut])
    return jnp.concatenate(parts, axis=1)


def relax_tiles(cells, spread_ref, tables, coef_ref, even_ref, flat_ref, store):
    target_ref, factor_ref, wall_ref = tables
    span = flat_ref.shape[1]

    def block(b, carry):
        start = pl.multiple_of(b * CELLS, CELLS)
        coef = coef_ref[pl.ds(start, CELLS), :]
        even_ref[...] = dot(coef, spread_ref[...])
        for l in range(span // WIDE):
            columns = slice(l * WIDE, (l + 1) * WIDE)
            store(start, l, relaxed(coef, even_ref, flat_ref[pl.ds(start, CELLS), columns],
                                    target_ref[:, columns], factor_ref[:, columns], wall_ref[:, columns]))
        return carry

    lax.fori_loop(0, cells // CELLS, block, 0)


PAD = 8


def main_kernel(relax, exact, blocks, rows, ncols, flat_ref, coef_ref, low_ref, high_ref, kind_ref, code_ref,
                spread_ref, target_ref, factor_ref, wall_ref, sums_ref, stencil_ref,
                out_ref, parts_ref, field_ref, even_ref, strip_ref, half_ref):
    i = pl.program_id(0)
    block = rows * ncols
    span = flat_ref.shape[1]
    edge = 2 * ncols

    @pl.when(i == 0)
    def _():
        for l in range(span // WIDE):
            columns = slice(l * WIDE, (l + 1) * WIDE)
            for ref, start in ((low_ref, 0), (high_ref, edge + blocks * block)):
                values = ref[:, columns]
                field_ref[pl.ds(start, edge), columns] = values if relax else turned(values, l, span)
        strip_ref[...] = jnp.zeros_like(strip_ref)

    @pl.when(i < blocks)
    def _():
        base = edge + i * block

        def store(start, l, values):
            columns = slice(l * WIDE, (l + 1) * WIDE)
            field_ref[pl.ds(pl.multiple_of(base + start, edge), values.shape[0]), columns] = values

        if relax:
            relax_tiles(block, spread_ref, (target_ref, factor_ref, wall_ref), coef_ref, even_ref,
                        flat_ref, store)
        else:
            for l in range(span // WIDE):
                for start in range(0, block, edge):
                    store(start, l, turned(flat_ref[start:start + edge, l * WIDE:(l + 1) * WIDE], l, span))

    @pl.when(i > 0)
    def _():
        base = (i - 1) * block
        nothing = jnp.minimum(i, 0)

        def lanes(l, carry):
            for h in range(WIDE // LANES):
                columns = pl.ds(pl.multiple_of(l * WIDE, WIDE) + h * LANES, LANES)
                table = stencil_ref[:, columns]
                x0, x1, x2, vx, y0, y1, y2, vy = (table[8 * k:8 * k + 8][None] for k in range(8))
                x_up = jnp.broadcast_to(vx > 0, (ncols // 8, 8, LANES))
                ahead = 1 if h == 0 else -1

                def field(k):
                    start = pl.multiple_of(base + k * ncols, ncols)
                    return field_ref[pl.ds(start, ncols), columns].reshape(ncols // 8, 8, LANES)

                for r in range(rows):
                    near = jnp.where(x_up, field(r + 1), field(r + 3))
                    far = jnp.where(x_up, field(r), field(r + 4))
                    rowwise = x0 * field(r + 2) + x1 * near + x2 * far
                    slot = h * rows + r
                    strip_ref[slot, PAD:PAD + ncols, :] = rowwise.reshape(ncols, LANES)

                    def strip(k):
                        return strip_ref[slot, pl.ds(nothing + PAD + k, ncols), :].reshape(ncols // 8, 8, LANES)

                    value = y0 * rowwise + y1 * strip(ahead) + y2 * strip(2 * ahead)
                    value = value.reshape(ncols, LANES)
                    cut = slice(r * ncols, (r + 1) * ncols)
                    out_ref[cut, columns] = value
                    upper = value.astype(jnp.bfloat16)
                    half_ref[0, cut, columns] = upper
                    if exact:
                        half_ref[1, cut, columns] = (value - upper.astype(jnp.float32)).astype(jnp.bfloat16)
            return carry

        lax.fori_loop(0, span // WIDE, lanes, 0)
        table = dot(half_ref[0], sums_ref[...])
        if exact:
            table = table + dot(half_ref[1], sums_ref[...])
        for g in range(block // LANES):
            total = table[g * LANES:(g + 1) * LANES, :].T
            group = (i - 1) * (block // LANES) + g
            kind = kind_ref[pl.ds(group, 1), :]
            code = code_ref[pl.ds(group, 1), :]
            gas = kind == 0

            def keep(*codes):
                hit = (code == codes[0]) | (code == codes[1])
                return jnp.where(gas | jnp.logical_not(hit), 1.0, 0.0)

            kept = (keep(0, 2) * total[0:16] + keep(0, 3) * total[16:32]
                    + keep(1, 2) * total[32:48] + keep(1, 3) * total[48:64])
            incident = jnp.where(code == 0, total[64:65], jnp.where(code == 1, total[65:66], jnp.where(
                code == 2, total[66:67], total[67:68])))
            parts_ref[pl.ds(pl.multiple_of(group * ROWS, ROWS), ROWS), :] = jnp.concatenate(
                [kept[0:10], kept[10:13] + kept[13:16], incident, jnp.zeros((2, LANES), jnp.float32)], axis=0)


def advance(relax, exact, flat, coef, low, high, kind, code, spread, tables, sums, stencil, ncols):
    cells, span = flat.shape
    rows = 8
    block = rows * ncols
    blocks = cells // block
    groups = cells // LANES
    whole = pl.BlockSpec(memory_space=pltpu.VMEM)
    return pl.pallas_call(
        functools.partial(main_kernel, relax, exact, blocks, rows, ncols),
        grid=(blocks + 1,),
        out_shape=(jax.ShapeDtypeStruct((cells, span), jnp.float32),
                   jax.ShapeDtypeStruct((groups * ROWS, LANES), jnp.float32)),
        in_specs=[pl.BlockSpec((block, span), lambda i: (jnp.minimum(i, blocks - 1), 0)),
                  pl.BlockSpec((block, COEF), lambda i: (jnp.minimum(i, blocks - 1), 0)),
                  whole, whole, whole, whole, whole, whole, whole, whole, whole, whole],
        out_specs=(pl.BlockSpec((block, span), lambda i: (jnp.maximum(i - 1, 0), 0)), whole),
        scratch_shapes=[pltpu.VMEM((cells + 4 * ncols, span), jnp.float32),
                        pltpu.VMEM((CELLS, 2 * LANES), jnp.float32),
                        pltpu.VMEM((WIDE // LANES * rows, ncols + 2 * PAD, LANES), jnp.float32),
                        pltpu.VMEM((1 + exact, block, span), jnp.bfloat16)],
        compiler_params=pltpu.CompilerParams(vmem_limit_bytes=VMEM_LIMIT),
        name="advance" if relax else "transport",
    )(flat, coef, low, high, kind, code, spread, *tables, sums, stencil)


def last_kernel(flat_ref, coef_ref, spread_ref, target_ref, factor_ref, wall_ref, out_ref, even_ref):
    span = flat_ref.shape[1]

    def store(start, l, values):
        out_ref[pl.ds(start, CELLS), l * WIDE:(l + 1) * WIDE] = turned(values, l, span, back=True)

    relax_tiles(flat_ref.shape[0], spread_ref, (target_ref, factor_ref, wall_ref), coef_ref, even_ref,
                flat_ref, store)


def finish(flat, coef, spread, tables, ncols):
    cells, span = flat.shape
    block = 8 * ncols
    whole = pl.BlockSpec(memory_space=pltpu.VMEM)
    return pl.pallas_call(
        last_kernel,
        grid=(cells // block,),
        out_shape=jax.ShapeDtypeStruct((cells, span), jnp.float32),
        in_specs=[pl.BlockSpec((block, span), lambda i: (i, 0)),
                  pl.BlockSpec((block, COEF), lambda i: (i, 0)),
                  whole, whole, whole, whole],
        out_specs=pl.BlockSpec((block, span), lambda i: (i, 0)),
        scratch_shapes=[pltpu.VMEM((CELLS, 2 * LANES), jnp.float32)],
        compiler_params=pltpu.CompilerParams(vmem_limit_bytes=VMEM_LIMIT),
        name="finish",
    )(flat, coef, spread, *tables)


def exchange(first, last):
    size = lax.axis_size("space")
    up = [(i, (i + 1) % size) for i in range(size - 1)]
    down = [(j, i) for i, j in up]
    return lax.ppermute(last, "space", up), lax.ppermute(first, "space", down)


def total(parts):
    count = lax.axis_size("vel")
    rows = parts.shape[0] // count
    pieces = parts.reshape(count, rows, LANES)
    swapped = lax.all_to_all(pieces, "vel", 0, 0)
    own = jnp.sum(swapped, axis=0)
    spread = lax.all_to_all(jnp.broadcast_to(own[None], (count, rows, LANES)), "vel", 0, 0)
    return spread.reshape(count * rows, LANES)


def shards(dist, cell_kind, normal_code, wall_temp):
    nrows, ncols, span = dist.shape
    cells = nrows * ncols
    groups = cells // LANES
    kind = cell_kind.reshape(groups, LANES)
    code = normal_code.reshape(groups, LANES)
    temp = wall_temp.reshape(groups, LANES)
    flat = dist.reshape(cells, span)
    target, factor, wall, sums, stencil, spread = setup(span)
    tables = (target, factor, wall)
    edge = 2 * ncols
    coef = jnp.zeros((cells, COEF), jnp.bfloat16)
    low, high = flat[:edge], flat[cells - edge:]
    for step in range(STEPS):
        final = step == STEPS - 1
        low, high = exchange(low, high)
        flat, parts = advance(step > 0, final, flat, coef, low, high, kind, code, spread, tables, sums, stencil, ncols)
        coef, flux, *ends = state(not final, total(parts), kind, code, temp, flat, spread, tables, ncols)
        if not final:
            low, high = ends
    current = finish(flat, coef, spread, tables, ncols)
    columns = ncols // lax.axis_size("vel")
    own_flux = lax.dynamic_slice_in_dim(flux.reshape(nrows, ncols), lax.axis_index("vel") * columns, columns, 1)
    return current.reshape(nrows, ncols, span), own_flux


def solution(mesh):
    placed = (P("space", None, "vel"), P("space", None), P("space", None), P("space", None))
    return jax.shard_map(
        shards,
        mesh=mesh,
        in_specs=placed,
        out_specs=(P("space", None, "vel"), P("space", "vel")),
        check_vma=False,
    )
```

time: 1130 us -> 327 us (0.29)
  other arithmetic: 722 us -> 0.07 us
  Pallas kernels: 0 us -> 167 us
  waiting for transfers between devices: 168 us -> 39.4 us
  matrix products: 79.5 us -> 0 us
  local copies, waits for them, and re-layouts: 47.8 us -> 12.1 us
  between operations: 14.7 us -> 0.8 us
  starting transfers between devices: 21.1 us -> 33 us
    add x18 -> x0, other arithmetic: 473 us -> none  [the longest x7 337 us: relax_shakhov(): return target + (values - target) * jnp.exp(-TIME_STEP / collision_interval)]
    reduce_sum x5 -> x4, other arithmetic: 188 us -> 0.07 us  [total(): own = jnp.sum(swapped, axis=0)]
    psum x5 -> x0, waiting for transfers between devices: 168 us -> none  [the longest x4 132 us: reduce_stats(): total = lax.psum(parts, 'vel')]
    pallas_call x0 -> x10, Pallas kernels: none -> 167 us  [the longest x4 127 us: advance(): pl.pallas_call(functools.partial(main_kernel, relax, exact, blocks, rows,...]
    dot_general x5 -> x0, matrix products: 79.5 us -> none  [project_moments(): jnp.einsum('kv,nv->kn', table, values, precision=lax.Precision.HIGHEST)]
    psum x4 -> x0, blocking collectives: 70 us -> none  [shards(): incident = lax.psum(incident_part, 'vel')]
    all_to_all x0 -> x6, blocking collectives: none -> 68.2 us  [the longest x4 47.8 us: total(): swapped = lax.all_to_all(pieces, 'vel', 0, 0)]
    select_n x4 -> x0, other arithmetic: 57 us -> none  [shards(): bounded = jnp.where(emit, emitted[:, None] * wall_maxwell, flat)]
  transfers between devices with their start and end apart: 13 -> 10, of which waited for: 5 -> 10; matrix products, arithmetic and copies ran while one was open for 18% -> 1% of each run, Pallas kernels for 0% -> 0%
where the time goes in v1:
time: 327 us; the launch traced here: 321 us
  Pallas kernels  167 us (51%)
  blocking collectives  68.2 us (21%)
  waiting for transfers between devices  39.4 us (12%)
  starting transfers between devices  33 us (10%)
  local copies, waits for them, and re-layouts  12.1 us (4%)
    pallas_call x4, Pallas kernels, advance(): pl.pallas_call(functools.partial(main_kernel, relax, exact, blocks, rows,...  127 us
    all_to_all x4, blocking collectives, total(): swapped = lax.all_to_all(pieces, 'vel', 0, 0)  47.8 us
    ppermute x8, starting transfers between devices, exchange(): return (lax.ppermute(last, 'space', up), lax.ppermute(first, 'space', down))  26.2 us
    ppermute x8, waiting for transfers between devices, exchange(): return (lax.ppermute(last, 'space', up), lax.ppermute(first, 'space', down))  25.4 us
    pallas_call x4, Pallas kernels, state(): pl.pallas_call(functools.partial(state_kernel, groups, with_edges), grid=...  20.9 us
    all_to_all x2, blocking collectives, total(): lax.all_to_all(jnp.broadcast_to(own[None], (count, rows, LANES)), 'vel',...  20.4 us
    pallas_call x1, Pallas kernels, finish(): pl.pallas_call(last_kernel, grid=(cells // block,), out_shape=jax.ShapeDt...  17.6 us
    all_to_all x2, waiting for transfers between devices, total(): lax.all_to_all(jnp.broadcast_to(own[None], (count, rows, LANES)), 'vel',...  14 us
  transfers between devices with their start and end apart: 10, of which 10 were waited for; matrix products, arithmetic and copies ran while one was open for 1% of the time, Pallas kernels for 0%

profile of v1, /device:TPU:4, one launch (start us, length us, event | category | flops | bytes accessed | tf_op | source)
XLA Modules:
  0.0 320.6 jit_solution(12057571299995191382)
XLA Ops:
  0.6 0.0 copy-start.10
  0.6 1.3 fusion
  1.9 1.9 collective-permute-start
  3.8 4.5 %collective-permute-start.1 = (f32[128,1024]{1,0:T(8,128)S(1)}, f32[128,1024]{1,0:T(8,128)S(1)}, u32[]{:S(2)}, u32[]{:S(2)}) collective-permute-start(f32[128,1024]{1,0:T(8,128)S(1)} %bitcast.18), channel_id=1, source_target_pairs={{4,0},{8,4},{12,8},{16,12},{20,16},{24,20},{28,24},{5,1},{9,5},{13... | collective-permute-start | bytes 1572872 | tf_op jit(solution)/shard_map/ppermute | solution.py:461
  8.4 1.4 setup.1
  9.8 1.4 reshape.53.kind_ref
  11.2 1.4 reshape.54.code_ref
  12.6 3.5 %collective-permute-done.low_ref = f32[128,1024]{1,0:T(8,128)S(1)} collective-permute-done((f32[128,1024]{1,0:T(8,128)S(1)}, f32[128,1024]{1,0:T(8,128)S(1)}, u32[]{:S(2)}, u32[]{:S(2)}) %collective-permute-start) | collective-permute-done | bytes 524320 | tf_op jit(solution)/shard_map/ppermute | solution.py:461
  16.1 0.0 copy-start.2
  16.1 0.9 collective-permute-done.1.high_ref
  17.0 0.0 copy-start.3
  17.0 1.2 broadcast_in_dim.10.coef_ref
  18.2 0.0 copy-done.2
  18.2 0.0 copy-done.3
  18.2 27.3 %transport.1 = (f32[4096,1024]{1,0:T(8,128)}, f32[512,128]{1,0:T(8,128)}) custom-call(f32[4096,1024]{1,0:T(8,128)} %bitcast.12, bf16[4096,128]{1,0:T(8,128)(2,1)} %broadcast_in_dim.10.coef_ref, f32[128,1024]{1,0:T(8,128)} %copy-done.2, f32[128,1024]{1,0:T(8,128)} %copy-done.3, s32[32,128]{1,0:T(8,128)} %reshape.53.kind_ref, s32[32,128]{1,0:T(8,128)} %reshape.54.code_ref, ...), custom_call_target="tpu_custom_call" | custom-call | tf_op jit(solution)/shard_map/transport/pallas_call | solution.py:411
  45.5 13.1 %all_to_all.40 = f32[4,128,128]{2,1,0:T(8,128)S(1)} all-to-all(f32[4,128,128]{2,1,0:T(8,128)} %bitcast.23), channel_id=1, replica_groups=mesh['space'=8,'vel'=4] {'vel'}, dimensions={0} | all-to-all | bytes 524288 | tf_op jit(solution)/shard_map/all_to_all | solution.py:468
  58.7 0.7 broadcast_in_dim.11
  59.4 3.4 %all-to-all-start.1 = ((f32[4,128,128]{2,1,0:T(8,128)}), f32[4,128,128]{2,1,0:T(8,128)S(1)}, u32[]{:S(2)}, u32[]{:S(2)}) async-start(f32[4,128,128]{2,1,0:T(8,128)} %broadcast_in_dim.11), calls=%async_computation.1 | async-start | bytes 524288 | tf_op jit(solution)/shard_map/all_to_all | solution.py:470
  62.8 0.0 copy-done.10
  62.8 0.7 reshape.57.temp_ref
  63.5 7.3 %all-to-all-done.1 = f32[4,128,128]{2,1,0:T(8,128)S(1)} async-done(((f32[4,128,128]{2,1,0:T(8,128)}), f32[4,128,128]{2,1,0:T(8,128)S(1)}, u32[]{:S(2)}, u32[]{:S(2)}) %all-to-all-start.1) | async-done | bytes 262176 | tf_op jit(solution)/shard_map/all_to_all | solution.py:470
  70.7 0.0 copy-start.1
  70.7 0.7 copy-done.1
  71.4 5.3 %state.4 = (bf16[4096,128]{1,0:T(8,128)(2,1)}, f32[32,128]{1,0:T(8,128)}, f32[128,1024]{1,0:T(8,128)}, f32[128,1024]{1,0:T(8,128)}) custom-call(f32[512,128]{1,0:T(8,128)} %bitcast.15, s32[32,128]{1,0:T(8,128)} %reshape.53.kind_ref, s32[32,128]{1,0:T(8,128)} %reshape.54.code_ref, f32[32,128]{1,0:T(8,128)} %reshape.57.temp_ref, ...), custom_call_target="tpu_custom_call" | custom-call | tf_op jit(solution)/shard_map/state/pallas_call | solution.py:261
  76.8 1.9 collective-permute-start.2
  78.7 4.7 %collective-permute-start.3 = (f32[128,1024]{1,0:T(8,128)}, f32[128,1024]{1,0:T(8,128)S(1)}, u32[]{:S(2)}, u32[]{:S(2)}) collective-permute-start(f32[128,1024]{1,0:T(8,128)} %get-tuple-element.37), channel_id=1, source_target_pairs={{4,0},{8,4},{12,8},{16,12},{20,16},{24,20},{28,24},{5,1},{9,5},{13... | collective-permute-start | bytes 1572872 | tf_op jit(solution)/shard_map/ppermute | solution.py:461
  83.4 5.1 %collective-permute-done.2.low_ref = f32[128,1024]{1,0:T(8,128)S(1)} collective-permute-done((f32[128,1024]{1,0:T(8,128)}, f32[128,1024]{1,0:T(8,128)S(1)}, u32[]{:S(2)}, u32[]{:S(2)}) %collective-permute-start.2) | collective-permute-done | bytes 524320 | tf_op jit(solution)/shard_map/ppermute | solution.py:461
  88.5 1.9 collective-permute-done.3.high_ref
  90.4 0.0 copy-start.8
  90.4 0.0 copy-done.5
  90.4 0.8 copy-done.8
  91.2 31.8 %advance.3 = (f32[4096,1024]{1,0:T(8,128)}, f32[512,128]{1,0:T(8,128)}) custom-call(f32[4096,1024]{1,0:T(8,128)} %get-tuple-element.33.first_ref.last_ref.flat_ref, bf16[4096,128]{1,0:T(8,128)(2,1)} %get-tuple-element.35.coef_ref, f32[128,1024]{1,0:T(8,128)} %copy-done.5, f32[128,1024]{1,0:T(8,128)} %copy-done.8, s32[32,128]{1,0:T(8,128)} %reshape.53.kind_ref, ...), custom_call_target="tpu_custom_call" | custom-call | tf_op jit(solution)/shard_map/advance/pallas_call | solution.py:411
  123.0 10.8 %all_to_all.41 = f32[4,128,128]{2,1,0:T(8,128)S(1)} all-to-all(f32[4,128,128]{2,1,0:T(8,128)} %bitcast.21), channel_id=1, replica_groups=mesh['space'=8,'vel'=4] {'vel'}, dimensions={0} | all-to-all | bytes 524288 | tf_op jit(solution)/shard_map/all_to_all | solution.py:468
  133.8 10.2 %all_to_all.42 = f32[4,128,128]{2,1,0:T(8,128)} all-to-all(f32[4,128,128]{2,1,0:T(8,128)S(1)} %broadcast_in_dim.12), channel_id=1, replica_groups=mesh['space'=8,'vel'=4] {'vel'}, dimensions={0} | all-to-all | bytes 524288 | tf_op jit(solution)/shard_map/all_to_all | solution.py:470
  144.0 5.3 %state.5 = (bf16[4096,128]{1,0:T(8,128)(2,1)}, f32[32,128]{1,0:T(8,128)}, f32[128,1024]{1,0:T(8,128)}, f32[128,1024]{1,0:T(8,128)}) custom-call(f32[512,128]{1,0:T(8,128)} %bitcast.16, s32[32,128]{1,0:T(8,128)} %reshape.53.kind_ref, s32[32,128]{1,0:T(8,128)} %reshape.54.code_ref, f32[32,128]{1,0:T(8,128)} %reshape.57.temp_ref, ...), custom_call_target="tpu_custom_call" | custom-call | tf_op jit(solution)/shard_map/state/pallas_call | solution.py:261
  149.3 1.9 collective-permute-start.4
  151.2 4.5 %collective-permute-start.5 = (f32[128,1024]{1,0:T(8,128)}, f32[128,1024]{1,0:T(8,128)S(1)}, u32[]{:S(2)}, u32[]{:S(2)}) collective-permute-start(f32[128,1024]{1,0:T(8,128)} %get-tuple-element.42), channel_id=1, source_target_pairs={{4,0},{8,4},{12,8},{16,12},{20,16},{24,20},{28,24},{5,1},{9,5},{13... | collective-permute-start | bytes 1572872 | tf_op jit(solution)/shard_map/ppermute | solution.py:461
  155.8 5.1 %collective-permute-done.4.low_ref = f32[128,1024]{1,0:T(8,128)S(1)} collective-permute-done((f32[128,1024]{1,0:T(8,128)}, f32[128,1024]{1,0:T(8,128)S(1)}, u32[]{:S(2)}, u32[]{:S(2)}) %collective-permute-start.4) | collective-permute-done | bytes 524320 | tf_op jit(solution)/shard_map/ppermute | solution.py:461
  160.9 0.0 copy-start.6
  160.9 1.9 collective-permute-done.5.high_ref
  162.8 0.0 copy-done.6
  162.8 0.8 copy-done.9
  163.6 31.7 %advance.4 = (f32[4096,1024]{1,0:T(8,128)}, f32[512,128]{1,0:T(8,128)}) custom-call(f32[4096,1024]{1,0:T(8,128)} %get-tuple-element.38.first_ref.last_ref.flat_ref, bf16[4096,128]{1,0:T(8,128)(2,1)} %get-tuple-element.40.coef_ref, f32[128,1024]{1,0:T(8,128)} %copy-done.6, f32[128,1024]{1,0:T(8,128)} %copy-done.9, s32[32,128]{1,0:T(8,128)} %reshape.53.kind_ref, ...), custom_call_target="tpu_custom_call" | custom-call | tf_op jit(solution)/shard_map/advance/pallas_call | solution.py:411
  195.3 12.0 %all_to_all.43 = f32[4,128,128]{2,1,0:T(8,128)S(1)} all-to-all(f32[4,128,128]{2,1,0:T(8,128)} %bitcast.22), channel_id=1, replica_groups=mesh['space'=8,'vel'=4] {'vel'}, dimensions={0} | all-to-all | bytes 524288 | tf_op jit(solution)/shard_map/all_to_all | solution.py:468
  207.3 10.2 %all_to_all.44 = f32[4,128,128]{2,1,0:T(8,128)} all-to-all(f32[4,128,128]{2,1,0:T(8,128)S(1)} %broadcast_in_dim.13), channel_id=1, replica_groups=mesh['space'=8,'vel'=4] {'vel'}, dimensions={0} | all-to-all | bytes 524288 | tf_op jit(solution)/shard_map/all_to_all | solution.py:470
  217.5 5.3 %state.6 = (bf16[4096,128]{1,0:T(8,128)(2,1)}, f32[32,128]{1,0:T(8,128)}, f32[128,1024]{1,0:T(8,128)}, f32[128,1024]{1,0:T(8,128)}) custom-call(f32[512,128]{1,0:T(8,128)} %bitcast.17, s32[32,128]{1,0:T(8,128)} %reshape.53.kind_ref, s32[32,128]{1,0:T(8,128)} %reshape.54.code_ref, f32[32,128]{1,0:T(8,128)} %reshape.57.temp_ref, ...), custom_call_target="tpu_custom_call" | custom-call | tf_op jit(solution)/shard_map/state/pallas_call | solution.py:261
  222.9 1.9 collective-permute-start.6
  224.8 4.7 %collective-permute-start.7 = (f32[128,1024]{1,0:T(8,128)}, f32[128,1024]{1,0:T(8,128)S(1)}, u32[]{:S(2)}, u32[]{:S(2)}) collective-permute-start(f32[128,1024]{1,0:T(8,128)} %get-tuple-element.47), channel_id=1, source_target_pairs={{4,0},{8,4},{12,8},{16,12},{20,16},{24,20},{28,24},{5,1},{9,5},{13... | collective-permute-start | bytes 1572872 | tf_op jit(solution)/shard_map/ppermute | solution.py:461
  229.5 5.0 %collective-permute-done.6.low_ref = f32[128,1024]{1,0:T(8,128)S(1)} collective-permute-done((f32[128,1024]{1,0:T(8,128)}, f32[128,1024]{1,0:T(8,128)S(1)}, u32[]{:S(2)}, u32[]{:S(2)}) %collective-permute-start.6) | collective-permute-done | bytes 524320 | tf_op jit(solution)/shard_map/ppermute | solution.py:461
  234.5 2.0 collective-permute-done.7.high_ref
  236.5 0.0 copy-done.4
  236.5 0.8 copy-done.7
  237.3 36.4 %advance.5 = (f32[4096,1024]{1,0:T(8,128)}, f32[512,128]{1,0:T(8,128)}) custom-call(f32[4096,1024]{1,0:T(8,128)} %get-tuple-element.43.first_ref.last_ref.flat_ref, bf16[4096,128]{1,0:T(8,128)(2,1)} %get-tuple-element.45.coef_ref, f32[128,1024]{1,0:T(8,128)} %copy-done.4, f32[128,1024]{1,0:T(8,128)} %copy-done.7, s32[32,128]{1,0:T(8,128)} %reshape.53.kind_ref, ...), custom_call_target="tpu_custom_call" | custom-call | tf_op jit(solution)/shard_map/advance/pallas_call | solution.py:411
  273.7 12.0 %all_to_all.45 = f32[4,128,128]{2,1,0:T(8,128)S(1)} all-to-all(f32[4,128,128]{2,1,0:T(8,128)} %bitcast.20), channel_id=1, replica_groups=mesh['space'=8,'vel'=4] {'vel'}, dimensions={0} | all-to-all | bytes 524288 | tf_op jit(solution)/shard_map/all_to_all | solution.py:468
  285.7 0.7 broadcast_in_dim.14
  286.4 3.4 %all-to-all-start.7 = ((f32[4,128,128]{2,1,0:T(8,128)}), f32[4,128,128]{2,1,0:T(8,128)S(1)}, u32[]{:S(2)}, u32[]{:S(2)}) async-start(f32[4,128,128]{2,1,0:T(8,128)} %broadcast_in_dim.14), calls=%async_computation.7 | async-start | bytes 524288 | tf_op jit(solution)/shard_map/all_to_all | solution.py:470
  289.8 6.7 %all-to-all-done.7 = f32[4,128,128]{2,1,0:T(8,128)S(1)} async-done(((f32[4,128,128]{2,1,0:T(8,128)}), f32[4,128,128]{2,1,0:T(8,128)S(1)}, u32[]{:S(2)}, u32[]{:S(2)}) %all-to-all-start.7) | async-done | bytes 262176 | tf_op jit(solution)/shard_map/all_to_all | solution.py:470
  296.6 0.7 copy-done
  297.3 4.9 %state.7 = (bf16[4096,128]{1,0:T(8,128)(2,1)}, f32[32,128]{1,0:T(8,128)}) custom-call(f32[512,128]{1,0:T(8,128)} %bitcast.14, s32[32,128]{1,0:T(8,128)} %reshape.53.kind_ref, s32[32,128]{1,0:T(8,128)} %reshape.54.code_ref, f32[32,128]{1,0:T(8,128)} %reshape.57.temp_ref, f32[4096,1024]{1,0:T(8,128)} %get-tuple-element.48.first_ref.last_ref.flat_ref, ...), custom_call_target="tpu_custom_call" | custom-call | tf_op jit(solution)/shard_map/state/pallas_call | solution.py:261
  302.2 17.6 %finish.1 = f32[4096,1024]{1,0:T(8,128)} custom-call(f32[4096,1024]{1,0:T(8,128)} %get-tuple-element.48.first_ref.last_ref.flat_ref, bf16[4096,128]{1,0:T(8,128)(2,1)} %get-tuple-element.50.coef_ref, bf16[128,256]{1,0:T(8,128)(2,1)} %get-tuple-element.27.spread_ref, bf16[128,1024]{1,0:T(8,128)(2,1)} %get-tuple-element.28.target_ref, ...), custom_call_target="tpu_custom_call" | custom-call | tf_op jit(solution)/shard_map/finish/pallas_call | solution.py:443
  319.8 0.0 copy-done.11
  319.8 0.1 reshape.65
  319.9 0.1 constant_dynamic-slice_fusion
  320.0 0.7 copy.7
  (12 shorter events, 0.1 us)
Async XLA Ops:
  0.6 62.2 %copy-start.10 = (f32[64,64]{1,0:T(8,128)S(1)}, f32[64,64]{1,0:T(8,128)}, u32[]{:S(2)}) copy-start(f32[64,64]{1,0:T(8,128)} %param.7) | copy-start | bytes 49156
  1.9 14.2 %collective-permute-start = (f32[128,1024]{1,0:T(8,128)S(1)}, f32[128,1024]{1,0:T(8,128)S(1)}, u32[]{:S(2)}, u32[]{:S(2)}) collective-permute-start(f32[128,1024]{1,0:T(8,128)S(1)} %bitcast.19), channel_id=1, source_target_pairs={{0,4},{4,8},{8,12},{12,16},{16,20},{20,24},{24,28},{1,5},{5,9},{9,... | collective-permute-start | bytes 1572872 | tf_op jit(solution)/shard_map/ppermute | solution.py:461
  3.8 13.2 %collective-permute-start.1 = (f32[128,1024]{1,0:T(8,128)S(1)}, f32[128,1024]{1,0:T(8,128)S(1)}, u32[]{:S(2)}, u32[]{:S(2)}) collective-permute-start(f32[128,1024]{1,0:T(8,128)S(1)} %bitcast.18), channel_id=1, source_target_pairs={{4,0},{8,4},{12,8},{16,12},{20,16},{24,20},{28,24},{5,1},{9,5},{13... | collective-permute-start | bytes 1572872 | tf_op jit(solution)/shard_map/ppermute | solution.py:461
  16.1 2.1 copy-start.2
  17.0 1.2 copy-start.3
  59.4 11.3 %all-to-all-start.1 = ((f32[4,128,128]{2,1,0:T(8,128)}), f32[4,128,128]{2,1,0:T(8,128)S(1)}, u32[]{:S(2)}, u32[]{:S(2)}) async-start(f32[4,128,128]{2,1,0:T(8,128)} %broadcast_in_dim.11), calls=%async_computation.1 | async-start | bytes 524288 | tf_op jit(solution)/shard_map/all_to_all | solution.py:470
  70.7 0.7 copy-start.1
  76.8 11.8 %collective-permute-start.2 = (f32[128,1024]{1,0:T(8,128)}, f32[128,1024]{1,0:T(8,128)S(1)}, u32[]{:S(2)}, u32[]{:S(2)}) collective-permute-start(f32[128,1024]{1,0:T(8,128)} %get-tuple-element.36), channel_id=1, source_target_pairs={{0,4},{4,8},{8,12},{12,16},{16,20},{20,24},{24,28},{1,5},{5,9},{9,... | collective-permute-start | bytes 1572872 | tf_op jit(solution)/shard_map/ppermute | solution.py:461
  78.7 11.7 %collective-permute-start.3 = (f32[128,1024]{1,0:T(8,128)}, f32[128,1024]{1,0:T(8,128)S(1)}, u32[]{:S(2)}, u32[]{:S(2)}) collective-permute-start(f32[128,1024]{1,0:T(8,128)} %get-tuple-element.37), channel_id=1, source_target_pairs={{4,0},{8,4},{12,8},{16,12},{20,16},{24,20},{28,24},{5,1},{9,5},{13... | collective-permute-start | bytes 1572872 | tf_op jit(solution)/shard_map/ppermute | solution.py:461
  88.5 1.9 copy-start.5
  90.4 0.8 copy-start.8
  149.3 11.6 %collective-permute-start.4 = (f32[128,1024]{1,0:T(8,128)}, f32[128,1024]{1,0:T(8,128)S(1)}, u32[]{:S(2)}, u32[]{:S(2)}) collective-permute-start(f32[128,1024]{1,0:T(8,128)} %get-tuple-element.41), channel_id=1, source_target_pairs={{0,4},{4,8},{8,12},{12,16},{16,20},{20,24},{24,28},{1,5},{5,9},{9,... | collective-permute-start | bytes 1572872 | tf_op jit(solution)/shard_map/ppermute | solution.py:461
  151.2 11.5 %collective-permute-start.5 = (f32[128,1024]{1,0:T(8,128)}, f32[128,1024]{1,0:T(8,128)S(1)}, u32[]{:S(2)}, u32[]{:S(2)}) collective-permute-start(f32[128,1024]{1,0:T(8,128)} %get-tuple-element.42), channel_id=1, source_target_pairs={{4,0},{8,4},{12,8},{16,12},{20,16},{24,20},{28,24},{5,1},{9,5},{13... | collective-permute-start | bytes 1572872 | tf_op jit(solution)/shard_map/ppermute | solution.py:461
  160.9 1.9 copy-start.6
  162.8 0.8 copy-start.9
  222.9 11.6 %collective-permute-start.6 = (f32[128,1024]{1,0:T(8,128)}, f32[128,1024]{1,0:T(8,128)S(1)}, u32[]{:S(2)}, u32[]{:S(2)}) collective-permute-start(f32[128,1024]{1,0:T(8,128)} %get-tuple-element.46), channel_id=1, source_target_pairs={{0,4},{4,8},{8,12},{12,16},{16,20},{20,24},{24,28},{1,5},{5,9},{9,... | collective-permute-start | bytes 1572872 | tf_op jit(solution)/shard_map/ppermute | solution.py:461
  224.8 11.7 %collective-permute-start.7 = (f32[128,1024]{1,0:T(8,128)}, f32[128,1024]{1,0:T(8,128)S(1)}, u32[]{:S(2)}, u32[]{:S(2)}) collective-permute-start(f32[128,1024]{1,0:T(8,128)} %get-tuple-element.47), channel_id=1, source_target_pairs={{4,0},{8,4},{12,8},{16,12},{20,16},{24,20},{28,24},{5,1},{9,5},{13... | collective-permute-start | bytes 1572872 | tf_op jit(solution)/shard_map/ppermute | solution.py:461
  234.5 2.0 copy-start.4
  236.5 0.8 copy-start.7
  286.4 10.2 %all-to-all-start.7 = ((f32[4,128,128]{2,1,0:T(8,128)}), f32[4,128,128]{2,1,0:T(8,128)S(1)}, u32[]{:S(2)}, u32[]{:S(2)}) async-start(f32[4,128,128]{2,1,0:T(8,128)} %broadcast_in_dim.14), calls=%async_computation.7 | async-start | bytes 524288 | tf_op jit(solution)/shard_map/all_to_all | solution.py:470
  296.6 0.7 copy-start
  302.2 17.6 %copy-start.11 = (f32[32,128]{1,0:T(8,128)S(1)}, f32[32,128]{1,0:T(8,128)}, u32[]{:S(2)}) copy-start(f32[32,128]{1,0:T(8,128)} %get-tuple-element.51) | copy-start | bytes 49156

commit v2 on v1

--- a/solution.py
+++ b/solution.py
@@ -22,7 +22,9 @@
 WEIGHT = SPACING**3 / (2.0 * math.pi) ** 1.5
 LOG2E = math.log2(math.e)
 LANES = 128
-ROWS = 16
+MOMENTS = 16
+ROWS = 14
+GAS = 10
 OFF = 1024.0
 
 T_SQ_HI, T_SQ_LO, T_X, T_Y, T_Z, T_ONE = range(6)
@@ -31,7 +33,8 @@
 W_SQ_HI, W_SQ_LO, W_ONE, W_XP, W_XN, W_YP, W_YN = range(22, 29)
 B_E, B_W = 29, 30
 PART = 32
-COEF = 128
+COEF = 2 * PART
+STRIDE = COEF + 1
 
 VMEM_LIMIT = 60 * 1024 * 1024
 
@@ -69,18 +72,17 @@
     for k, feature in enumerate(features):
         feature_ref[k:k + 1, :] = feature[0:1]
     row = lax.broadcasted_iota(jnp.int32, (PART, span), 0)
-    blank = jnp.zeros((COEF - 3 * PART, span), jnp.float32)
     for ref, low, high in ((target_ref, T_SQ_HI, P_ONE), (factor_ref, P_ONE, W_SQ_HI),
                            (wall_ref, W_SQ_HI, B_E)):
         chosen = jnp.where((row >= low) & (row < high), feature_ref[...], 0.0)
-        ref[...] = jnp.concatenate([chosen, chosen, chosen, blank], axis=0).astype(jnp.bfloat16)
+        ref[...] = jnp.concatenate([chosen, chosen], axis=0).astype(jnp.bfloat16)
     quadrants = (xp * yp, xp * (one - yp), (one - xp) * yp, (one - xp) * (one - yp))
     moment = feature_ref[P_ONE:W_SQ_HI, :]
     moment_ref[...] = jnp.zeros_like(moment_ref)
     for k, quadrant in enumerate(quadrants):
-        moment_ref[ROWS * k:ROWS * (k + 1), :] = moment * quadrant[0:1]
+        moment_ref[MOMENTS * k:MOMENTS * (k + 1), :] = moment * quadrant[0:1]
     for k, speed in enumerate((-x, x, -y, y)):
-        moment_ref[4 * ROWS + k:4 * ROWS + k + 1, :] = jnp.maximum(speed, 0.0)[0:1]
+        moment_ref[4 * MOMENTS + k:4 * MOMENTS + k + 1, :] = jnp.maximum(speed, 0.0)[0:1]
     for l in range(span // LANES):
         cut = slice(l * LANES, (l + 1) * LANES)
         sums_ref[cut, :] = moment_ref[:, cut].T.astype(jnp.bfloat16)
@@ -93,7 +95,7 @@
     row = lax.broadcasted_iota(jnp.int32, (COEF, 2 * LANES), 0)
     column = lax.broadcasted_iota(jnp.int32, (COEF, 2 * LANES), 1)
     want = jnp.where(column < LANES, B_E, B_W)
-    hit = (row % PART == want) & (row < 3 * PART)
+    hit = row % PART == want
     spread_ref[...] = jnp.where(hit, 1.0, 0.0).astype(jnp.bfloat16)
 
 
@@ -121,16 +123,20 @@
     return jnp.dot(a, b, preferred_element_type=jnp.float32)
 
 
-def state_kernel(groups, with_edges, sums_ref, kind_ref, code_ref, temp_ref, first_ref, last_ref, spread_ref,
-                 target_ref, factor_ref, wall_ref, coef_ref, flux_ref, *outer):
-    stack_ref = outer[-1]
+def gas_kernel(count, size, *refs):
+    part_refs = refs[:count]
+    kind_ref, code_ref, temp_ref, out_ref = refs[count:]
+    mine = pl.ds(pl.multiple_of(lax.axis_index("vel") * size, size), size)
 
     def read(k, scale):
-        return sums_ref[pl.ds(k, groups, stride=ROWS), :] * (WEIGHT * scale)
-
-    kind = kind_ref[...]
-    code = code_ref[...]
-    wall = temp_ref[...]
+        value = part_refs[0][pl.ds(k, size, stride=ROWS), :]
+        for ref in part_refs[1:]:
+            value = value + ref[pl.ds(k, size, stride=ROWS), :]
+        return value * (WEIGHT * scale)
+
+    kind = kind_ref[mine, :]
+    code = code_ref[mine, :]
+    wall = temp_ref[mine, :]
     s0 = s1 = s2 = s3 = jnp.zeros_like(wall)
     inverse = 1.0 / wall
     for j in range(NQ // 2):
@@ -148,7 +154,7 @@
     share = jnp.where(kind == 2, SIGMA, 0.0)
     emitted = share * saturated + (1.0 - share) * incident / norm
     boundary = kind > 0
-    flux_ref[...] = jnp.where(boundary, emitted * norm - incident, 0.0)
+    flux = jnp.where(boundary, emitted * norm - incident, 0.0)
     em = jnp.where(boundary, emitted, 0.0)
     along_x = code < 2
     sign = jnp.where((code == 0) | (code == 2), 1.0, -1.0)
@@ -184,6 +190,45 @@
     qx = heat(mxs, ux, mx, (mxx, mxy, mxz))
     qy = heat(mys, uy, my, (mxy, myy, myz))
     qz = heat(mzs, uz, mz, (mxz, myz, mzz))
+    for k, value in enumerate((rho, ux, uy, uz, temp, qx, qy, qz, em, flux)):
+        out_ref[k * size:(k + 1) * size, :] = value
+
+
+def gas(parts, kind, code, temp):
+    size = parts[0].shape[0] // ROWS
+    whole = pl.BlockSpec(memory_space=pltpu.VMEM)
+    return pl.pallas_call(
+        functools.partial(gas_kernel, len(parts), size),
+        out_shape=jax.ShapeDtypeStruct((GAS * size, LANES), jnp.float32),
+        in_specs=[whole] * (len(parts) + 3),
+        out_specs=whole,
+        name="gas",
+    )(*parts, kind, code, temp)
+
+
+def state_kernel(count, groups, with_edges, *refs):
+    piece_refs = refs[:count]
+    kind_ref, code_ref, temp_ref, *refs = refs[count:]
+    if with_edges:
+        first_ref, last_ref, spread_ref, target_ref, factor_ref, wall_ref, coef_ref, low_ref, high_ref, *refs = refs
+    else:
+        coef_ref, flux_ref, *refs = refs
+    stack_ref, field_ref = refs
+    size = groups // count
+    me = lax.axis_index("vel")
+    for away, ref in enumerate(piece_refs):
+        owner = lax.rem(me + (count - away), count)
+        for k in range(GAS):
+            field_ref[k, pl.ds(pl.multiple_of(owner * size, size), size), :] = ref[k * size:(k + 1) * size, :]
+    kind = kind_ref[...]
+    code = code_ref[...]
+    wall = temp_ref[...]
+    rho, ux, uy, uz, temp, qx, qy, qz, em, flux = (field_ref[k] for k in range(GAS))
+    if not with_edges:
+        flux_ref[...] = flux
+    inverse = 1.0 / wall
+    uu = ux * ux + uy * uy + uz * uz
+    boundary = kind > 0
     pressure = rho * temp
     per_t = 1.0 / temp
     decay = jnp.exp((-TIME_STEP / SHEAR_EXPONENT) * pressure * jnp.exp(-0.72 * jnp.log(temp)))
@@ -219,25 +264,22 @@
     zero = jnp.zeros_like(wall)
     for k in range(PART):
         value = rows.get(k)
-        for part in range(3):
+        for part in range(2):
             if value is None:
-                stack_ref[pl.ds(part * PART + k, groups, stride=COEF), :] = zero
+                stack_ref[pl.ds(part * PART + k, groups, stride=STRIDE), :] = zero
                 continue
             hi = value.astype(jnp.bfloat16).astype(jnp.float32)
-            stack_ref[pl.ds(part * PART + k, groups, stride=COEF), :] = hi
+            stack_ref[pl.ds(part * PART + k, groups, stride=STRIDE), :] = hi
             value = value - hi
-    blank = jnp.zeros((COEF - 3 * PART, LANES), jnp.float32)
 
     def turn(g, carry):
-        start = pl.multiple_of(g * COEF, COEF)
-        block = jnp.concatenate([stack_ref[pl.ds(start, 3 * PART), :], blank], axis=0)
-        coef_ref[pl.ds(start, LANES), :] = block.T.astype(jnp.bfloat16)
+        block = stack_ref[pl.ds(g * STRIDE, COEF), :]
+        coef_ref[pl.ds(pl.multiple_of(g * LANES, LANES), LANES), :] = block.T.astype(jnp.bfloat16)
         return carry
 
-    lax.fori_loop(0, groups, turn, 0, unroll=4)
+    lax.fori_loop(0, groups, turn, 0, unroll=8)
     if not with_edges:
         return
-    low_ref, high_ref = outer[:2]
     size = low_ref.shape[0]
     for flat_ref, start, out_ref in ((first_ref, 0, low_ref), (last_ref, groups * LANES - size, high_ref)):
         coef = coef_ref[start:start + size, :]
@@ -248,27 +290,33 @@
                                           factor_ref[:, columns], wall_ref[:, columns])
 
 
-def state(with_edges, sums, kind, code, temp, flat, spread, tables, ncols):
+def state(with_edges, pieces, kind, code, temp, flat, spread, tables, ncols):
     groups = kind.shape[0]
     cells, span = flat.shape
     size = 2 * ncols
     last = cells // size - 1
     whole = pl.BlockSpec(memory_space=pltpu.VMEM)
-    out_shape = (jax.ShapeDtypeStruct((cells, COEF), jnp.bfloat16),
-                 jax.ShapeDtypeStruct((groups, LANES), jnp.float32))
+    operands = [*pieces, kind, code, temp]
+    in_specs = [whole] * len(operands)
+    out_shape = (jax.ShapeDtypeStruct((cells, COEF), jnp.bfloat16),)
     if with_edges:
+        operands += [flat, flat, spread, *tables]
+        in_specs += [pl.BlockSpec((size, span), lambda i: (0, 0)),
+                     pl.BlockSpec((size, span), lambda i: (last, 0))] + [whole] * 4
         out_shape += (jax.ShapeDtypeStruct((size, span), jnp.float32),) * 2
+    else:
+        out_shape += (jax.ShapeDtypeStruct((groups, LANES), jnp.float32),)
     return pl.pallas_call(
-        functools.partial(state_kernel, groups, with_edges),
+        functools.partial(state_kernel, len(pieces), groups, with_edges),
         grid=(1,),
         out_shape=out_shape,
-        in_specs=[whole] * 4 + [pl.BlockSpec((size, span), lambda i: (0, 0)),
-                                pl.BlockSpec((size, span), lambda i: (last, 0))] + [whole] * 4,
+        in_specs=in_specs,
         out_specs=(whole,) * len(out_shape),
-        scratch_shapes=[pltpu.VMEM((groups * COEF, LANES), jnp.float32)],
+        scratch_shapes=[pltpu.VMEM((groups * STRIDE + 7, LANES), jnp.float32),
+                        pltpu.VMEM((GAS, groups, LANES), jnp.float32)],
         compiler_params=pltpu.CompilerParams(vmem_limit_bytes=VMEM_LIMIT),
         name="state",
-    )(sums, kind, code, temp, flat, flat, spread, *tables)
+    )(*operands)
 
 
 CELLS = 256
@@ -306,124 +354,190 @@
 
 
 PAD = 8
-
-
-def main_kernel(relax, exact, blocks, rows, ncols, flat_ref, coef_ref, low_ref, high_ref, kind_ref, code_ref,
-                spread_ref, target_ref, factor_ref, wall_ref, sums_ref, stencil_ref,
-                out_ref, parts_ref, field_ref, even_ref, strip_ref, half_ref):
+BLOCK = 8
+
+
+def transport(exact, field_ref, base, ncols, group, kind_ref, code_ref, sums_ref, stencil_ref,
+              out_ref, parts_ref, strip_ref, half_ref):
+    span = out_ref.shape[1]
+    nothing = jnp.minimum(pl.program_id(0), 0)
+    table = None
+    for l in range(span // WIDE):
+        for h in range(WIDE // LANES):
+            columns = slice(l * WIDE + h * LANES, l * WIDE + (h + 1) * LANES)
+            x0, x1, x2, vx, y0, y1, y2, vy = (stencil_ref[8 * k:8 * k + 8, columns][None] for k in range(8))
+            x_up = jnp.broadcast_to(vx > 0, (ncols // 8, 8, LANES))
+            ahead = 1 if h == 0 else -1
+
+            def field(k):
+                start = pl.multiple_of(base + k * ncols, ncols)
+                return field_ref[pl.ds(start, ncols), columns].reshape(ncols // 8, 8, LANES)
+
+            for r in range(BLOCK):
+                near = jnp.where(x_up, field(r + 1), field(r + 3))
+                far = jnp.where(x_up, field(r), field(r + 4))
+                rowwise = x0 * field(r + 2) + x1 * near + x2 * far
+                slot = h * BLOCK + r
+                strip_ref[slot, PAD:PAD + ncols, :] = rowwise.reshape(ncols, LANES)
+
+                def strip(k):
+                    return strip_ref[slot, pl.ds(nothing + PAD + k, ncols), :].reshape(ncols // 8, 8, LANES)
+
+                value = y0 * rowwise + y1 * strip(ahead) + y2 * strip(2 * ahead)
+                value = value.reshape(ncols, LANES)
+                cut = slice(r * ncols, (r + 1) * ncols)
+                out_ref[cut, columns] = value
+                upper = value.astype(jnp.bfloat16)
+                half_ref[0, cut, columns] = upper
+                if exact:
+                    half_ref[1, cut, columns] = (value - upper.astype(jnp.float32)).astype(jnp.bfloat16)
+        columns = slice(l * WIDE, (l + 1) * WIDE)
+        for k in range(1 + exact):
+            term = dot(half_ref[k, :, columns], sums_ref[columns, :])
+            table = term if table is None else table + term
+    for g in range(BLOCK * ncols // LANES):
+        total = table[g * LANES:(g + 1) * LANES, :].T
+        kind = kind_ref[pl.ds(group + g, 1), :]
+        code = code_ref[pl.ds(group + g, 1), :]
+        gas = kind == 0
+
+        def keep(*codes):
+            hit = (code == codes[0]) | (code == codes[1])
+            return jnp.where(gas | jnp.logical_not(hit), 1.0, 0.0)
+
+        kept = (keep(0, 2) * total[0:16] + keep(0, 3) * total[16:32]
+                + keep(1, 2) * total[32:48] + keep(1, 3) * total[48:64])
+        incident = jnp.where(code == 0, total[64:65], jnp.where(code == 1, total[65:66], jnp.where(
+            code == 2, total[66:67], total[67:68])))
+        parts_ref[pl.ds((group + g) * ROWS, ROWS), :] = jnp.concatenate(
+            [kept[0:10], kept[10:13] + kept[13:16], incident], axis=0)
+
+
+def inner_kernel(relax, exact, ncols, flat_ref, coef_ref, kind_ref, code_ref,
+                 spread_ref, target_ref, factor_ref, wall_ref, sums_ref, stencil_ref,
+                 out_ref, parts_ref, head_ref, tail_ref, field_ref, even_ref, strip_ref, half_ref):
     i = pl.program_id(0)
-    block = rows * ncols
+    block = BLOCK * ncols
     span = flat_ref.shape[1]
     edge = 2 * ncols
+    base = i * block
 
     @pl.when(i == 0)
     def _():
+        strip_ref[...] = jnp.zeros_like(strip_ref)
+
+    def store(start, l, values):
+        columns = slice(l * WIDE, (l + 1) * WIDE)
+        field_ref[pl.ds(pl.multiple_of(base + start, edge), values.shape[0]), columns] = values
+
+    if relax:
+        relax_tiles(block, spread_ref, (target_ref, factor_ref, wall_ref), coef_ref, even_ref,
+                    flat_ref, store)
+    else:
+        for l in range(span // WIDE):
+            for start in range(0, block, edge):
+                store(start, l, turned(flat_ref[start:start + edge, l * WIDE:(l + 1) * WIDE], l, span))
+
+    @pl.when(i > 1)
+    def _():
+        transport(exact, field_ref, base - block - edge, ncols, (i - 1) * (block // LANES), kind_ref, code_ref,
+                  sums_ref, stencil_ref, out_ref, parts_ref, strip_ref, half_ref)
+
+    @pl.when(i == pl.num_programs(0) - 1)
+    def _():
+        size = head_ref.shape[0]
+        head_ref[...] = field_ref[:size, :]
+        tail_ref[...] = field_ref[field_ref.shape[0] - size:, :]
+
+
+def outer_kernel(relax, exact, blocks, ncols, count, flat_ref, given_ref, head_ref, tail_ref, low_ref, high_ref,
+                 kind_ref, code_ref, sums_ref, stencil_ref, out_ref, *refs):
+    slot_refs = refs[:count]
+    parts_ref, field_ref, strip_ref, half_ref = refs[count:]
+    i = pl.program_id(0)
+    block = BLOCK * ncols
+    edge = 2 * ncols
+    size = head_ref.shape[0]
+    span = out_ref.shape[1]
+
+    def halo(ref, start):
         for l in range(span // WIDE):
             columns = slice(l * WIDE, (l + 1) * WIDE)
-            for ref, start in ((low_ref, 0), (high_ref, edge + blocks * block)):
-                values = ref[:, columns]
-                field_ref[pl.ds(start, edge), columns] = values if relax else turned(values, l, span)
+            values = ref[:, columns]
+            field_ref[start:start + edge, columns] = values if relax else turned(values, l, span)
+
+    @pl.when(i == 0)
+    def _():
         strip_ref[...] = jnp.zeros_like(strip_ref)
-
-    @pl.when(i < blocks)
+        parts_ref[...] = given_ref[...]
+        halo(low_ref, 0)
+        field_ref[edge:, :] = head_ref[...]
+
+    @pl.when(i == 1)
     def _():
-        base = edge + i * block
-
-        def store(start, l, values):
-            columns = slice(l * WIDE, (l + 1) * WIDE)
-            field_ref[pl.ds(pl.multiple_of(base + start, edge), values.shape[0]), columns] = values
-
-        if relax:
-            relax_tiles(block, spread_ref, (target_ref, factor_ref, wall_ref), coef_ref, even_ref,
-                        flat_ref, store)
-        else:
-            for l in range(span // WIDE):
-                for start in range(0, block, edge):
-                    store(start, l, turned(flat_ref[start:start + edge, l * WIDE:(l + 1) * WIDE], l, span))
-
-    @pl.when(i > 0)
+        field_ref[:size, :] = tail_ref[...]
+        halo(high_ref, size)
+
+    transport(exact, field_ref, 0, ncols, i * ((blocks - 1) * (block // LANES)), kind_ref, code_ref,
+              sums_ref, stencil_ref, out_ref, parts_ref, strip_ref, half_ref)
+
+    @pl.when(i == 1)
     def _():
-        base = (i - 1) * block
-        nothing = jnp.minimum(i, 0)
-
-        def lanes(l, carry):
-            for h in range(WIDE // LANES):
-                columns = pl.ds(pl.multiple_of(l * WIDE, WIDE) + h * LANES, LANES)
-                table = stencil_ref[:, columns]
-                x0, x1, x2, vx, y0, y1, y2, vy = (table[8 * k:8 * k + 8][None] for k in range(8))
-                x_up = jnp.broadcast_to(vx > 0, (ncols // 8, 8, LANES))
-                ahead = 1 if h == 0 else -1
-
-                def field(k):
-                    start = pl.multiple_of(base + k * ncols, ncols)
-                    return field_ref[pl.ds(start, ncols), columns].reshape(ncols // 8, 8, LANES)
-
-                for r in range(rows):
-                    near = jnp.where(x_up, field(r + 1), field(r + 3))
-                    far = jnp.where(x_up, field(r), field(r + 4))
-                    rowwise = x0 * field(r + 2) + x1 * near + x2 * far
-                    slot = h * rows + r
-                    strip_ref[slot, PAD:PAD + ncols, :] = rowwise.reshape(ncols, LANES)
-
-                    def strip(k):
-                        return strip_ref[slot, pl.ds(nothing + PAD + k, ncols), :].reshape(ncols // 8, 8, LANES)
-
-                    value = y0 * rowwise + y1 * strip(ahead) + y2 * strip(2 * ahead)
-                    value = value.reshape(ncols, LANES)
-                    cut = slice(r * ncols, (r + 1) * ncols)
-                    out_ref[cut, columns] = value
-                    upper = value.astype(jnp.bfloat16)
-                    half_ref[0, cut, columns] = upper
-                    if exact:
-                        half_ref[1, cut, columns] = (value - upper.astype(jnp.float32)).astype(jnp.bfloat16)
-            return carry
-
-        lax.fori_loop(0, span // WIDE, lanes, 0)
-        table = dot(half_ref[0], sums_ref[...])
-        if exact:
-            table = table + dot(half_ref[1], sums_ref[...])
-        for g in range(block // LANES):
-            total = table[g * LANES:(g + 1) * LANES, :].T
-            group = (i - 1) * (block // LANES) + g
-            kind = kind_ref[pl.ds(group, 1), :]
-            code = code_ref[pl.ds(group, 1), :]
-            gas = kind == 0
-
-            def keep(*codes):
-                hit = (code == codes[0]) | (code == codes[1])
-                return jnp.where(gas | jnp.logical_not(hit), 1.0, 0.0)
-
-            kept = (keep(0, 2) * total[0:16] + keep(0, 3) * total[16:32]
-                    + keep(1, 2) * total[32:48] + keep(1, 3) * total[48:64])
-            incident = jnp.where(code == 0, total[64:65], jnp.where(code == 1, total[65:66], jnp.where(
-                code == 2, total[66:67], total[67:68])))
-            parts_ref[pl.ds(pl.multiple_of(group * ROWS, ROWS), ROWS), :] = jnp.concatenate(
-                [kept[0:10], kept[10:13] + kept[13:16], incident, jnp.zeros((2, LANES), jnp.float32)], axis=0)
-
-
-def advance(relax, exact, flat, coef, low, high, kind, code, spread, tables, sums, stencil, ncols):
+        me = lax.axis_index("vel")
+        rows = slot_refs[0].shape[0]
+        for away, ref in enumerate(slot_refs):
+            owner = lax.rem(me + away, count)
+            ref[...] = parts_ref[pl.ds(pl.multiple_of(owner * rows, 4), rows), :]
+
+
+def inner(relax, exact, flat, coef, kind, code, spread, tables, sums, stencil, ncols):
     cells, span = flat.shape
-    rows = 8
-    block = rows * ncols
+    block = BLOCK * ncols
     blocks = cells // block
     groups = cells // LANES
     whole = pl.BlockSpec(memory_space=pltpu.VMEM)
+    end = jax.ShapeDtypeStruct(((BLOCK + 2) * ncols, span), jnp.float32)
     return pl.pallas_call(
-        functools.partial(main_kernel, relax, exact, blocks, rows, ncols),
-        grid=(blocks + 1,),
+        functools.partial(inner_kernel, relax, exact, ncols),
+        grid=(blocks,),
         out_shape=(jax.ShapeDtypeStruct((cells, span), jnp.float32),
-                   jax.ShapeDtypeStruct((groups * ROWS, LANES), jnp.float32)),
-        in_specs=[pl.BlockSpec((block, span), lambda i: (jnp.minimum(i, blocks - 1), 0)),
-                  pl.BlockSpec((block, COEF), lambda i: (jnp.minimum(i, blocks - 1), 0)),
-                  whole, whole, whole, whole, whole, whole, whole, whole, whole, whole],
-        out_specs=(pl.BlockSpec((block, span), lambda i: (jnp.maximum(i - 1, 0), 0)), whole),
-        scratch_shapes=[pltpu.VMEM((cells + 4 * ncols, span), jnp.float32),
+                   jax.ShapeDtypeStruct((groups * ROWS, LANES), jnp.float32), end, end),
+        in_specs=[pl.BlockSpec((block, span), lambda i: (i, 0)),
+                  pl.BlockSpec((block, COEF), lambda i: (i, 0))] + [whole] * 8,
+        out_specs=(pl.BlockSpec((block, span), lambda i: (jnp.maximum(i - 1, 1), 0)), whole, whole, whole),
+        scratch_shapes=[pltpu.VMEM((cells, span), jnp.float32),
                         pltpu.VMEM((CELLS, 2 * LANES), jnp.float32),
-                        pltpu.VMEM((WIDE // LANES * rows, ncols + 2 * PAD, LANES), jnp.float32),
+                        pltpu.VMEM((WIDE // LANES * BLOCK, ncols + 2 * PAD, LANES), jnp.float32),
                         pltpu.VMEM((1 + exact, block, span), jnp.bfloat16)],
         compiler_params=pltpu.CompilerParams(vmem_limit_bytes=VMEM_LIMIT),
-        name="advance" if relax else "transport",
-    )(flat, coef, low, high, kind, code, spread, *tables, sums, stencil)
+        cost_estimate=pl.CostEstimate(flops=12 * cells * span * COEF, bytes_accessed=8 * cells * span,
+                                      transcendentals=2 * cells * span),
+        name="inner" if relax else "inner_first",
+    )(flat, coef, kind, code, spread, *tables, sums, stencil)
+
+
+def outer(relax, exact, flat, parts, head, tail, low, high, kind, code, sums, stencil, ncols):
+    cells, span = flat.shape
+    block = BLOCK * ncols
+    blocks = cells // block
+    count = lax.axis_size("vel")
+    whole = pl.BlockSpec(memory_space=pltpu.VMEM)
+    slot = jax.ShapeDtypeStruct((parts.shape[0] // count, LANES), jnp.float32)
+    flat, *slots = pl.pallas_call(
+        functools.partial(outer_kernel, relax, exact, blocks, ncols, count),
+        grid=(2,),
+        out_shape=(jax.ShapeDtypeStruct((cells, span), jnp.float32),) + (slot,) * count,
+        in_specs=[pl.BlockSpec(memory_space=pl.ANY)] + [whole] * 9,
+        out_specs=(pl.BlockSpec((block, span), lambda i: (i * (blocks - 1), 0)),) + (whole,) * count,
+        scratch_shapes=[pltpu.VMEM(parts.shape, jnp.float32),
+                        pltpu.VMEM(((BLOCK + 4) * ncols, span), jnp.float32),
+                        pltpu.VMEM((WIDE // LANES * BLOCK, ncols + 2 * PAD, LANES), jnp.float32),
+                        pltpu.VMEM((1 + exact, block, span), jnp.bfloat16)],
+        input_output_aliases={0: 0},
+        compiler_params=pltpu.CompilerParams(vmem_limit_bytes=VMEM_LIMIT),
+        name="outer" if relax else "outer_first",
+    )(flat, parts, head, tail, low, high, kind, code, sums, stencil)
+    return flat, slots
 
 
 def last_kernel(flat_ref, coef_ref, spread_ref, target_ref, factor_ref, wall_ref, out_ref, even_ref):
@@ -461,14 +575,10 @@
     return lax.ppermute(last, "space", up), lax.ppermute(first, "space", down)
 
 
-def total(parts):
-    count = lax.axis_size("vel")
-    rows = parts.shape[0] // count
-    pieces = parts.reshape(count, rows, LANES)
-    swapped = lax.all_to_all(pieces, "vel", 0, 0)
-    own = jnp.sum(swapped, axis=0)
-    spread = lax.all_to_all(jnp.broadcast_to(own[None], (count, rows, LANES)), "vel", 0, 0)
-    return spread.reshape(count * rows, LANES)
+def swap(slots):
+    count = len(slots)
+    return [slots[0]] + [lax.ppermute(slots[k], "vel", [(i, (i + k) % count) for i in range(count)])
+                         for k in range(1, count)]
 
 
 def shards(dist, cell_kind, normal_code, wall_temp):
@@ -487,10 +597,13 @@
     for step in range(STEPS):
         final = step == STEPS - 1
         low, high = exchange(low, high)
-        flat, parts = advance(step > 0, final, flat, coef, low, high, kind, code, spread, tables, sums, stencil, ncols)
-        coef, flux, *ends = state(not final, total(parts), kind, code, temp, flat, spread, tables, ncols)
+        flat, parts, head, tail = inner(step > 0, final, flat, coef, kind, code, spread, tables, sums, stencil, ncols)
+        flat, slots = outer(step > 0, final, flat, parts, head, tail, low, high, kind, code, sums, stencil, ncols)
+        own = gas(swap(slots), kind, code, temp)
+        coef, *others = state(not final, swap([own] * len(slots)), kind, code, temp, flat, spread, tables, ncols)
         if not final:
-            low, high = ends
+            low, high = others
+    flux = others[0]
     current = finish(flat, coef, spread, tables, ncols)
     columns = ncols // lax.axis_size("vel")
     own_flux = lax.dynamic_slice_in_dim(flux.reshape(nrows, ncols), lax.axis_index("vel") * columns, columns, 1)

time: 327 us -> 293 us (0.90); the launches traced: 321 us -> 292 us
  blocking collectives: 68.2 us -> 0 us
  starting transfers between devices: 33 us -> 59.1 us
  Pallas kernels: 167 us -> 187 us
  waiting for transfers between devices: 39.4 us -> 28.6 us
  local copies, waits for them, and re-layouts: 12.1 us -> 16.5 us
    all_to_all x6 -> x0, blocking collectives: 68.2 us -> none  [the longest x4 47.8 us: total(): swapped = lax.all_to_all(pieces, 'vel', 0, 0)]
    ppermute x0 -> x24, starting transfers between devices: none -> 32.7 us  [swap(): lax.ppermute(slots[k], 'vel', [(i, (i + k) % count) for i in range(count)])]
    ppermute x0 -> x24, waiting for transfers between devices: none -> 28.6 us  [swap(): lax.ppermute(slots[k], 'vel', [(i, (i + k) % count) for i in range(count)])]
    ppermute x8, waiting for transfers between devices: 25.4 us -> 0.02 us  [exchange(): return (lax.ppermute(last, 'space', up), lax.ppermute(first, 'space', down))]
    pallas_call x8 -> x16, Pallas kernels: 148 us -> 168 us  [the longest x4 107 us: inner(): pl.pallas_call(functools.partial(inner_kernel, relax, exact, ncols), grid...]
    all_to_all x2 -> x0, waiting for transfers between devices: 14 us -> none  [total(): lax.all_to_all(jnp.broadcast_to(own[None], (count, rows, LANES)), 'vel',...]
    all_to_all x2 -> x0, starting transfers between devices: 6.81 us -> none  [total(): lax.all_to_all(jnp.broadcast_to(own[None], (count, rows, LANES)), 'vel',...]
    unnamed x25 -> x67, local copies, waits for them, and re-layouts: 4.5 us -> 9.7 us
  transfers between devices with their start and end apart: 10 -> 32, of which waited for: 10 -> 24; matrix products, arithmetic and copies ran while one was open for 1% -> 2% of each run, Pallas kernels for 0% -> 37%
where the time goes in v2:
time: 293 us; the launch traced here: 292 us
  Pallas kernels  187 us (64%)
  starting transfers between devices  59.1 us (20%)
  waiting for transfers between devices  28.6 us (10%)
  local copies, waits for them, and re-layouts  16.5 us (6%)
    pallas_call x4, Pallas kernels, inner(): pl.pallas_call(functools.partial(inner_kernel, relax, exact, ncols), grid...  107 us
    pallas_call x4, Pallas kernels, outer(): pl.pallas_call(functools.partial(outer_kernel, relax, exact, blocks, ncol...  39.8 us
    ppermute x24, starting transfers between devices, swap(): lax.ppermute(slots[k], 'vel', [(i, (i + k) % count) for i in range(count)])  32.7 us
    ppermute x24, waiting for transfers between devices, swap(): lax.ppermute(slots[k], 'vel', [(i, (i + k) % count) for i in range(count)])  28.6 us
    ppermute x8, starting transfers between devices, exchange(): return (lax.ppermute(last, 'space', up), lax.ppermute(first, 'space', down))  26.5 us
    pallas_call x1, Pallas kernels, finish(): pl.pallas_call(last_kernel, grid=(cells // block,), out_shape=jax.ShapeDt...  17.3 us
    pallas_call x4, Pallas kernels, state(): pl.pallas_call(functools.partial(state_kernel, len(pieces), groups, with_...  14.5 us
    unnamed x67, local copies, waits for them, and re-layouts  9.7 us
  transfers between devices with their start and end apart: 32, of which 24 were waited for; matrix products, arithmetic and copies ran while one was open for 2% of the time, Pallas kernels for 37%

profile of v2, /device:TPU:4, one launch (start us, length us, event | category | flops | bytes accessed | tf_op | source)
XLA Modules:
  0.0 291.8 jit_solution(6618082954486214247)
XLA Ops:
  0.6 1.3 fusion
  1.9 1.9 collective-permute-start
  3.8 4.5 %collective-permute-start.1 = (f32[128,1024]{1,0:T(8,128)S(1)}, f32[128,1024]{1,0:T(8,128)S(1)}, u32[]{:S(2)}, u32[]{:S(2)}) collective-permute-start(f32[128,1024]{1,0:T(8,128)S(1)} %bitcast.6), channel_id=1, source_target_pairs={{4,0},{8,4},{12,8},{16,12},{20,16},{24,20},{28,24},{5,1},{9,5},{13... | collective-permute-start | bytes 1572872 | tf_op jit(solution)/shard_map/ppermute | solution.py:575
  8.4 1.2 setup.1
  9.6 1.4 reshape.25.kind_ref.refs_4_
  11.0 1.4 reshape.26.code_ref.refs_5_
  12.4 1.1 broadcast_in_dim.3.coef_ref
  13.6 23.3 %inner_first.1 = (f32[4096,1024]{1,0:T(8,128)}, f32[448,128]{1,0:T(8,128)}, f32[640,1024]{1,0:T(8,128)}, f32[640,1024]{1,0:T(8,128)}) custom-call(f32[4096,1024]{1,0:T(8,128)} %bitcast.4, bf16[4096,64]{1,0:T(8,128)(2,1)} %broadcast_in_dim.3.coef_ref, s32[32,128]{1,0:T(8,128)} %reshape.25.kind_ref.refs_4_, s32[32,128]{1,0:T(8,128)} %reshape.26.code_ref.refs_5_, ...), custom_call_target="tpu_custom_call" | custom-call | flops 3221225472 | bytes 33554432 | tf_op jit(solution)/shard_map/inner_first/pallas_call | solution.py:500
  37.9 10.0 %outer_first.1 = (f32[4096,1024]{1,0:T(8,128)}, f32[112,128]{1,0:T(8,128)}, f32[112,128]{1,0:T(8,128)}, f32[112,128]{1,0:T(8,128)}, f32[112,128]{1,0:T(8,128)}) custom-call(f32[4096,1024]{1,0:T(8,128)} %get-tuple-element.61.flat_ref, f32[448,128]{1,0:T(8,128)} %get-tuple-element.62.given_ref, ...), custom_call_target="tpu_custom_call", output_to_operand_aliasing={{0}: (0, {})} | custom-call | tf_op jit(solution)/shard_map/outer_first/pallas_call | solution.py:526
  47.9 1.6 collective-permute-start.2
  49.5 2.6 collective-permute-start.3
  52.1 1.3 collective-permute-start.4
  54.6 1.4 collective-permute-done.3.refs_2_
  57.2 1.6 gas.4.refs_0_
  59.4 3.0 %collective-permute-start.6 = (f32[80,128]{1,0:T(8,128)}, f32[80,128]{1,0:T(8,128)S(1)}, u32[]{:S(2)}, u32[]{:S(2)}) collective-permute-start(f32[80,128]{1,0:T(8,128)} %gas.4.refs_0_), channel_id=1, source_target_pairs={{0,2},{1,3},{2,0},{3,1},{4,6},{5,7},{6,4},{7,5},{8,10},{9,11},{10,... | collective-permute-start | bytes 122888 | tf_op jit(solution)/shard_map/ppermute | solution.py:580
  62.6 2.3 collective-permute-done.5.refs_1_
  65.5 1.1 collective-permute-done.7.refs_3_
  67.2 4.0 %state.4 = (bf16[4096,64]{1,0:T(8,128)(2,1)}, f32[128,1024]{1,0:T(8,128)}, f32[128,1024]{1,0:T(8,128)}) custom-call(f32[80,128]{1,0:T(8,128)} %gas.4.refs_0_, f32[80,128]{1,0:T(8,128)} %copy-done.20, f32[80,128]{1,0:T(8,128)} %copy-done.23, f32[80,128]{1,0:T(8,128)} %copy-done.26, s32[32,128]{1,0:T(8,128)} %reshape.25.kind_ref.refs_4_, ...), custom_call_target="tpu_custom_call" | custom-call | tf_op jit(solution)/shard_map/state/pallas_call | solution.py:309
  71.2 1.9 collective-permute-start.8
  73.1 4.7 %collective-permute-start.9 = (f32[128,1024]{1,0:T(8,128)}, f32[128,1024]{1,0:T(8,128)S(1)}, u32[]{:S(2)}, u32[]{:S(2)}) collective-permute-start(f32[128,1024]{1,0:T(8,128)} %get-tuple-element.76), channel_id=1, source_target_pairs={{4,0},{8,4},{12,8},{16,12},{20,16},{24,20},{28,24},{5,1},{9,5},{13... | collective-permute-start | bytes 1572872 | tf_op jit(solution)/shard_map/ppermute | solution.py:575
  77.8 27.2 %inner.3 = (f32[4096,1024]{1,0:T(8,128)}, f32[448,128]{1,0:T(8,128)}, f32[640,1024]{1,0:T(8,128)}, f32[640,1024]{1,0:T(8,128)}) custom-call(f32[4096,1024]{1,0:T(8,128)} %get-tuple-element.65.refs_7_.refs_8_.flat_ref, bf16[4096,64]{1,0:T(8,128)(2,1)} %get-tuple-element.70.coef_ref, s32[32,128]{1,0:T(8,128)} %reshape.25.kind_ref.refs_4_, ...), custom_call_target="tpu_custom_call" | custom-call | flops 3221225472 | bytes 33554432 | tf_op jit(solution)/shard_map/inner/pallas_call | solution.py:500
  106.0 9.7 %outer.3 = (f32[4096,1024]{1,0:T(8,128)}, f32[112,128]{1,0:T(8,128)}, f32[112,128]{1,0:T(8,128)}, f32[112,128]{1,0:T(8,128)}, f32[112,128]{1,0:T(8,128)}) custom-call(f32[4096,1024]{1,0:T(8,128)} %get-tuple-element.71.flat_ref, f32[448,128]{1,0:T(8,128)} %get-tuple-element.72.given_ref, ...), custom_call_target="tpu_custom_call", output_to_operand_aliasing={{0}: (0, {})} | custom-call | tf_op jit(solution)/shard_map/outer/pallas_call | solution.py:526
  115.7 0.8 collective-permute-start.10
  116.5 2.0 collective-permute-start.11
  118.6 1.1 collective-permute-start.12
  119.6 2.4 collective-permute-done.10.refs_1_
  122.1 1.1 collective-permute-done.11.refs_2_
  124.0 1.6 gas.5.refs_0_
  125.6 1.2 collective-permute-start.13
  126.8 2.0 collective-permute-start.14
  129.4 2.2 collective-permute-done.13.refs_1_
  131.6 0.9 collective-permute-done.14.refs_2_
  133.6 4.0 %state.5 = (bf16[4096,64]{1,0:T(8,128)(2,1)}, f32[128,1024]{1,0:T(8,128)}, f32[128,1024]{1,0:T(8,128)}) custom-call(f32[80,128]{1,0:T(8,128)} %gas.5.refs_0_, f32[80,128]{1,0:T(8,128)} %copy-done.21, f32[80,128]{1,0:T(8,128)} %copy-done.24, f32[80,128]{1,0:T(8,128)} %copy-done.27, s32[32,128]{1,0:T(8,128)} %reshape.25.kind_ref.refs_4_, ...), custom_call_target="tpu_custom_call" | custom-call | tf_op jit(solution)/shard_map/state/pallas_call | solution.py:309
  137.6 1.9 collective-permute-start.16
  139.5 4.8 %collective-permute-start.17 = (f32[128,1024]{1,0:T(8,128)}, f32[128,1024]{1,0:T(8,128)S(1)}, u32[]{:S(2)}, u32[]{:S(2)}) collective-permute-start(f32[128,1024]{1,0:T(8,128)} %get-tuple-element.88), channel_id=1, source_target_pairs={{4,0},{8,4},{12,8},{16,12},{20,16},{24,20},{28,24},{5,1},{9,5},{13... | collective-permute-start | bytes 1572872 | tf_op jit(solution)/shard_map/ppermute | solution.py:575
  144.3 27.3 %inner.4 = (f32[4096,1024]{1,0:T(8,128)}, f32[448,128]{1,0:T(8,128)}, f32[640,1024]{1,0:T(8,128)}, f32[640,1024]{1,0:T(8,128)}) custom-call(f32[4096,1024]{1,0:T(8,128)} %get-tuple-element.77.refs_7_.refs_8_.flat_ref, bf16[4096,64]{1,0:T(8,128)(2,1)} %get-tuple-element.82.coef_ref, s32[32,128]{1,0:T(8,128)} %reshape.25.kind_ref.refs_4_, ...), custom_call_target="tpu_custom_call" | custom-call | flops 3221225472 | bytes 33554432 | tf_op jit(solution)/shard_map/inner/pallas_call | solution.py:500
  172.6 9.7 %outer.4 = (f32[4096,1024]{1,0:T(8,128)}, f32[112,128]{1,0:T(8,128)}, f32[112,128]{1,0:T(8,128)}, f32[112,128]{1,0:T(8,128)}, f32[112,128]{1,0:T(8,128)}) custom-call(f32[4096,1024]{1,0:T(8,128)} %get-tuple-element.83.flat_ref, f32[448,128]{1,0:T(8,128)} %get-tuple-element.84.given_ref, ...), custom_call_target="tpu_custom_call", output_to_operand_aliasing={{0}: (0, {})} | custom-call | tf_op jit(solution)/shard_map/outer/pallas_call | solution.py:526
  182.3 1.2 collective-permute-start.18
  183.5 1.8 collective-permute-start.19
  185.3 1.0 collective-permute-start.20
  186.3 2.3 collective-permute-done.18.refs_1_
  188.6 1.3 collective-permute-done.19.refs_2_
  190.8 1.6 gas.6.refs_0_
  192.4 0.9 collective-permute-start.21
  193.3 2.2 collective-permute-start.22
  196.2 2.2 collective-permute-done.21.refs_1_
  198.4 0.8 collective-permute-done.22.refs_2_
  200.3 4.0 %state.6 = (bf16[4096,64]{1,0:T(8,128)(2,1)}, f32[128,1024]{1,0:T(8,128)}, f32[128,1024]{1,0:T(8,128)}) custom-call(f32[80,128]{1,0:T(8,128)} %gas.6.refs_0_, f32[80,128]{1,0:T(8,128)} %copy-done.22, f32[80,128]{1,0:T(8,128)} %copy-done.25, f32[80,128]{1,0:T(8,128)} %copy-done.28, s32[32,128]{1,0:T(8,128)} %reshape.25.kind_ref.refs_4_, ...), custom_call_target="tpu_custom_call" | custom-call | tf_op jit(solution)/shard_map/state/pallas_call | solution.py:309
  204.3 1.9 collective-permute-start.24
  206.2 4.8 %collective-permute-start.25 = (f32[128,1024]{1,0:T(8,128)}, f32[128,1024]{1,0:T(8,128)S(1)}, u32[]{:S(2)}, u32[]{:S(2)}) collective-permute-start(f32[128,1024]{1,0:T(8,128)} %get-tuple-element.100), channel_id=1, source_target_pairs={{4,0},{8,4},{12,8},{16,12},{20,16},{24,20},{28,24},{5,1},{9,5},{13... | collective-permute-start | bytes 1572872 | tf_op jit(solution)/shard_map/ppermute | solution.py:575
  211.0 29.6 %inner.5 = (f32[4096,1024]{1,0:T(8,128)}, f32[448,128]{1,0:T(8,128)}, f32[640,1024]{1,0:T(8,128)}, f32[640,1024]{1,0:T(8,128)}) custom-call(f32[4096,1024]{1,0:T(8,128)} %get-tuple-element.89.refs_7_.refs_8_.flat_ref, bf16[4096,64]{1,0:T(8,128)(2,1)} %get-tuple-element.94.coef_ref, s32[32,128]{1,0:T(8,128)} %reshape.25.kind_ref.refs_4_, ...), custom_call_target="tpu_custom_call" | custom-call | flops 3221225472 | bytes 33554432 | tf_op jit(solution)/shard_map/inner/pallas_call | solution.py:500
  241.6 10.4 %outer.5 = (f32[4096,1024]{1,0:T(8,128)}, f32[112,128]{1,0:T(8,128)}, f32[112,128]{1,0:T(8,128)}, f32[112,128]{1,0:T(8,128)}, f32[112,128]{1,0:T(8,128)}) custom-call(f32[4096,1024]{1,0:T(8,128)} %get-tuple-element.95.flat_ref, f32[448,128]{1,0:T(8,128)} %get-tuple-element.96.given_ref, ...), custom_call_target="tpu_custom_call", output_to_operand_aliasing={{0}: (0, {})} | custom-call | tf_op jit(solution)/shard_map/outer/pallas_call | solution.py:526
  252.0 1.4 collective-permute-start.26
  253.4 1.7 collective-permute-start.27
  255.1 0.8 collective-permute-start.28
  256.0 2.3 collective-permute-done.26.refs_1_
  258.3 1.3 collective-permute-done.27.refs_2_
  260.7 1.6 gas.7.refs_0_
  263.1 2.2 collective-permute-start.30
  265.2 0.9 collective-permute-start.31
  266.1 2.3 collective-permute-done.29.refs_1_
  270.3 2.6 state.7
  272.9 0.8 reshape.29
  274.4 17.3 %finish.1 = f32[4096,1024]{1,0:T(8,128)} custom-call(f32[4096,1024]{1,0:T(8,128)} %get-tuple-element.101.flat_ref, bf16[4096,64]{1,0:T(8,128)(2,1)} %get-tuple-element.106.coef_ref, bf16[64,256]{1,0:T(8,128)(2,1)} %get-tuple-element.55.spread_ref.refs_9_, bf16[64,1024]{1,0:T(8,128)(2,1)} %get-tuple-element.56.target_ref.refs_10_, ...), custom_call_target="tpu_custom_call" | custom-call | tf_op jit(solution)/shard_map/finish/pallas_call | solution.py:557
  (92 shorter events, 18.1 us)
Async XLA Ops:
  1.9 35.0 %collective-permute-start = (f32[128,1024]{1,0:T(8,128)S(1)}, f32[128,1024]{1,0:T(8,128)S(1)}, u32[]{:S(2)}, u32[]{:S(2)}) collective-permute-start(f32[128,1024]{1,0:T(8,128)S(1)} %bitcast.7), channel_id=1, source_target_pairs={{0,4},{4,8},{8,12},{12,16},{16,20},{20,24},{24,28},{1,5},{5,9},{9,... | collective-permute-start | bytes 1572872 | tf_op jit(solution)/shard_map/ppermute | solution.py:575
  3.8 33.1 %collective-permute-start.1 = (f32[128,1024]{1,0:T(8,128)S(1)}, f32[128,1024]{1,0:T(8,128)S(1)}, u32[]{:S(2)}, u32[]{:S(2)}) collective-permute-start(f32[128,1024]{1,0:T(8,128)S(1)} %bitcast.6), channel_id=1, source_target_pairs={{4,0},{8,4},{12,8},{16,12},{20,16},{24,20},{28,24},{5,1},{9,5},{13... | collective-permute-start | bytes 1572872 | tf_op jit(solution)/shard_map/ppermute | solution.py:575
  13.6 39.8 %copy-start.32 = (f32[64,64]{1,0:T(8,128)S(1)}, f32[64,64]{1,0:T(8,128)}, u32[]{:S(2)}) copy-start(f32[64,64]{1,0:T(8,128)} %param.7) | copy-start | bytes 49156
  36.9 0.8 copy-start
  36.9 1.0 copy-start.1
  47.9 6.8 %collective-permute-start.2 = (f32[112,128]{1,0:T(8,128)}, f32[112,128]{1,0:T(8,128)S(1)}, u32[]{:S(2)}, u32[]{:S(2)}) collective-permute-start(f32[112,128]{1,0:T(8,128)} %get-tuple-element.67), channel_id=1, source_target_pairs={{0,1},{1,2},{2,3},{3,0},{4,5},{5,6},{6,7},{7,4},{8,9},{9,10},{10,1... | collective-permute-start | bytes 172040 | tf_op jit(solution)/shard_map/ppermute | solution.py:580
  49.5 6.6 %collective-permute-start.3 = (f32[112,128]{1,0:T(8,128)}, f32[112,128]{1,0:T(8,128)S(1)}, u32[]{:S(2)}, u32[]{:S(2)}) collective-permute-start(f32[112,128]{1,0:T(8,128)} %get-tuple-element.68), channel_id=1, source_target_pairs={{0,2},{1,3},{2,0},{3,1},{4,6},{5,7},{6,4},{7,5},{8,10},{9,11},{10,... | collective-permute-start | bytes 172040 | tf_op jit(solution)/shard_map/ppermute | solution.py:580
  52.1 4.5 %collective-permute-start.4 = (f32[112,128]{1,0:T(8,128)}, f32[112,128]{1,0:T(8,128)S(1)}, u32[]{:S(2)}, u32[]{:S(2)}) collective-permute-start(f32[112,128]{1,0:T(8,128)} %get-tuple-element.69), channel_id=1, source_target_pairs={{0,3},{1,0},{2,1},{3,2},{4,7},{5,4},{6,5},{7,6},{8,11},{9,8},{10,9... | collective-permute-start | bytes 172040 | tf_op jit(solution)/shard_map/ppermute | solution.py:580
  54.6 1.9 copy-start.8
  56.1 0.6 copy-start.12
  56.5 0.6 copy-start.16
  58.8 6.1 %collective-permute-start.5 = (f32[80,128]{1,0:T(8,128)}, f32[80,128]{1,0:T(8,128)S(1)}, u32[]{:S(2)}, u32[]{:S(2)}) collective-permute-start(f32[80,128]{1,0:T(8,128)} %gas.4.refs_0_), channel_id=1, source_target_pairs={{0,1},{1,2},{2,3},{3,0},{4,5},{5,6},{6,7},{7,4},{8,9},{9,10},{10,1... | collective-permute-start | bytes 122888 | tf_op jit(solution)/shard_map/ppermute | solution.py:580
  59.4 6.1 %collective-permute-start.6 = (f32[80,128]{1,0:T(8,128)}, f32[80,128]{1,0:T(8,128)S(1)}, u32[]{:S(2)}, u32[]{:S(2)}) collective-permute-start(f32[80,128]{1,0:T(8,128)} %gas.4.refs_0_), channel_id=1, source_target_pairs={{0,2},{1,3},{2,0},{3,1},{4,6},{5,7},{6,4},{7,5},{8,10},{9,11},{10,... | collective-permute-start | bytes 122888 | tf_op jit(solution)/shard_map/ppermute | solution.py:580
  62.4 4.2 %collective-permute-start.7 = (f32[80,128]{1,0:T(8,128)}, f32[80,128]{1,0:T(8,128)S(1)}, u32[]{:S(2)}, u32[]{:S(2)}) collective-permute-start(f32[80,128]{1,0:T(8,128)} %gas.4.refs_0_), channel_id=1, source_target_pairs={{0,3},{1,0},{2,1},{3,2},{4,7},{5,4},{6,5},{7,6},{8,11},{9,8},{10,9... | collective-permute-start | bytes 122888 | tf_op jit(solution)/shard_map/ppermute | solution.py:580
  64.9 1.7 copy-start.20
  65.5 1.1 copy-start.23
  66.6 0.6 copy-start.26
  71.2 33.8 %collective-permute-start.8 = (f32[128,1024]{1,0:T(8,128)}, f32[128,1024]{1,0:T(8,128)S(1)}, u32[]{:S(2)}, u32[]{:S(2)}) collective-permute-start(f32[128,1024]{1,0:T(8,128)} %get-tuple-element.75), channel_id=1, source_target_pairs={{0,4},{4,8},{8,12},{12,16},{16,20},{20,24},{24,28},{1,5},{5,9},{9,... | collective-permute-start | bytes 1572872 | tf_op jit(solution)/shard_map/ppermute | solution.py:575
  73.1 31.9 %collective-permute-start.9 = (f32[128,1024]{1,0:T(8,128)}, f32[128,1024]{1,0:T(8,128)S(1)}, u32[]{:S(2)}, u32[]{:S(2)}) collective-permute-start(f32[128,1024]{1,0:T(8,128)} %get-tuple-element.76), channel_id=1, source_target_pairs={{4,0},{8,4},{12,8},{16,12},{20,16},{24,20},{28,24},{5,1},{9,5},{13... | collective-permute-start | bytes 1572872 | tf_op jit(solution)/shard_map/ppermute | solution.py:575
  105.0 0.8 copy-start.3
  105.0 1.0 copy-start.6
  115.7 6.3 %collective-permute-start.10 = (f32[112,128]{1,0:T(8,128)}, f32[112,128]{1,0:T(8,128)S(1)}, u32[]{:S(2)}, u32[]{:S(2)}) collective-permute-start(f32[112,128]{1,0:T(8,128)} %get-tuple-element.79), channel_id=1, source_target_pairs={{0,1},{1,2},{2,3},{3,0},{4,5},{5,6},{6,7},{7,4},{8,9},{9,10},{10,1... | collective-permute-start | bytes 172040 | tf_op jit(solution)/shard_map/ppermute | solution.py:580
  116.5 6.6 %collective-permute-start.11 = (f32[112,128]{1,0:T(8,128)}, f32[112,128]{1,0:T(8,128)S(1)}, u32[]{:S(2)}, u32[]{:S(2)}) collective-permute-start(f32[112,128]{1,0:T(8,128)} %get-tuple-element.80), channel_id=1, source_target_pairs={{0,2},{1,3},{2,0},{3,1},{4,6},{5,7},{6,4},{7,5},{8,10},{9,11},{10,... | collective-permute-start | bytes 172040 | tf_op jit(solution)/shard_map/ppermute | solution.py:580
  118.6 4.8 %collective-permute-start.12 = (f32[112,128]{1,0:T(8,128)}, f32[112,128]{1,0:T(8,128)S(1)}, u32[]{:S(2)}, u32[]{:S(2)}) collective-permute-start(f32[112,128]{1,0:T(8,128)} %get-tuple-element.81), channel_id=1, source_target_pairs={{0,3},{1,0},{2,1},{3,2},{4,7},{5,4},{6,5},{7,6},{8,11},{9,8},{10,9... | collective-permute-start | bytes 172040 | tf_op jit(solution)/shard_map/ppermute | solution.py:580
  122.1 1.3 copy-start.9
  123.2 0.6 copy-start.13
  123.3 0.6 copy-start.17
  125.6 6.0 %collective-permute-start.13 = (f32[80,128]{1,0:T(8,128)}, f32[80,128]{1,0:T(8,128)S(1)}, u32[]{:S(2)}, u32[]{:S(2)}) collective-permute-start(f32[80,128]{1,0:T(8,128)} %gas.5.refs_0_), channel_id=1, source_target_pairs={{0,1},{1,2},{2,3},{3,0},{4,5},{5,6},{6,7},{7,4},{8,9},{9,10},{10,1... | collective-permute-start | bytes 122888 | tf_op jit(solution)/shard_map/ppermute | solution.py:580
  126.8 5.7 %collective-permute-start.14 = (f32[80,128]{1,0:T(8,128)}, f32[80,128]{1,0:T(8,128)S(1)}, u32[]{:S(2)}, u32[]{:S(2)}) collective-permute-start(f32[80,128]{1,0:T(8,128)} %gas.5.refs_0_), channel_id=1, source_target_pairs={{0,2},{1,3},{2,0},{3,1},{4,6},{5,7},{6,4},{7,5},{8,10},{9,11},{10,... | collective-permute-start | bytes 122888 | tf_op jit(solution)/shard_map/ppermute | solution.py:580
  128.8 4.2 %collective-permute-start.15 = (f32[80,128]{1,0:T(8,128)}, f32[80,128]{1,0:T(8,128)S(1)}, u32[]{:S(2)}, u32[]{:S(2)}) collective-permute-start(f32[80,128]{1,0:T(8,128)} %gas.5.refs_0_), channel_id=1, source_target_pairs={{0,3},{1,0},{2,1},{3,2},{4,7},{5,4},{6,5},{7,6},{8,11},{9,8},{10,9... | collective-permute-start | bytes 122888 | tf_op jit(solution)/shard_map/ppermute | solution.py:580
  131.6 1.4 copy-start.21
  133.0 0.6 copy-start.27
  137.6 34.0 %collective-permute-start.16 = (f32[128,1024]{1,0:T(8,128)}, f32[128,1024]{1,0:T(8,128)S(1)}, u32[]{:S(2)}, u32[]{:S(2)}) collective-permute-start(f32[128,1024]{1,0:T(8,128)} %get-tuple-element.87), channel_id=1, source_target_pairs={{0,4},{4,8},{8,12},{12,16},{16,20},{20,24},{24,28},{1,5},{5,9},{9,... | collective-permute-start | bytes 1572872 | tf_op jit(solution)/shard_map/ppermute | solution.py:575
  139.5 32.1 %collective-permute-start.17 = (f32[128,1024]{1,0:T(8,128)}, f32[128,1024]{1,0:T(8,128)S(1)}, u32[]{:S(2)}, u32[]{:S(2)}) collective-permute-start(f32[128,1024]{1,0:T(8,128)} %get-tuple-element.88), channel_id=1, source_target_pairs={{4,0},{8,4},{12,8},{16,12},{20,16},{24,20},{28,24},{5,1},{9,5},{13... | collective-permute-start | bytes 1572872 | tf_op jit(solution)/shard_map/ppermute | solution.py:575
  171.6 0.8 copy-start.4
  171.6 1.0 copy-start.7
  182.3 6.3 %collective-permute-start.18 = (f32[112,128]{1,0:T(8,128)}, f32[112,128]{1,0:T(8,128)S(1)}, u32[]{:S(2)}, u32[]{:S(2)}) collective-permute-start(f32[112,128]{1,0:T(8,128)} %get-tuple-element.91), channel_id=1, source_target_pairs={{0,1},{1,2},{2,3},{3,0},{4,5},{5,6},{6,7},{7,4},{8,9},{9,10},{10,1... | collective-permute-start | bytes 172040 | tf_op jit(solution)/shard_map/ppermute | solution.py:580
  183.5 6.4 %collective-permute-start.19 = (f32[112,128]{1,0:T(8,128)}, f32[112,128]{1,0:T(8,128)S(1)}, u32[]{:S(2)}, u32[]{:S(2)}) collective-permute-start(f32[112,128]{1,0:T(8,128)} %get-tuple-element.92), channel_id=1, source_target_pairs={{0,2},{1,3},{2,0},{3,1},{4,6},{5,7},{6,4},{7,5},{8,10},{9,11},{10,... | collective-permute-start | bytes 172040 | tf_op jit(solution)/shard_map/ppermute | solution.py:580
  185.3 4.9 %collective-permute-start.20 = (f32[112,128]{1,0:T(8,128)}, f32[112,128]{1,0:T(8,128)S(1)}, u32[]{:S(2)}, u32[]{:S(2)}) collective-permute-start(f32[112,128]{1,0:T(8,128)} %get-tuple-element.93), channel_id=1, source_target_pairs={{0,3},{1,0},{2,1},{3,2},{4,7},{5,4},{6,5},{7,6},{8,11},{9,8},{10,9... | collective-permute-start | bytes 172040 | tf_op jit(solution)/shard_map/ppermute | solution.py:580
  188.5 1.6 copy-start.10
  189.8 0.6 copy-start.14
  190.2 0.6 copy-start.18
  192.4 6.1 %collective-permute-start.21 = (f32[80,128]{1,0:T(8,128)}, f32[80,128]{1,0:T(8,128)S(1)}, u32[]{:S(2)}, u32[]{:S(2)}) collective-permute-start(f32[80,128]{1,0:T(8,128)} %gas.6.refs_0_), channel_id=1, source_target_pairs={{0,1},{1,2},{2,3},{3,0},{4,5},{5,6},{6,7},{7,4},{8,9},{9,10},{10,1... | collective-permute-start | bytes 122888 | tf_op jit(solution)/shard_map/ppermute | solution.py:580
  193.3 6.0 %collective-permute-start.22 = (f32[80,128]{1,0:T(8,128)}, f32[80,128]{1,0:T(8,128)S(1)}, u32[]{:S(2)}, u32[]{:S(2)}) collective-permute-start(f32[80,128]{1,0:T(8,128)} %gas.6.refs_0_), channel_id=1, source_target_pairs={{0,2},{1,3},{2,0},{3,1},{4,6},{5,7},{6,4},{7,5},{8,10},{9,11},{10,... | collective-permute-start | bytes 122888 | tf_op jit(solution)/shard_map/ppermute | solution.py:580
  195.5 4.2 %collective-permute-start.23 = (f32[80,128]{1,0:T(8,128)}, f32[80,128]{1,0:T(8,128)S(1)}, u32[]{:S(2)}, u32[]{:S(2)}) collective-permute-start(f32[80,128]{1,0:T(8,128)} %gas.6.refs_0_), channel_id=1, source_target_pairs={{0,3},{1,0},{2,1},{3,2},{4,7},{5,4},{6,5},{7,6},{8,11},{9,8},{10,9... | collective-permute-start | bytes 122888 | tf_op jit(solution)/shard_map/ppermute | solution.py:580
  198.4 1.3 copy-start.22
  199.3 0.6 copy-start.25
  199.7 0.6 copy-start.28
  204.3 36.3 %collective-permute-start.24 = (f32[128,1024]{1,0:T(8,128)}, f32[128,1024]{1,0:T(8,128)S(1)}, u32[]{:S(2)}, u32[]{:S(2)}) collective-permute-start(f32[128,1024]{1,0:T(8,128)} %get-tuple-element.99), channel_id=1, source_target_pairs={{0,4},{4,8},{8,12},{12,16},{16,20},{20,24},{24,28},{1,5},{5,9},{9,... | collective-permute-start | bytes 1572872 | tf_op jit(solution)/shard_map/ppermute | solution.py:575
  206.2 34.5 %collective-permute-start.25 = (f32[128,1024]{1,0:T(8,128)}, f32[128,1024]{1,0:T(8,128)S(1)}, u32[]{:S(2)}, u32[]{:S(2)}) collective-permute-start(f32[128,1024]{1,0:T(8,128)} %get-tuple-element.100), channel_id=1, source_target_pairs={{4,0},{8,4},{12,8},{16,12},{20,16},{24,20},{28,24},{5,1},{9,5},{13... | collective-permute-start | bytes 1572872 | tf_op jit(solution)/shard_map/ppermute | solution.py:575
  240.6 0.8 copy-start.2
  240.7 1.0 copy-start.5
  252.0 6.2 %collective-permute-start.26 = (f32[112,128]{1,0:T(8,128)}, f32[112,128]{1,0:T(8,128)S(1)}, u32[]{:S(2)}, u32[]{:S(2)}) collective-permute-start(f32[112,128]{1,0:T(8,128)} %get-tuple-element.103), channel_id=1, source_target_pairs={{0,1},{1,2},{2,3},{3,0},{4,5},{5,6},{6,7},{7,4},{8,9},{9,10},{10,1... | collective-permute-start | bytes 172040 | tf_op jit(solution)/shard_map/ppermute | solution.py:580
  253.4 6.2 %collective-permute-start.27 = (f32[112,128]{1,0:T(8,128)}, f32[112,128]{1,0:T(8,128)S(1)}, u32[]{:S(2)}, u32[]{:S(2)}) collective-permute-start(f32[112,128]{1,0:T(8,128)} %get-tuple-element.104), channel_id=1, source_target_pairs={{0,2},{1,3},{2,0},{3,1},{4,6},{5,7},{6,4},{7,5},{8,10},{9,11},{10,... | collective-permute-start | bytes 172040 | tf_op jit(solution)/shard_map/ppermute | solution.py:580
  255.1 4.9 %collective-permute-start.28 = (f32[112,128]{1,0:T(8,128)}, f32[112,128]{1,0:T(8,128)S(1)}, u32[]{:S(2)}, u32[]{:S(2)}) collective-permute-start(f32[112,128]{1,0:T(8,128)} %get-tuple-element.105), channel_id=1, source_target_pairs={{0,3},{1,0},{2,1},{3,2},{4,7},{5,4},{6,5},{7,6},{8,11},{9,8},{10,9... | collective-permute-start | bytes 172040 | tf_op jit(solution)/shard_map/ppermute | solution.py:580
  258.3 1.8 copy-start.11
  259.6 0.6 copy-start.15
  260.1 0.6 copy-start.19
  262.3 6.1 %collective-permute-start.29 = (f32[80,128]{1,0:T(8,128)}, f32[80,128]{1,0:T(8,128)S(1)}, u32[]{:S(2)}, u32[]{:S(2)}) collective-permute-start(f32[80,128]{1,0:T(8,128)} %gas.7.refs_0_), channel_id=1, source_target_pairs={{0,1},{1,2},{2,3},{3,0},{4,5},{5,6},{6,7},{7,4},{8,9},{9,10},{10,1... | collective-permute-start | bytes 122888 | tf_op jit(solution)/shard_map/ppermute | solution.py:580
  263.1 6.0 %collective-permute-start.30 = (f32[80,128]{1,0:T(8,128)}, f32[80,128]{1,0:T(8,128)S(1)}, u32[]{:S(2)}, u32[]{:S(2)}) collective-permute-start(f32[80,128]{1,0:T(8,128)} %gas.7.refs_0_), channel_id=1, source_target_pairs={{0,2},{1,3},{2,0},{3,1},{4,6},{5,7},{6,4},{7,5},{8,10},{9,11},{10,... | collective-permute-start | bytes 122888 | tf_op jit(solution)/shard_map/ppermute | solution.py:580
  265.2 4.3 %collective-permute-start.31 = (f32[80,128]{1,0:T(8,128)}, f32[80,128]{1,0:T(8,128)S(1)}, u32[]{:S(2)}, u32[]{:S(2)}) collective-permute-start(f32[80,128]{1,0:T(8,128)} %gas.7.refs_0_), channel_id=1, source_target_pairs={{0,3},{1,0},{2,1},{3,2},{4,7},{5,4},{6,5},{7,6},{8,11},{9,8},{10,9... | collective-permute-start | bytes 122888 | tf_op jit(solution)/shard_map/ppermute | solution.py:580
  268.4 1.1 copy-start.29
  269.0 0.6 copy-start.30
  269.7 0.6 copy-start.31
  (1 other events, 0.6 us)

commit v3 on v2

--- a/solution.py
+++ b/solution.py
@@ -319,7 +319,7 @@
     )(*operands)
 
 
-CELLS = 256
+CELLS = 512
 WIDE = 256
 
 
@@ -357,31 +357,35 @@
 BLOCK = 8
 
 
-def transport(exact, field_ref, base, ncols, group, kind_ref, code_ref, sums_ref, stencil_ref,
+def transport(exact, rows, field_ref, base, ncols, group, kind_ref, code_ref, sums_ref, stencil_ref,
               out_ref, parts_ref, strip_ref, half_ref):
     span = out_ref.shape[1]
     nothing = jnp.minimum(pl.program_id(0), 0)
+    shape = (ncols // 8, 8, LANES)
     table = None
     for l in range(span // WIDE):
         for h in range(WIDE // LANES):
             columns = slice(l * WIDE + h * LANES, l * WIDE + (h + 1) * LANES)
-            x0, x1, x2, vx, y0, y1, y2, vy = (stencil_ref[8 * k:8 * k + 8, columns][None] for k in range(8))
-            x_up = jnp.broadcast_to(vx > 0, (ncols // 8, 8, LANES))
+            x0, x1, x2, vx, y0, y1, y2, _ = (stencil_ref[8 * k:8 * k + 8, columns][None] for k in range(8))
+            x_up = jnp.broadcast_to(vx > 0, shape)
             ahead = 1 if h == 0 else -1
 
             def field(k):
                 start = pl.multiple_of(base + k * ncols, ncols)
-                return field_ref[pl.ds(start, ncols), columns].reshape(ncols // 8, 8, LANES)
-
-            for r in range(BLOCK):
-                near = jnp.where(x_up, field(r + 1), field(r + 3))
-                far = jnp.where(x_up, field(r), field(r + 4))
-                rowwise = x0 * field(r + 2) + x1 * near + x2 * far
+                return field_ref[pl.ds(start, ncols), columns].reshape(shape)
+
+            window = [field(k) for k in range(4)]
+            for r in range(rows):
+                window.append(field(r + 4))
+                near = jnp.where(x_up, window[1], window[3])
+                far = jnp.where(x_up, window[0], window[4])
+                rowwise = x0 * window[2] + x1 * near + x2 * far
+                window = window[1:]
                 slot = h * BLOCK + r
                 strip_ref[slot, PAD:PAD + ncols, :] = rowwise.reshape(ncols, LANES)
 
                 def strip(k):
-                    return strip_ref[slot, pl.ds(nothing + PAD + k, ncols), :].reshape(ncols // 8, 8, LANES)
+                    return strip_ref[slot, pl.ds(nothing + PAD + k, ncols), :].reshape(shape)
 
                 value = y0 * rowwise + y1 * strip(ahead) + y2 * strip(2 * ahead)
                 value = value.reshape(ncols, LANES)
@@ -395,7 +399,7 @@
         for k in range(1 + exact):
             term = dot(half_ref[k, :, columns], sums_ref[columns, :])
             table = term if table is None else table + term
-    for g in range(BLOCK * ncols // LANES):
+    for g in range(rows * ncols // LANES):
         total = table[g * LANES:(g + 1) * LANES, :].T
         kind = kind_ref[pl.ds(group + g, 1), :]
         code = code_ref[pl.ds(group + g, 1), :]
@@ -413,52 +417,63 @@
             [kept[0:10], kept[10:13] + kept[13:16], incident], axis=0)
 
 
-def inner_kernel(relax, exact, ncols, flat_ref, coef_ref, kind_ref, code_ref,
-                 spread_ref, target_ref, factor_ref, wall_ref, sums_ref, stencil_ref,
-                 out_ref, parts_ref, head_ref, tail_ref, field_ref, even_ref, strip_ref, half_ref):
+END = 2
+
+
+def inner_kernel(relax, exact, blocks, ncols, flat_ref, kind_ref, code_ref, sums_ref, stencil_ref, *refs):
+    if relax:
+        coef_ref, spread_ref, target_ref, factor_ref, wall_ref, *refs = refs
+    out_ref, parts_ref, head_ref, tail_ref, field_ref, even_ref, strip_ref, half_ref = refs
     i = pl.program_id(0)
     block = BLOCK * ncols
     span = flat_ref.shape[1]
-    edge = 2 * ncols
-    base = i * block
+    edge = END * ncols
 
     @pl.when(i == 0)
     def _():
         strip_ref[...] = jnp.zeros_like(strip_ref)
-
-    def store(start, l, values):
-        columns = slice(l * WIDE, (l + 1) * WIDE)
-        field_ref[pl.ds(pl.multiple_of(base + start, edge), values.shape[0]), columns] = values
-
-    if relax:
-        relax_tiles(block, spread_ref, (target_ref, factor_ref, wall_ref), coef_ref, even_ref,
-                    flat_ref, store)
-    else:
-        for l in range(span // WIDE):
-            for start in range(0, block, edge):
-                store(start, l, turned(flat_ref[start:start + edge, l * WIDE:(l + 1) * WIDE], l, span))
-
-    @pl.when(i > 1)
+        blank = jnp.zeros((edge, span), jnp.float32)
+        field_ref[:edge, :] = blank
+        field_ref[field_ref.shape[0] - edge:, :] = blank
+
+    @pl.when(i < blocks)
     def _():
-        transport(exact, field_ref, base - block - edge, ncols, (i - 1) * (block // LANES), kind_ref, code_ref,
+        base = edge + i * block
+
+        def store(start, l, values):
+            columns = slice(l * WIDE, (l + 1) * WIDE)
+            field_ref[pl.ds(pl.multiple_of(base + start, edge), values.shape[0]), columns] = values
+
+        if relax:
+            relax_tiles(block, spread_ref, (target_ref, factor_ref, wall_ref), coef_ref, even_ref,
+                        flat_ref, store)
+        else:
+            for l in range(span // WIDE):
+                for start in range(0, block, edge):
+                    store(start, l, turned(flat_ref[start:start + edge, l * WIDE:(l + 1) * WIDE], l, span))
+
+    @pl.when(i > 0)
+    def _():
+        transport(exact, BLOCK, field_ref, (i - 1) * block, ncols, (i - 1) * (block // LANES), kind_ref, code_ref,
                   sums_ref, stencil_ref, out_ref, parts_ref, strip_ref, half_ref)
 
-    @pl.when(i == pl.num_programs(0) - 1)
+    @pl.when(i == blocks)
     def _():
         size = head_ref.shape[0]
-        head_ref[...] = field_ref[:size, :]
-        tail_ref[...] = field_ref[field_ref.shape[0] - size:, :]
-
-
-def outer_kernel(relax, exact, blocks, ncols, count, flat_ref, given_ref, head_ref, tail_ref, low_ref, high_ref,
+        last = field_ref.shape[0] - edge
+        head_ref[...] = field_ref[edge:edge + size, :]
+        tail_ref[...] = field_ref[last - size:last, :]
+
+
+def outer_kernel(relax, exact, ncols, count, flat_ref, given_ref, head_ref, tail_ref, low_ref, high_ref,
                  kind_ref, code_ref, sums_ref, stencil_ref, out_ref, *refs):
     slot_refs = refs[:count]
     parts_ref, field_ref, strip_ref, half_ref = refs[count:]
     i = pl.program_id(0)
-    block = BLOCK * ncols
-    edge = 2 * ncols
+    edge = END * ncols
     size = head_ref.shape[0]
     span = out_ref.shape[1]
+    groups = parts_ref.shape[0] // ROWS
 
     def halo(ref, start):
         for l in range(span // WIDE):
@@ -478,7 +493,7 @@
         field_ref[:size, :] = tail_ref[...]
         halo(high_ref, size)
 
-    transport(exact, field_ref, 0, ncols, i * ((blocks - 1) * (block // LANES)), kind_ref, code_ref,
+    transport(exact, END, field_ref, 0, ncols, i * (groups - edge // LANES), kind_ref, code_ref,
               sums_ref, stencil_ref, out_ref, parts_ref, strip_ref, half_ref)
 
     @pl.when(i == 1)
@@ -496,16 +511,20 @@
     blocks = cells // block
     groups = cells // LANES
     whole = pl.BlockSpec(memory_space=pltpu.VMEM)
-    end = jax.ShapeDtypeStruct(((BLOCK + 2) * ncols, span), jnp.float32)
+    end = jax.ShapeDtypeStruct((2 * END * ncols, span), jnp.float32)
+    operands = [flat, kind, code, sums, stencil]
+    in_specs = [pl.BlockSpec((block, span), lambda i: (jnp.minimum(i, blocks - 1), 0))] + [whole] * 4
+    if relax:
+        operands += [coef, spread, *tables]
+        in_specs += [pl.BlockSpec((block, COEF), lambda i: (jnp.minimum(i, blocks - 1), 0))] + [whole] * 4
     return pl.pallas_call(
-        functools.partial(inner_kernel, relax, exact, ncols),
-        grid=(blocks,),
+        functools.partial(inner_kernel, relax, exact, blocks, ncols),
+        grid=(blocks + 1,),
         out_shape=(jax.ShapeDtypeStruct((cells, span), jnp.float32),
                    jax.ShapeDtypeStruct((groups * ROWS, LANES), jnp.float32), end, end),
-        in_specs=[pl.BlockSpec((block, span), lambda i: (i, 0)),
-                  pl.BlockSpec((block, COEF), lambda i: (i, 0))] + [whole] * 8,
-        out_specs=(pl.BlockSpec((block, span), lambda i: (jnp.maximum(i - 1, 1), 0)), whole, whole, whole),
-        scratch_shapes=[pltpu.VMEM((cells, span), jnp.float32),
+        in_specs=in_specs,
+        out_specs=(pl.BlockSpec((block, span), lambda i: (jnp.maximum(i - 1, 0), 0)), whole, whole, whole),
+        scratch_shapes=[pltpu.VMEM((cells + 2 * END * ncols, span), jnp.float32),
                         pltpu.VMEM((CELLS, 2 * LANES), jnp.float32),
                         pltpu.VMEM((WIDE // LANES * BLOCK, ncols + 2 * PAD, LANES), jnp.float32),
                         pltpu.VMEM((1 + exact, block, span), jnp.bfloat16)],
@@ -513,26 +532,26 @@
         cost_estimate=pl.CostEstimate(flops=12 * cells * span * COEF, bytes_accessed=8 * cells * span,
                                       transcendentals=2 * cells * span),
         name="inner" if relax else "inner_first",
-    )(flat, coef, kind, code, spread, *tables, sums, stencil)
+    )(*operands)
 
 
 def outer(relax, exact, flat, parts, head, tail, low, high, kind, code, sums, stencil, ncols):
     cells, span = flat.shape
-    block = BLOCK * ncols
-    blocks = cells // block
+    edge = END * ncols
+    last = cells // edge - 1
     count = lax.axis_size("vel")
     whole = pl.BlockSpec(memory_space=pltpu.VMEM)
     slot = jax.ShapeDtypeStruct((parts.shape[0] // count, LANES), jnp.float32)
     flat, *slots = pl.pallas_call(
-        functools.partial(outer_kernel, relax, exact, blocks, ncols, count),
+        functools.partial(outer_kernel, relax, exact, ncols, count),
         grid=(2,),
         out_shape=(jax.ShapeDtypeStruct((cells, span), jnp.float32),) + (slot,) * count,
         in_specs=[pl.BlockSpec(memory_space=pl.ANY)] + [whole] * 9,
-        out_specs=(pl.BlockSpec((block, span), lambda i: (i * (blocks - 1), 0)),) + (whole,) * count,
+        out_specs=(pl.BlockSpec((edge, span), lambda i: (i * last, 0)),) + (whole,) * count,
         scratch_shapes=[pltpu.VMEM(parts.shape, jnp.float32),
-                        pltpu.VMEM(((BLOCK + 4) * ncols, span), jnp.float32),
+                        pltpu.VMEM((3 * edge, span), jnp.float32),
                         pltpu.VMEM((WIDE // LANES * BLOCK, ncols + 2 * PAD, LANES), jnp.float32),
-                        pltpu.VMEM((1 + exact, block, span), jnp.bfloat16)],
+                        pltpu.VMEM((1 + exact, edge, span), jnp.bfloat16)],
         input_output_aliases={0: 0},
         compiler_params=pltpu.CompilerParams(vmem_limit_bytes=VMEM_LIMIT),
         name="outer" if relax else "outer_first",
@@ -592,7 +611,7 @@
     target, factor, wall, sums, stencil, spread = setup(span)
     tables = (target, factor, wall)
     edge = 2 * ncols
-    coef = jnp.zeros((cells, COEF), jnp.bfloat16)
+    coef = None
     low, high = flat[:edge], flat[cells - edge:]
     for step in range(STEPS):
         final = step == STEPS - 1

time: 293 us -> 272 us (0.928)
  Pallas kernels: 187 us -> 168 us
    pallas_call x8, Pallas kernels: 147 us -> 128 us  [the longest x4 109 us: inner(): pl.pallas_call(functools.partial(inner_kernel, relax, exact, blocks, ncol...]
  transfers between devices with their start and end apart: 32 -> 32, of which waited for: 24 -> 24; matrix products, arithmetic and copies ran while one was open for 2% -> 1% of each run, Pallas kernels for 37% -> 41%
where the time goes in v3:
time: 272 us; the launch traced here: 271 us
  Pallas kernels  168 us (62%)
  starting transfers between devices  58.7 us (22%)
  waiting for transfers between devices  28.6 us (11%)
  local copies, waits for them, and re-layouts  15.3 us (6%)
    pallas_call x4, Pallas kernels, inner(): pl.pallas_call(functools.partial(inner_kernel, relax, exact, blocks, ncol...  109 us
    ppermute x24, starting transfers between devices, swap(): lax.ppermute(slots[k], 'vel', [(i, (i + k) % count) for i in range(count)])  32.7 us
    ppermute x24, waiting for transfers between devices, swap(): lax.ppermute(slots[k], 'vel', [(i, (i + k) % count) for i in range(count)])  28.5 us
    ppermute x8, starting transfers between devices, exchange(): return (lax.ppermute(last, 'space', up), lax.ppermute(first, 'space', down))  26 us
    pallas_call x4, Pallas kernels, outer(): pl.pallas_call(functools.partial(outer_kernel, relax, exact, ncols, count...  19.4 us
    pallas_call x1, Pallas kernels, finish(): pl.pallas_call(last_kernel, grid=(cells // block,), out_shape=jax.ShapeDt...  17.4 us
    pallas_call x4, Pallas kernels, state(): pl.pallas_call(functools.partial(state_kernel, len(pieces), groups, with_...  14.5 us
    unnamed x67, local copies, waits for them, and re-layouts  9.63 us
  transfers between devices with their start and end apart: 32, of which 24 were waited for; matrix products, arithmetic and copies ran while one was open for 1% of the time, Pallas kernels for 41%

profile of v3, /device:TPU:4, one launch (start us, length us, event | category | flops | bytes accessed | tf_op | source)
XLA Modules:
  0.0 271.1 jit_solution(17714811622121544236)
XLA Ops:
  0.6 1.3 fusion
  1.9 1.9 collective-permute-start
  3.8 4.5 %collective-permute-start.1 = (f32[128,1024]{1,0:T(8,128)S(1)}, f32[128,1024]{1,0:T(8,128)S(1)}, u32[]{:S(2)}, u32[]{:S(2)}) collective-permute-start(f32[128,1024]{1,0:T(8,128)S(1)} %bitcast.6), channel_id=1, source_target_pairs={{4,0},{8,4},{12,8},{16,12},{20,16},{24,20},{28,24},{5,1},{9,5},{13... | collective-permute-start | bytes 1572872 | tf_op jit(solution)/shard_map/ppermute | solution.py:594
  8.4 1.2 setup.1
  9.6 1.4 reshape.25.kind_ref.refs_4_
  11.0 1.4 reshape.26.code_ref.refs_5_
  12.5 23.7 %inner_first.1 = (f32[4096,1024]{1,0:T(8,128)}, f32[448,128]{1,0:T(8,128)}, f32[256,1024]{1,0:T(8,128)}, f32[256,1024]{1,0:T(8,128)}) custom-call(f32[4096,1024]{1,0:T(8,128)} %bitcast.4, s32[32,128]{1,0:T(8,128)} %reshape.25.kind_ref.refs_4_, s32[32,128]{1,0:T(8,128)} %reshape.26.code_ref.refs_5_, bf16[1024,128]{1,0:T(8,128)(2,1)} %get-tuple-element.55.sums_ref, ...), custom_call_target="tpu_custom_call" | custom-call | flops 3221225472 | bytes 33554432 | tf_op jit(solution)/shard_map/inner_first/pallas_call | solution.py:520
  37.1 5.0 %outer_first.1 = (f32[4096,1024]{1,0:T(8,128)}, f32[112,128]{1,0:T(8,128)}, f32[112,128]{1,0:T(8,128)}, f32[112,128]{1,0:T(8,128)}, f32[112,128]{1,0:T(8,128)}) custom-call(f32[4096,1024]{1,0:T(8,128)} %get-tuple-element.57.flat_ref, f32[448,128]{1,0:T(8,128)} %get-tuple-element.58.given_ref, ...), custom_call_target="tpu_custom_call", output_to_operand_aliasing={{0}: (0, {})} | custom-call | tf_op jit(solution)/shard_map/outer_first/pallas_call | solution.py:545
  42.1 1.6 collective-permute-start.2
  43.7 2.6 collective-permute-start.3
  46.3 1.3 collective-permute-start.4
  48.9 1.4 collective-permute-done.3.refs_2_
  51.4 1.6 gas.4.refs_0_
  53.6 3.0 %collective-permute-start.6 = (f32[80,128]{1,0:T(8,128)}, f32[80,128]{1,0:T(8,128)S(1)}, u32[]{:S(2)}, u32[]{:S(2)}) collective-permute-start(f32[80,128]{1,0:T(8,128)} %gas.4.refs_0_), channel_id=1, source_target_pairs={{0,2},{1,3},{2,0},{3,1},{4,6},{5,7},{6,4},{7,5},{8,10},{9,11},{10,... | collective-permute-start | bytes 122888 | tf_op jit(solution)/shard_map/ppermute | solution.py:599
  56.8 2.3 collective-permute-done.5.refs_1_
  59.7 1.1 collective-permute-done.7.refs_3_
  61.5 4.0 %state.4 = (bf16[4096,64]{1,0:T(8,128)(2,1)}, f32[128,1024]{1,0:T(8,128)}, f32[128,1024]{1,0:T(8,128)}) custom-call(f32[80,128]{1,0:T(8,128)} %gas.4.refs_0_, f32[80,128]{1,0:T(8,128)} %copy-done.20, f32[80,128]{1,0:T(8,128)} %copy-done.23, f32[80,128]{1,0:T(8,128)} %copy-done.26, s32[32,128]{1,0:T(8,128)} %reshape.25.kind_ref.refs_4_, ...), custom_call_target="tpu_custom_call" | custom-call | tf_op jit(solution)/shard_map/state/pallas_call | solution.py:309
  65.4 1.9 collective-permute-start.8
  67.3 4.5 %collective-permute-start.9 = (f32[128,1024]{1,0:T(8,128)}, f32[128,1024]{1,0:T(8,128)S(1)}, u32[]{:S(2)}, u32[]{:S(2)}) collective-permute-start(f32[128,1024]{1,0:T(8,128)} %get-tuple-element.76), channel_id=1, source_target_pairs={{4,0},{8,4},{12,8},{16,12},{20,16},{24,20},{28,24},{5,1},{9,5},{13... | collective-permute-start | bytes 1572872 | tf_op jit(solution)/shard_map/ppermute | solution.py:594
  71.9 27.4 %inner.3 = (f32[4096,1024]{1,0:T(8,128)}, f32[448,128]{1,0:T(8,128)}, f32[256,1024]{1,0:T(8,128)}, f32[256,1024]{1,0:T(8,128)}) custom-call(f32[4096,1024]{1,0:T(8,128)} %get-tuple-element.61.refs_7_.refs_8_.flat_ref, s32[32,128]{1,0:T(8,128)} %reshape.25.kind_ref.refs_4_, s32[32,128]{1,0:T(8,128)} %reshape.26.code_ref.refs_5_, ...), custom_call_target="tpu_custom_call" | custom-call | flops 3221225472 | bytes 33554432 | tf_op jit(solution)/shard_map/inner/pallas_call | solution.py:520
  100.2 4.8 %outer.3 = (f32[4096,1024]{1,0:T(8,128)}, f32[112,128]{1,0:T(8,128)}, f32[112,128]{1,0:T(8,128)}, f32[112,128]{1,0:T(8,128)}, f32[112,128]{1,0:T(8,128)}) custom-call(f32[4096,1024]{1,0:T(8,128)} %get-tuple-element.71.flat_ref, f32[448,128]{1,0:T(8,128)} %get-tuple-element.72.given_ref, ...), custom_call_target="tpu_custom_call", output_to_operand_aliasing={{0}: (0, {})} | custom-call | tf_op jit(solution)/shard_map/outer/pallas_call | solution.py:545
  105.7 2.0 collective-permute-start.11
  107.8 1.1 collective-permute-start.12
  108.9 2.4 collective-permute-done.10.refs_1_
  111.3 1.0 collective-permute-done.11.refs_2_
  113.1 1.6 gas.5.refs_0_
  114.7 1.3 collective-permute-start.13
  116.0 2.0 collective-permute-start.14
  118.5 2.2 collective-permute-done.13.refs_1_
  120.7 0.9 collective-permute-done.14.refs_2_
  122.8 4.0 %state.5 = (bf16[4096,64]{1,0:T(8,128)(2,1)}, f32[128,1024]{1,0:T(8,128)}, f32[128,1024]{1,0:T(8,128)}) custom-call(f32[80,128]{1,0:T(8,128)} %gas.5.refs_0_, f32[80,128]{1,0:T(8,128)} %copy-done.21, f32[80,128]{1,0:T(8,128)} %copy-done.24, f32[80,128]{1,0:T(8,128)} %copy-done.27, s32[32,128]{1,0:T(8,128)} %reshape.25.kind_ref.refs_4_, ...), custom_call_target="tpu_custom_call" | custom-call | tf_op jit(solution)/shard_map/state/pallas_call | solution.py:309
  126.8 1.9 collective-permute-start.16
  128.7 4.7 %collective-permute-start.17 = (f32[128,1024]{1,0:T(8,128)}, f32[128,1024]{1,0:T(8,128)S(1)}, u32[]{:S(2)}, u32[]{:S(2)}) collective-permute-start(f32[128,1024]{1,0:T(8,128)} %get-tuple-element.88), channel_id=1, source_target_pairs={{4,0},{8,4},{12,8},{16,12},{20,16},{24,20},{28,24},{5,1},{9,5},{13... | collective-permute-start | bytes 1572872 | tf_op jit(solution)/shard_map/ppermute | solution.py:594
  133.4 27.4 %inner.4 = (f32[4096,1024]{1,0:T(8,128)}, f32[448,128]{1,0:T(8,128)}, f32[256,1024]{1,0:T(8,128)}, f32[256,1024]{1,0:T(8,128)}) custom-call(f32[4096,1024]{1,0:T(8,128)} %get-tuple-element.77.refs_7_.refs_8_.flat_ref, s32[32,128]{1,0:T(8,128)} %reshape.25.kind_ref.refs_4_, s32[32,128]{1,0:T(8,128)} %reshape.26.code_ref.refs_5_, ...), custom_call_target="tpu_custom_call" | custom-call | flops 3221225472 | bytes 33554432 | tf_op jit(solution)/shard_map/inner/pallas_call | solution.py:520
  160.8 0.8 copy-done.4
  161.8 4.7 %outer.4 = (f32[4096,1024]{1,0:T(8,128)}, f32[112,128]{1,0:T(8,128)}, f32[112,128]{1,0:T(8,128)}, f32[112,128]{1,0:T(8,128)}, f32[112,128]{1,0:T(8,128)}) custom-call(f32[4096,1024]{1,0:T(8,128)} %get-tuple-element.83.flat_ref, f32[448,128]{1,0:T(8,128)} %get-tuple-element.84.given_ref, ...), custom_call_target="tpu_custom_call", output_to_operand_aliasing={{0}: (0, {})} | custom-call | tf_op jit(solution)/shard_map/outer/pallas_call | solution.py:545
  166.5 1.1 collective-permute-start.18
  167.6 1.8 collective-permute-start.19
  169.5 1.0 collective-permute-start.20
  170.5 2.3 collective-permute-done.18.refs_1_
  172.8 1.3 collective-permute-done.19.refs_2_
  175.0 1.6 gas.6.refs_0_
  176.6 1.0 collective-permute-start.21
  177.6 2.1 collective-permute-start.22
  180.4 2.2 collective-permute-done.21.refs_1_
  182.6 0.8 collective-permute-done.22.refs_2_
  184.5 4.0 %state.6 = (bf16[4096,64]{1,0:T(8,128)(2,1)}, f32[128,1024]{1,0:T(8,128)}, f32[128,1024]{1,0:T(8,128)}) custom-call(f32[80,128]{1,0:T(8,128)} %gas.6.refs_0_, f32[80,128]{1,0:T(8,128)} %copy-done.22, f32[80,128]{1,0:T(8,128)} %copy-done.25, f32[80,128]{1,0:T(8,128)} %copy-done.28, s32[32,128]{1,0:T(8,128)} %reshape.25.kind_ref.refs_4_, ...), custom_call_target="tpu_custom_call" | custom-call | tf_op jit(solution)/shard_map/state/pallas_call | solution.py:309
  188.5 1.9 collective-permute-start.24
  190.4 4.5 %collective-permute-start.25 = (f32[128,1024]{1,0:T(8,128)}, f32[128,1024]{1,0:T(8,128)S(1)}, u32[]{:S(2)}, u32[]{:S(2)}) collective-permute-start(f32[128,1024]{1,0:T(8,128)} %get-tuple-element.100), channel_id=1, source_target_pairs={{4,0},{8,4},{12,8},{16,12},{20,16},{24,20},{28,24},{5,1},{9,5},{13... | collective-permute-start | bytes 1572872 | tf_op jit(solution)/shard_map/ppermute | solution.py:594
  194.9 30.3 %inner.5 = (f32[4096,1024]{1,0:T(8,128)}, f32[448,128]{1,0:T(8,128)}, f32[256,1024]{1,0:T(8,128)}, f32[256,1024]{1,0:T(8,128)}) custom-call(f32[4096,1024]{1,0:T(8,128)} %get-tuple-element.89.refs_7_.refs_8_.flat_ref, s32[32,128]{1,0:T(8,128)} %reshape.25.kind_ref.refs_4_, s32[32,128]{1,0:T(8,128)} %reshape.26.code_ref.refs_5_, ...), custom_call_target="tpu_custom_call" | custom-call | flops 3221225472 | bytes 33554432 | tf_op jit(solution)/shard_map/inner/pallas_call | solution.py:520
  226.2 4.9 %outer.5 = (f32[4096,1024]{1,0:T(8,128)}, f32[112,128]{1,0:T(8,128)}, f32[112,128]{1,0:T(8,128)}, f32[112,128]{1,0:T(8,128)}, f32[112,128]{1,0:T(8,128)}) custom-call(f32[4096,1024]{1,0:T(8,128)} %get-tuple-element.95.flat_ref, f32[448,128]{1,0:T(8,128)} %get-tuple-element.96.given_ref, ...), custom_call_target="tpu_custom_call", output_to_operand_aliasing={{0}: (0, {})} | custom-call | tf_op jit(solution)/shard_map/outer/pallas_call | solution.py:545
  231.2 1.3 collective-permute-start.26
  232.5 1.8 collective-permute-start.27
  234.3 0.9 collective-permute-start.28
  235.2 2.3 collective-permute-done.26.refs_1_
  237.4 1.3 collective-permute-done.27.refs_2_
  239.8 1.6 gas.7.refs_0_
  241.4 0.8 collective-permute-start.29
  242.2 2.1 collective-permute-start.30
  244.4 0.9 collective-permute-start.31
  245.3 2.3 collective-permute-done.29.refs_1_
  249.4 2.6 state.7
  252.1 0.8 reshape.29
  253.6 17.4 %finish.1 = f32[4096,1024]{1,0:T(8,128)} custom-call(f32[4096,1024]{1,0:T(8,128)} %get-tuple-element.101.flat_ref, bf16[4096,64]{1,0:T(8,128)(2,1)} %get-tuple-element.106.coef_ref, bf16[64,256]{1,0:T(8,128)(2,1)} %get-tuple-element.66.refs_9_.refs_1_.spread_ref, bf16[64,1024]{1,0:T(8,128)(2,1)} %get-tuple-element.67.refs_10_.refs_2_.target_ref, ...), custom_call_target="tpu_custom_call" | custom-call | tf_op jit(solution)/shard_map/finish/pallas_call | solution.py:576
  (91 shorter events, 17.1 us)
Async XLA Ops:
  1.9 34.2 %collective-permute-start = (f32[128,1024]{1,0:T(8,128)S(1)}, f32[128,1024]{1,0:T(8,128)S(1)}, u32[]{:S(2)}, u32[]{:S(2)}) collective-permute-start(f32[128,1024]{1,0:T(8,128)S(1)} %bitcast.7), channel_id=1, source_target_pairs={{0,4},{4,8},{8,12},{12,16},{16,20},{20,24},{24,28},{1,5},{5,9},{9,... | collective-permute-start | bytes 1572872 | tf_op jit(solution)/shard_map/ppermute | solution.py:594
  3.8 32.3 %collective-permute-start.1 = (f32[128,1024]{1,0:T(8,128)S(1)}, f32[128,1024]{1,0:T(8,128)S(1)}, u32[]{:S(2)}, u32[]{:S(2)}) collective-permute-start(f32[128,1024]{1,0:T(8,128)S(1)} %bitcast.6), channel_id=1, source_target_pairs={{4,0},{8,4},{12,8},{16,12},{20,16},{24,20},{28,24},{5,1},{9,5},{13... | collective-permute-start | bytes 1572872 | tf_op jit(solution)/shard_map/ppermute | solution.py:594
  12.5 35.2 %copy-start.32 = (f32[64,64]{1,0:T(8,128)S(1)}, f32[64,64]{1,0:T(8,128)}, u32[]{:S(2)}) copy-start(f32[64,64]{1,0:T(8,128)} %param.7) | copy-start | bytes 49156
  36.2 0.8 copy-start
  36.2 1.0 copy-start.1
  42.1 6.8 %collective-permute-start.2 = (f32[112,128]{1,0:T(8,128)}, f32[112,128]{1,0:T(8,128)S(1)}, u32[]{:S(2)}, u32[]{:S(2)}) collective-permute-start(f32[112,128]{1,0:T(8,128)} %get-tuple-element.63), channel_id=1, source_target_pairs={{0,1},{1,2},{2,3},{3,0},{4,5},{5,6},{6,7},{7,4},{8,9},{9,10},{10,1... | collective-permute-start | bytes 172040 | tf_op jit(solution)/shard_map/ppermute | solution.py:599
  43.7 6.6 %collective-permute-start.3 = (f32[112,128]{1,0:T(8,128)}, f32[112,128]{1,0:T(8,128)S(1)}, u32[]{:S(2)}, u32[]{:S(2)}) collective-permute-start(f32[112,128]{1,0:T(8,128)} %get-tuple-element.64), channel_id=1, source_target_pairs={{0,2},{1,3},{2,0},{3,1},{4,6},{5,7},{6,4},{7,5},{8,10},{9,11},{10,... | collective-permute-start | bytes 172040 | tf_op jit(solution)/shard_map/ppermute | solution.py:599
  46.3 4.5 %collective-permute-start.4 = (f32[112,128]{1,0:T(8,128)}, f32[112,128]{1,0:T(8,128)S(1)}, u32[]{:S(2)}, u32[]{:S(2)}) collective-permute-start(f32[112,128]{1,0:T(8,128)} %get-tuple-element.65), channel_id=1, source_target_pairs={{0,3},{1,0},{2,1},{3,2},{4,7},{5,4},{6,5},{7,6},{8,11},{9,8},{10,9... | collective-permute-start | bytes 172040 | tf_op jit(solution)/shard_map/ppermute | solution.py:599
  48.9 1.9 copy-start.8
  50.3 0.6 copy-start.12
  50.8 0.6 copy-start.16
  53.0 6.1 %collective-permute-start.5 = (f32[80,128]{1,0:T(8,128)}, f32[80,128]{1,0:T(8,128)S(1)}, u32[]{:S(2)}, u32[]{:S(2)}) collective-permute-start(f32[80,128]{1,0:T(8,128)} %gas.4.refs_0_), channel_id=1, source_target_pairs={{0,1},{1,2},{2,3},{3,0},{4,5},{5,6},{6,7},{7,4},{8,9},{9,10},{10,1... | collective-permute-start | bytes 122888 | tf_op jit(solution)/shard_map/ppermute | solution.py:599
  53.6 6.1 %collective-permute-start.6 = (f32[80,128]{1,0:T(8,128)}, f32[80,128]{1,0:T(8,128)S(1)}, u32[]{:S(2)}, u32[]{:S(2)}) collective-permute-start(f32[80,128]{1,0:T(8,128)} %gas.4.refs_0_), channel_id=1, source_target_pairs={{0,2},{1,3},{2,0},{3,1},{4,6},{5,7},{6,4},{7,5},{8,10},{9,11},{10,... | collective-permute-start | bytes 122888 | tf_op jit(solution)/shard_map/ppermute | solution.py:599
  56.6 4.2 %collective-permute-start.7 = (f32[80,128]{1,0:T(8,128)}, f32[80,128]{1,0:T(8,128)S(1)}, u32[]{:S(2)}, u32[]{:S(2)}) collective-permute-start(f32[80,128]{1,0:T(8,128)} %gas.4.refs_0_), channel_id=1, source_target_pairs={{0,3},{1,0},{2,1},{3,2},{4,7},{5,4},{6,5},{7,6},{8,11},{9,8},{10,9... | collective-permute-start | bytes 122888 | tf_op jit(solution)/shard_map/ppermute | solution.py:599
  59.1 1.7 copy-start.20
  59.7 1.1 copy-start.23
  60.9 0.6 copy-start.26
  65.4 33.8 %collective-permute-start.8 = (f32[128,1024]{1,0:T(8,128)}, f32[128,1024]{1,0:T(8,128)S(1)}, u32[]{:S(2)}, u32[]{:S(2)}) collective-permute-start(f32[128,1024]{1,0:T(8,128)} %get-tuple-element.75), channel_id=1, source_target_pairs={{0,4},{4,8},{8,12},{12,16},{16,20},{20,24},{24,28},{1,5},{5,9},{9,... | collective-permute-start | bytes 1572872 | tf_op jit(solution)/shard_map/ppermute | solution.py:594
  67.3 31.9 %collective-permute-start.9 = (f32[128,1024]{1,0:T(8,128)}, f32[128,1024]{1,0:T(8,128)S(1)}, u32[]{:S(2)}, u32[]{:S(2)}) collective-permute-start(f32[128,1024]{1,0:T(8,128)} %get-tuple-element.76), channel_id=1, source_target_pairs={{4,0},{8,4},{12,8},{16,12},{20,16},{24,20},{28,24},{5,1},{9,5},{13... | collective-permute-start | bytes 1572872 | tf_op jit(solution)/shard_map/ppermute | solution.py:594
  99.2 0.8 copy-start.3
  99.3 1.0 copy-start.6
  105.0 6.3 %collective-permute-start.10 = (f32[112,128]{1,0:T(8,128)}, f32[112,128]{1,0:T(8,128)S(1)}, u32[]{:S(2)}, u32[]{:S(2)}) collective-permute-start(f32[112,128]{1,0:T(8,128)} %get-tuple-element.79), channel_id=1, source_target_pairs={{0,1},{1,2},{2,3},{3,0},{4,5},{5,6},{6,7},{7,4},{8,9},{9,10},{10,1... | collective-permute-start | bytes 172040 | tf_op jit(solution)/shard_map/ppermute | solution.py:599
  105.7 6.6 %collective-permute-start.11 = (f32[112,128]{1,0:T(8,128)}, f32[112,128]{1,0:T(8,128)S(1)}, u32[]{:S(2)}, u32[]{:S(2)}) collective-permute-start(f32[112,128]{1,0:T(8,128)} %get-tuple-element.80), channel_id=1, source_target_pairs={{0,2},{1,3},{2,0},{3,1},{4,6},{5,7},{6,4},{7,5},{8,10},{9,11},{10,... | collective-permute-start | bytes 172040 | tf_op jit(solution)/shard_map/ppermute | solution.py:599
  107.8 4.7 %collective-permute-start.12 = (f32[112,128]{1,0:T(8,128)}, f32[112,128]{1,0:T(8,128)S(1)}, u32[]{:S(2)}, u32[]{:S(2)}) collective-permute-start(f32[112,128]{1,0:T(8,128)} %get-tuple-element.81), channel_id=1, source_target_pairs={{0,3},{1,0},{2,1},{3,2},{4,7},{5,4},{6,5},{7,6},{8,11},{9,8},{10,9... | collective-permute-start | bytes 172040 | tf_op jit(solution)/shard_map/ppermute | solution.py:599
  111.3 1.2 copy-start.9
  112.4 0.6 copy-start.13
  112.5 0.6 copy-start.17
  114.7 6.0 %collective-permute-start.13 = (f32[80,128]{1,0:T(8,128)}, f32[80,128]{1,0:T(8,128)S(1)}, u32[]{:S(2)}, u32[]{:S(2)}) collective-permute-start(f32[80,128]{1,0:T(8,128)} %gas.5.refs_0_), channel_id=1, source_target_pairs={{0,1},{1,2},{2,3},{3,0},{4,5},{5,6},{6,7},{7,4},{8,9},{9,10},{10,1... | collective-permute-start | bytes 122888 | tf_op jit(solution)/shard_map/ppermute | solution.py:599
  116.0 5.6 %collective-permute-start.14 = (f32[80,128]{1,0:T(8,128)}, f32[80,128]{1,0:T(8,128)S(1)}, u32[]{:S(2)}, u32[]{:S(2)}) collective-permute-start(f32[80,128]{1,0:T(8,128)} %gas.5.refs_0_), channel_id=1, source_target_pairs={{0,2},{1,3},{2,0},{3,1},{4,6},{5,7},{6,4},{7,5},{8,10},{9,11},{10,... | collective-permute-start | bytes 122888 | tf_op jit(solution)/shard_map/ppermute | solution.py:599
  118.0 4.2 %collective-permute-start.15 = (f32[80,128]{1,0:T(8,128)}, f32[80,128]{1,0:T(8,128)S(1)}, u32[]{:S(2)}, u32[]{:S(2)}) collective-permute-start(f32[80,128]{1,0:T(8,128)} %gas.5.refs_0_), channel_id=1, source_target_pairs={{0,3},{1,0},{2,1},{3,2},{4,7},{5,4},{6,5},{7,6},{8,11},{9,8},{10,9... | collective-permute-start | bytes 122888 | tf_op jit(solution)/shard_map/ppermute | solution.py:599
  120.7 1.5 copy-start.21
  121.6 0.6 copy-start.24
  122.2 0.6 copy-start.27
  126.8 34.0 %collective-permute-start.16 = (f32[128,1024]{1,0:T(8,128)}, f32[128,1024]{1,0:T(8,128)S(1)}, u32[]{:S(2)}, u32[]{:S(2)}) collective-permute-start(f32[128,1024]{1,0:T(8,128)} %get-tuple-element.87), channel_id=1, source_target_pairs={{0,4},{4,8},{8,12},{12,16},{16,20},{20,24},{24,28},{1,5},{5,9},{9,... | collective-permute-start | bytes 1572872 | tf_op jit(solution)/shard_map/ppermute | solution.py:594
  128.7 32.1 %collective-permute-start.17 = (f32[128,1024]{1,0:T(8,128)}, f32[128,1024]{1,0:T(8,128)S(1)}, u32[]{:S(2)}, u32[]{:S(2)}) collective-permute-start(f32[128,1024]{1,0:T(8,128)} %get-tuple-element.88), channel_id=1, source_target_pairs={{4,0},{8,4},{12,8},{16,12},{20,16},{24,20},{28,24},{5,1},{9,5},{13... | collective-permute-start | bytes 1572872 | tf_op jit(solution)/shard_map/ppermute | solution.py:594
  160.8 0.8 copy-start.4
  160.8 1.0 copy-start.7
  166.5 6.3 %collective-permute-start.18 = (f32[112,128]{1,0:T(8,128)}, f32[112,128]{1,0:T(8,128)S(1)}, u32[]{:S(2)}, u32[]{:S(2)}) collective-permute-start(f32[112,128]{1,0:T(8,128)} %get-tuple-element.91), channel_id=1, source_target_pairs={{0,1},{1,2},{2,3},{3,0},{4,5},{5,6},{6,7},{7,4},{8,9},{9,10},{10,1... | collective-permute-start | bytes 172040 | tf_op jit(solution)/shard_map/ppermute | solution.py:599
  167.6 6.5 %collective-permute-start.19 = (f32[112,128]{1,0:T(8,128)}, f32[112,128]{1,0:T(8,128)S(1)}, u32[]{:S(2)}, u32[]{:S(2)}) collective-permute-start(f32[112,128]{1,0:T(8,128)} %get-tuple-element.92), channel_id=1, source_target_pairs={{0,2},{1,3},{2,0},{3,1},{4,6},{5,7},{6,4},{7,5},{8,10},{9,11},{10,... | collective-permute-start | bytes 172040 | tf_op jit(solution)/shard_map/ppermute | solution.py:599
  169.5 4.9 %collective-permute-start.20 = (f32[112,128]{1,0:T(8,128)}, f32[112,128]{1,0:T(8,128)S(1)}, u32[]{:S(2)}, u32[]{:S(2)}) collective-permute-start(f32[112,128]{1,0:T(8,128)} %get-tuple-element.93), channel_id=1, source_target_pairs={{0,3},{1,0},{2,1},{3,2},{4,7},{5,4},{6,5},{7,6},{8,11},{9,8},{10,9... | collective-permute-start | bytes 172040 | tf_op jit(solution)/shard_map/ppermute | solution.py:599
  172.8 1.6 copy-start.10
  174.1 0.6 copy-start.14
  174.4 0.6 copy-start.18
  176.6 6.0 %collective-permute-start.21 = (f32[80,128]{1,0:T(8,128)}, f32[80,128]{1,0:T(8,128)S(1)}, u32[]{:S(2)}, u32[]{:S(2)}) collective-permute-start(f32[80,128]{1,0:T(8,128)} %gas.6.refs_0_), channel_id=1, source_target_pairs={{0,1},{1,2},{2,3},{3,0},{4,5},{5,6},{6,7},{7,4},{8,9},{9,10},{10,1... | collective-permute-start | bytes 122888 | tf_op jit(solution)/shard_map/ppermute | solution.py:599
  177.6 5.9 %collective-permute-start.22 = (f32[80,128]{1,0:T(8,128)}, f32[80,128]{1,0:T(8,128)S(1)}, u32[]{:S(2)}, u32[]{:S(2)}) collective-permute-start(f32[80,128]{1,0:T(8,128)} %gas.6.refs_0_), channel_id=1, source_target_pairs={{0,2},{1,3},{2,0},{3,1},{4,6},{5,7},{6,4},{7,5},{8,10},{9,11},{10,... | collective-permute-start | bytes 122888 | tf_op jit(solution)/shard_map/ppermute | solution.py:599
  179.7 4.2 %collective-permute-start.23 = (f32[80,128]{1,0:T(8,128)}, f32[80,128]{1,0:T(8,128)S(1)}, u32[]{:S(2)}, u32[]{:S(2)}) collective-permute-start(f32[80,128]{1,0:T(8,128)} %gas.6.refs_0_), channel_id=1, source_target_pairs={{0,3},{1,0},{2,1},{3,2},{4,7},{5,4},{6,5},{7,6},{8,11},{9,8},{10,9... | collective-permute-start | bytes 122888 | tf_op jit(solution)/shard_map/ppermute | solution.py:599
  182.6 1.3 copy-start.22
  183.5 0.6 copy-start.25
  188.5 36.8 %collective-permute-start.24 = (f32[128,1024]{1,0:T(8,128)}, f32[128,1024]{1,0:T(8,128)S(1)}, u32[]{:S(2)}, u32[]{:S(2)}) collective-permute-start(f32[128,1024]{1,0:T(8,128)} %get-tuple-element.99), channel_id=1, source_target_pairs={{0,4},{4,8},{8,12},{12,16},{16,20},{20,24},{24,28},{1,5},{5,9},{9,... | collective-permute-start | bytes 1572872 | tf_op jit(solution)/shard_map/ppermute | solution.py:594
  190.4 34.9 %collective-permute-start.25 = (f32[128,1024]{1,0:T(8,128)}, f32[128,1024]{1,0:T(8,128)S(1)}, u32[]{:S(2)}, u32[]{:S(2)}) collective-permute-start(f32[128,1024]{1,0:T(8,128)} %get-tuple-element.100), channel_id=1, source_target_pairs={{4,0},{8,4},{12,8},{16,12},{20,16},{24,20},{28,24},{5,1},{9,5},{13... | collective-permute-start | bytes 1572872 | tf_op jit(solution)/shard_map/ppermute | solution.py:594
  225.3 0.8 copy-start.2
  225.3 1.0 copy-start.5
  231.2 6.3 %collective-permute-start.26 = (f32[112,128]{1,0:T(8,128)}, f32[112,128]{1,0:T(8,128)S(1)}, u32[]{:S(2)}, u32[]{:S(2)}) collective-permute-start(f32[112,128]{1,0:T(8,128)} %get-tuple-element.103), channel_id=1, source_target_pairs={{0,1},{1,2},{2,3},{3,0},{4,5},{5,6},{6,7},{7,4},{8,9},{9,10},{10,1... | collective-permute-start | bytes 172040 | tf_op jit(solution)/shard_map/ppermute | solution.py:599
  232.5 6.2 %collective-permute-start.27 = (f32[112,128]{1,0:T(8,128)}, f32[112,128]{1,0:T(8,128)S(1)}, u32[]{:S(2)}, u32[]{:S(2)}) collective-permute-start(f32[112,128]{1,0:T(8,128)} %get-tuple-element.104), channel_id=1, source_target_pairs={{0,2},{1,3},{2,0},{3,1},{4,6},{5,7},{6,4},{7,5},{8,10},{9,11},{10,... | collective-permute-start | bytes 172040 | tf_op jit(solution)/shard_map/ppermute | solution.py:599
  234.3 4.9 %collective-permute-start.28 = (f32[112,128]{1,0:T(8,128)}, f32[112,128]{1,0:T(8,128)S(1)}, u32[]{:S(2)}, u32[]{:S(2)}) collective-permute-start(f32[112,128]{1,0:T(8,128)} %get-tuple-element.105), channel_id=1, source_target_pairs={{0,3},{1,0},{2,1},{3,2},{4,7},{5,4},{6,5},{7,6},{8,11},{9,8},{10,9... | collective-permute-start | bytes 172040 | tf_op jit(solution)/shard_map/ppermute | solution.py:599
  237.4 1.8 copy-start.11
  238.7 0.6 copy-start.15
  239.2 0.6 copy-start.19
  241.4 6.1 %collective-permute-start.29 = (f32[80,128]{1,0:T(8,128)}, f32[80,128]{1,0:T(8,128)S(1)}, u32[]{:S(2)}, u32[]{:S(2)}) collective-permute-start(f32[80,128]{1,0:T(8,128)} %gas.7.refs_0_), channel_id=1, source_target_pairs={{0,1},{1,2},{2,3},{3,0},{4,5},{5,6},{6,7},{7,4},{8,9},{9,10},{10,1... | collective-permute-start | bytes 122888 | tf_op jit(solution)/shard_map/ppermute | solution.py:599
  242.2 6.0 %collective-permute-start.30 = (f32[80,128]{1,0:T(8,128)}, f32[80,128]{1,0:T(8,128)S(1)}, u32[]{:S(2)}, u32[]{:S(2)}) collective-permute-start(f32[80,128]{1,0:T(8,128)} %gas.7.refs_0_), channel_id=1, source_target_pairs={{0,2},{1,3},{2,0},{3,1},{4,6},{5,7},{6,4},{7,5},{8,10},{9,11},{10,... | collective-permute-start | bytes 122888 | tf_op jit(solution)/shard_map/ppermute | solution.py:599
  244.4 4.3 %collective-permute-start.31 = (f32[80,128]{1,0:T(8,128)}, f32[80,128]{1,0:T(8,128)S(1)}, u32[]{:S(2)}, u32[]{:S(2)}) collective-permute-start(f32[80,128]{1,0:T(8,128)} %gas.7.refs_0_), channel_id=1, source_target_pairs={{0,3},{1,0},{2,1},{3,2},{4,7},{5,4},{6,5},{7,6},{8,11},{9,8},{10,9... | collective-permute-start | bytes 122888 | tf_op jit(solution)/shard_map/ppermute | solution.py:599
  247.5 1.1 copy-start.29
  248.2 0.6 copy-start.30
  248.8 0.6 copy-start.31
  (1 other events, 0.6 us)

commit v4 on v3

--- a/solution.py
+++ b/solution.py
@@ -36,11 +36,17 @@
 COEF = 2 * PART
 STRIDE = COEF + 1
 
-VMEM_LIMIT = 60 * 1024 * 1024
-
-
-def setup_kernel(span, target_ref, factor_ref, wall_ref, sums_ref, stencil_ref, spread_ref,
+VMEM_LIMIT = 44 * 1024 * 1024
+SMALL_LIMIT = 24 * 1024 * 1024
+
+
+def setup_kernel(span, kind_in_ref, code_in_ref, temp_in_ref, kind_ref, code_ref, temp_ref, target_ref, factor_ref, wall_ref, sums_ref, stencil_ref, spread_ref,
                  feature_ref, moment_ref):
+    for in_ref, ref in ((kind_in_ref, kind_ref), (code_in_ref, code_ref), (temp_in_ref, temp_ref)):
+        ncols = in_ref.shape[1]
+        joined = LANES // ncols
+        for k in range(joined):
+            ref[:, k * ncols:(k + 1) * ncols] = in_ref[pl.ds(k, ref.shape[0], stride=joined), :]
     shape = (8, span)
     place = lax.broadcasted_iota(jnp.int32, shape, 1)
     third = lax.axis_index("vel") * (span // WIDE) + place // WIDE
@@ -99,18 +105,21 @@
     spread_ref[...] = jnp.where(hit, 1.0, 0.0).astype(jnp.bfloat16)
 
 
-def setup(span):
+def setup(span, *given):
+    groups = given[0].size // LANES
+    whole = pl.BlockSpec(memory_space=pltpu.VMEM)
     table = jax.ShapeDtypeStruct((COEF, span), jnp.bfloat16)
     return pl.pallas_call(
         functools.partial(setup_kernel, span),
-        out_shape=(table, table, table,
+        out_shape=tuple(jax.ShapeDtypeStruct((groups, LANES), g.dtype) for g in given) + (table, table, table,
                    jax.ShapeDtypeStruct((span, LANES), jnp.bfloat16),
                    jax.ShapeDtypeStruct((64, span), jnp.float32),
                    jax.ShapeDtypeStruct((COEF, 2 * LANES), jnp.bfloat16)),
-        out_specs=(pl.BlockSpec(memory_space=pltpu.VMEM),) * 6,
+        in_specs=[whole] * 3,
+        out_specs=(whole,) * 9,
         scratch_shapes=[pltpu.VMEM((PART, span), jnp.float32), pltpu.VMEM((LANES, span), jnp.float32)],
         name="setup",
-    )()
+    )(*given)
 
 
 def turned(values, l, span, back=False):
@@ -290,36 +299,28 @@
                                           factor_ref[:, columns], wall_ref[:, columns])
 
 
-def state(with_edges, pieces, kind, code, temp, flat, spread, tables, ncols):
+def state(with_edges, pieces, kind, code, temp, first, last, spread, tables):
     groups = kind.shape[0]
-    cells, span = flat.shape
-    size = 2 * ncols
-    last = cells // size - 1
     whole = pl.BlockSpec(memory_space=pltpu.VMEM)
     operands = [*pieces, kind, code, temp]
-    in_specs = [whole] * len(operands)
-    out_shape = (jax.ShapeDtypeStruct((cells, COEF), jnp.bfloat16),)
+    out_shape = (jax.ShapeDtypeStruct((groups * LANES, COEF), jnp.bfloat16),)
     if with_edges:
-        operands += [flat, flat, spread, *tables]
-        in_specs += [pl.BlockSpec((size, span), lambda i: (0, 0)),
-                     pl.BlockSpec((size, span), lambda i: (last, 0))] + [whole] * 4
-        out_shape += (jax.ShapeDtypeStruct((size, span), jnp.float32),) * 2
+        operands += [first, last, spread, *tables]
+        out_shape += (jax.ShapeDtypeStruct(first.shape, jnp.float32),) * 2
     else:
         out_shape += (jax.ShapeDtypeStruct((groups, LANES), jnp.float32),)
     return pl.pallas_call(
         functools.partial(state_kernel, len(pieces), groups, with_edges),
-        grid=(1,),
         out_shape=out_shape,
-        in_specs=in_specs,
+        in_specs=[whole] * len(operands),
         out_specs=(whole,) * len(out_shape),
         scratch_shapes=[pltpu.VMEM((groups * STRIDE + 7, LANES), jnp.float32),
                         pltpu.VMEM((GAS, groups, LANES), jnp.float32)],
-        compiler_params=pltpu.CompilerParams(vmem_limit_bytes=VMEM_LIMIT),
+        compiler_params=pltpu.CompilerParams(vmem_limit_bytes=SMALL_LIMIT),
         name="state",
     )(*operands)
 
 
-CELLS = 512
 WIDE = 256
 
 
@@ -336,21 +337,16 @@
     return jnp.concatenate(parts, axis=1)
 
 
-def relax_tiles(cells, spread_ref, tables, coef_ref, even_ref, flat_ref, store):
-    target_ref, factor_ref, wall_ref = tables
-    span = flat_ref.shape[1]
-
-    def block(b, carry):
-        start = pl.multiple_of(b * CELLS, CELLS)
-        coef = coef_ref[pl.ds(start, CELLS), :]
-        even_ref[...] = dot(coef, spread_ref[...])
-        for l in range(span // WIDE):
-            columns = slice(l * WIDE, (l + 1) * WIDE)
-            store(start, l, relaxed(coef, even_ref, flat_ref[pl.ds(start, CELLS), columns],
-                                    target_ref[:, columns], factor_ref[:, columns], wall_ref[:, columns]))
+def relax_block(spread_ref, tables, coef_ref, even_ref, flat_ref, store):
+    even_ref[...] = dot(coef_ref[...], spread_ref[...])
+
+    def lane(l, carry):
+        columns = pl.ds(pl.multiple_of(l * WIDE, WIDE), WIDE)
+        target, factor, wall = (ref[:, columns] for ref in tables)
+        store(l, relaxed(coef_ref[...], even_ref, flat_ref[:, columns], target, factor, wall))
         return carry
 
-    lax.fori_loop(0, cells // CELLS, block, 0)
+    lax.fori_loop(0, flat_ref.shape[1] // WIDE, lane, 0)
 
 
 PAD = 8
@@ -360,12 +356,12 @@
 def transport(exact, rows, field_ref, base, ncols, group, kind_ref, code_ref, sums_ref, stencil_ref,
               out_ref, parts_ref, strip_ref, half_ref):
     span = out_ref.shape[1]
-    nothing = jnp.minimum(pl.program_id(0), 0)
+    nothing = jnp.minimum(lax.axis_index("vel"), 0)
     shape = (ncols // 8, 8, LANES)
-    table = None
-    for l in range(span // WIDE):
+
+    def lanes(l, carry):
         for h in range(WIDE // LANES):
-            columns = slice(l * WIDE + h * LANES, l * WIDE + (h + 1) * LANES)
+            columns = pl.ds(pl.multiple_of(l * WIDE + h * LANES, LANES), LANES)
             x0, x1, x2, vx, y0, y1, y2, _ = (stencil_ref[8 * k:8 * k + 8, columns][None] for k in range(8))
             x_up = jnp.broadcast_to(vx > 0, shape)
             ahead = 1 if h == 0 else -1
@@ -395,10 +391,12 @@
                 half_ref[0, cut, columns] = upper
                 if exact:
                     half_ref[1, cut, columns] = (value - upper.astype(jnp.float32)).astype(jnp.bfloat16)
-        columns = slice(l * WIDE, (l + 1) * WIDE)
-        for k in range(1 + exact):
-            term = dot(half_ref[k, :, columns], sums_ref[columns, :])
-            table = term if table is None else table + term
+        return carry
+
+    lax.fori_loop(0, span // WIDE, lanes, 0)
+    table = dot(half_ref[0], sums_ref[...])
+    if exact:
+        table = table + dot(half_ref[1], sums_ref[...])
     for g in range(rows * ncols // LANES):
         total = table[g * LANES:(g + 1) * LANES, :].T
         kind = kind_ref[pl.ds(group + g, 1), :]
@@ -438,19 +436,20 @@
 
     @pl.when(i < blocks)
     def _():
-        base = edge + i * block
-
-        def store(start, l, values):
-            columns = slice(l * WIDE, (l + 1) * WIDE)
-            field_ref[pl.ds(pl.multiple_of(base + start, edge), values.shape[0]), columns] = values
+        here = pl.ds(pl.multiple_of(edge + i * block, edge), block)
 
         if relax:
-            relax_tiles(block, spread_ref, (target_ref, factor_ref, wall_ref), coef_ref, even_ref,
-                        flat_ref, store)
+            def store(l, values):
+                field_ref[here, pl.ds(pl.multiple_of(l * WIDE, WIDE), WIDE)] = values
+
+            relax_block(spread_ref, (target_ref, factor_ref, wall_ref), coef_ref, even_ref, flat_ref, store)
         else:
-            for l in range(span // WIDE):
-                for start in range(0, block, edge):
-                    store(start, l, turned(flat_ref[start:start + edge, l * WIDE:(l + 1) * WIDE], l, span))
+            def lane(l, carry):
+                columns = pl.ds(pl.multiple_of(l * WIDE, WIDE), WIDE)
+                field_ref[here, columns] = turned(flat_ref[:, columns], l, span)
+                return carry
+
+            lax.fori_loop(0, span // WIDE, lane, 0)
 
     @pl.when(i > 0)
     def _():
@@ -466,14 +465,15 @@
 
 
 def outer_kernel(relax, exact, ncols, count, flat_ref, given_ref, head_ref, tail_ref, low_ref, high_ref,
-                 kind_ref, code_ref, sums_ref, stencil_ref, out_ref, *refs):
+                 kind_ref, code_ref, sums_ref, stencil_ref, out_ref, first_ref, last_ref, *refs):
     slot_refs = refs[:count]
-    parts_ref, field_ref, strip_ref, half_ref = refs[count:]
-    i = pl.program_id(0)
+    parts_ref, field_ref, strip_ref, half_ref, done_ref = refs[count:]
     edge = END * ncols
     size = head_ref.shape[0]
-    span = out_ref.shape[1]
+    span = first_ref.shape[1]
     groups = parts_ref.shape[0] // ROWS
+    strip_ref[...] = jnp.zeros_like(strip_ref)
+    parts_ref[...] = given_ref[...]
 
     def halo(ref, start):
         for l in range(span // WIDE):
@@ -481,28 +481,24 @@
             values = ref[:, columns]
             field_ref[start:start + edge, columns] = values if relax else turned(values, l, span)
 
-    @pl.when(i == 0)
-    def _():
-        strip_ref[...] = jnp.zeros_like(strip_ref)
-        parts_ref[...] = given_ref[...]
-        halo(low_ref, 0)
-        field_ref[edge:, :] = head_ref[...]
-
-    @pl.when(i == 1)
-    def _():
-        field_ref[:size, :] = tail_ref[...]
-        halo(high_ref, size)
-
-    transport(exact, END, field_ref, 0, ncols, i * (groups - edge // LANES), kind_ref, code_ref,
-              sums_ref, stencil_ref, out_ref, parts_ref, strip_ref, half_ref)
-
-    @pl.when(i == 1)
-    def _():
-        me = lax.axis_index("vel")
-        rows = slot_refs[0].shape[0]
-        for away, ref in enumerate(slot_refs):
-            owner = lax.rem(me + away, count)
-            ref[...] = parts_ref[pl.ds(pl.multiple_of(owner * rows, 4), rows), :]
+    halo(low_ref, 0)
+    field_ref[edge:edge + size, :] = head_ref[...]
+    field_ref[edge + size:edge + 2 * size, :] = tail_ref[...]
+    halo(high_ref, edge + 2 * size)
+    copies = []
+    for k, (ref, base, group, start) in enumerate((
+            (first_ref, 0, 0, 0), (last_ref, edge + size, groups - edge // LANES, out_ref.shape[0] - edge))):
+        transport(exact, END, field_ref, base, ncols, group, kind_ref, code_ref,
+                  sums_ref, stencil_ref, ref, parts_ref, strip_ref, half_ref)
+        copies.append(pltpu.make_async_copy(ref, out_ref.at[pl.ds(start, edge), :], done_ref.at[k]))
+        copies[-1].start()
+    me = lax.axis_index("vel")
+    rows = slot_refs[0].shape[0]
+    for away, ref in enumerate(slot_refs):
+        owner = lax.rem(me + away, count)
+        ref[...] = parts_ref[pl.ds(pl.multiple_of(owner * rows, 4), rows), :]
+    for copy in copies:
+        copy.wait()
 
 
 def inner(relax, exact, flat, coef, kind, code, spread, tables, sums, stencil, ncols):
@@ -525,7 +521,7 @@
         in_specs=in_specs,
         out_specs=(pl.BlockSpec((block, span), lambda i: (jnp.maximum(i - 1, 0), 0)), whole, whole, whole),
         scratch_shapes=[pltpu.VMEM((cells + 2 * END * ncols, span), jnp.float32),
-                        pltpu.VMEM((CELLS, 2 * LANES), jnp.float32),
+                        pltpu.VMEM((block, 2 * LANES), jnp.float32),
                         pltpu.VMEM((WIDE // LANES * BLOCK, ncols + 2 * PAD, LANES), jnp.float32),
                         pltpu.VMEM((1 + exact, block, span), jnp.bfloat16)],
         compiler_params=pltpu.CompilerParams(vmem_limit_bytes=VMEM_LIMIT),
@@ -538,35 +534,34 @@
 def outer(relax, exact, flat, parts, head, tail, low, high, kind, code, sums, stencil, ncols):
     cells, span = flat.shape
     edge = END * ncols
-    last = cells // edge - 1
     count = lax.axis_size("vel")
     whole = pl.BlockSpec(memory_space=pltpu.VMEM)
     slot = jax.ShapeDtypeStruct((parts.shape[0] // count, LANES), jnp.float32)
-    flat, *slots = pl.pallas_call(
+    rim = jax.ShapeDtypeStruct((edge, span), jnp.float32)
+    flat, first, last, *slots = pl.pallas_call(
         functools.partial(outer_kernel, relax, exact, ncols, count),
-        grid=(2,),
-        out_shape=(jax.ShapeDtypeStruct((cells, span), jnp.float32),) + (slot,) * count,
+        out_shape=(jax.ShapeDtypeStruct((cells, span), jnp.float32), rim, rim) + (slot,) * count,
         in_specs=[pl.BlockSpec(memory_space=pl.ANY)] + [whole] * 9,
-        out_specs=(pl.BlockSpec((edge, span), lambda i: (i * last, 0)),) + (whole,) * count,
+        out_specs=(pl.BlockSpec(memory_space=pl.ANY),) + (whole,) * (count + 2),
         scratch_shapes=[pltpu.VMEM(parts.shape, jnp.float32),
-                        pltpu.VMEM((3 * edge, span), jnp.float32),
+                        pltpu.VMEM((6 * edge, span), jnp.float32),
                         pltpu.VMEM((WIDE // LANES * BLOCK, ncols + 2 * PAD, LANES), jnp.float32),
-                        pltpu.VMEM((1 + exact, edge, span), jnp.bfloat16)],
+                        pltpu.VMEM((1 + exact, edge, span), jnp.bfloat16),
+                        pltpu.SemaphoreType.DMA((2,))],
         input_output_aliases={0: 0},
-        compiler_params=pltpu.CompilerParams(vmem_limit_bytes=VMEM_LIMIT),
+        compiler_params=pltpu.CompilerParams(vmem_limit_bytes=SMALL_LIMIT),
         name="outer" if relax else "outer_first",
     )(flat, parts, head, tail, low, high, kind, code, sums, stencil)
-    return flat, slots
+    return flat, first, last, slots
 
 
 def last_kernel(flat_ref, coef_ref, spread_ref, target_ref, factor_ref, wall_ref, out_ref, even_ref):
     span = flat_ref.shape[1]
 
-    def store(start, l, values):
-        out_ref[pl.ds(start, CELLS), l * WIDE:(l + 1) * WIDE] = turned(values, l, span, back=True)
-
-    relax_tiles(flat_ref.shape[0], spread_ref, (target_ref, factor_ref, wall_ref), coef_ref, even_ref,
-                flat_ref, store)
+    def store(l, values):
+        out_ref[:, pl.ds(pl.multiple_of(l * WIDE, WIDE), WIDE)] = turned(values, l, span, back=True)
+
+    relax_block(spread_ref, (target_ref, factor_ref, wall_ref), coef_ref, even_ref, flat_ref, store)
 
 
 def finish(flat, coef, spread, tables, ncols):
@@ -581,7 +576,7 @@
                   pl.BlockSpec((block, COEF), lambda i: (i, 0)),
                   whole, whole, whole, whole],
         out_specs=pl.BlockSpec((block, span), lambda i: (i, 0)),
-        scratch_shapes=[pltpu.VMEM((CELLS, 2 * LANES), jnp.float32)],
+        scratch_shapes=[pltpu.VMEM((block, 2 * LANES), jnp.float32)],
         compiler_params=pltpu.CompilerParams(vmem_limit_bytes=VMEM_LIMIT),
         name="finish",
     )(flat, coef, spread, *tables)
@@ -603,12 +598,8 @@
 def shards(dist, cell_kind, normal_code, wall_temp):
     nrows, ncols, span = dist.shape
     cells = nrows * ncols
-    groups = cells // LANES
-    kind = cell_kind.reshape(groups, LANES)
-    code = normal_code.reshape(groups, LANES)
-    temp = wall_temp.reshape(groups, LANES)
     flat = dist.reshape(cells, span)
-    target, factor, wall, sums, stencil, spread = setup(span)
+    kind, code, temp, target, factor, wall, sums, stencil, spread = setup(span, cell_kind, normal_code, wall_temp)
     tables = (target, factor, wall)
     edge = 2 * ncols
     coef = None
@@ -617,9 +608,9 @@
         final = step == STEPS - 1
         low, high = exchange(low, high)
         flat, parts, head, tail = inner(step > 0, final, flat, coef, kind, code, spread, tables, sums, stencil, ncols)
-        flat, slots = outer(step > 0, final, flat, parts, head, tail, low, high, kind, code, sums, stencil, ncols)
+        flat, first, last, slots = outer(step > 0, final, flat, parts, head, tail, low, high, kind, code, sums, stencil, ncols)
         own = gas(swap(slots), kind, code, temp)
-        coef, *others = state(not final, swap([own] * len(slots)), kind, code, temp, flat, spread, tables, ncols)
+        coef, *others = state(not final, swap([own] * len(slots)), kind, code, temp, first, last, spread, tables)
         if not final:
             low, high = others
     flux = others[0]

time: 272 us -> 327 us (1.20)
  local copies, waits for them, and re-layouts: 15.3 us -> 61.9 us
  Pallas kernels: 168 us -> 176 us
    unnamed x67 -> x105, local copies, waits for them, and re-layouts: 9.63 us -> 59.5 us
    pallas_call x4, Pallas kernels: 109 us -> 134 us  [inner(): pl.pallas_call(functools.partial(inner_kernel, relax, exact, blocks, ncol...]
    pallas_call x4, Pallas kernels: 19.4 us -> 8.8 us  [outer(): pl.pallas_call(functools.partial(outer_kernel, relax, exact, ncols, count...]
    pallas_call x4, Pallas kernels: 14.5 us -> 4.88 us  [state(): pl.pallas_call(functools.partial(state_kernel, len(pieces), groups, with_...]
    reshape x3 -> x0, local copies, waits for them, and re-layouts: 3.52 us -> none  [the longest x1 1.43 us: shards(): kind = cell_kind.reshape(groups, LANES)]
  transfers between devices with their start and end apart: 32 -> 32, of which waited for: 24 -> 24; matrix products, arithmetic and copies ran while one was open for 1% -> 0% of each run, Pallas kernels for 41% -> 42%
where the time goes in v4:
time: 327 us; the launch traced here: 326 us
  Pallas kernels  176 us (54%)
  local copies, waits for them, and re-layouts  61.9 us (19%)
  starting transfers between devices  58.3 us (18%)
  waiting for transfers between devices  28.6 us (9%)
    pallas_call x4, Pallas kernels, inner(): pl.pallas_call(functools.partial(inner_kernel, relax, exact, blocks, ncol...  134 us
    unnamed x105, local copies, waits for them, and re-layouts  59.5 us
    ppermute x24, starting transfers between devices, swap(): lax.ppermute(slots[k], 'vel', [(i, (i + k) % count) for i in range(count)])  32.5 us
    ppermute x24, waiting for transfers between devices, swap(): lax.ppermute(slots[k], 'vel', [(i, (i + k) % count) for i in range(count)])  28.6 us
    ppermute x8, starting transfers between devices, exchange(): return (lax.ppermute(last, 'space', up), lax.ppermute(first, 'space', down))  25.8 us
    pallas_call x1, Pallas kernels, finish(): pl.pallas_call(last_kernel, grid=(cells // block,), out_shape=jax.ShapeDt...  19.9 us
    pallas_call x4, Pallas kernels, outer(): pl.pallas_call(functools.partial(outer_kernel, relax, exact, ncols, count...  8.8 us
  transfers between devices with their start and end apart: 32, of which 24 were waited for; matrix products, arithmetic and copies ran while one was open for 0% of the time, Pallas kernels for 42%

profile of v4, /device:TPU:4, one launch (start us, length us, event | category | flops | bytes accessed | tf_op | source)
XLA Modules:
  0.0 326.0 jit_solution(17442126322953427059)
XLA Ops:
  0.6 2.3 fusion
  2.9 1.9 collective-permute-start
  4.8 4.5 %collective-permute-start.1 = (f32[128,1024]{1,0:T(8,128)}, f32[128,1024]{1,0:T(8,128)S(1)}, u32[]{:S(2)}, u32[]{:S(2)}) collective-permute-start(f32[128,1024]{1,0:T(8,128)} %bitcast.2), channel_id=1, source_target_pairs={{4,0},{8,4},{12,8},{16,12},{20,16},{24,20},{28,24},{5,1},{9,5},{13... | collective-permute-start | bytes 1572872 | tf_op jit(solution)/shard_map/ppermute | solution.py:589
  9.4 1.9 setup.1
  11.3 0.9 copy-done.8
  12.3 0.9 copy-done.10
  14.7 27.4 %inner_first.1 = (f32[4096,1024]{1,0:T(8,128)}, f32[448,128]{1,0:T(8,128)S(1)}, f32[256,1024]{1,0:T(8,128)S(1)}, f32[256,1024]{1,0:T(8,128)S(1)}) custom-call(f32[4096,1024]{1,0:T(8,128)} %bitcast.4, s32[32,128]{1,0:T(8,128)S(1)} %copy-done.15, s32[32,128]{1,0:T(8,128)S(1)} %copy-done.21, bf16[1024,128]{1,0:T(8,128)(2,1)S(1)} %copy-done.8, ...), custom_call_target="tpu_custom_call" | custom-call | flops 3221225472 | bytes 33554432 | tf_op jit(solution)/shard_map/inner_first/pallas_call | solution.py:516
  42.2 5.8 %copy-done.6 = f32[4096,1024]{1,0:T(8,128)S(1)} copy-done((f32[4096,1024]{1,0:T(8,128)S(1)}, f32[4096,1024]{1,0:T(8,128)}, u32[]{:S(2)}) %copy-start.6) | copy-done | bytes 16777240
  48.0 2.0 outer_first.1
  50.0 6.2 %copy-done.7 = f32[4096,1024]{1,0:T(8,128)} copy-done((f32[4096,1024]{1,0:T(8,128)}, f32[4096,1024]{1,0:T(8,128)S(1)}, u32[]{:S(2)}) %copy-start.7) | copy-done | bytes 16777240
  56.8 1.6 collective-permute-start.2
  58.4 2.6 collective-permute-start.3
  61.0 1.3 collective-permute-start.4
  62.3 1.0 collective-permute-done.2.refs_1_
  63.3 1.4 collective-permute-done.3.refs_2_
  65.8 1.6 gas.4.refs_0_
  68.0 3.0 collective-permute-start.6
  71.2 2.3 collective-permute-done.5.refs_1_
  74.1 1.1 collective-permute-done.7.refs_3_
  76.1 1.4 state.4
  77.5 1.9 collective-permute-start.8
  79.4 4.5 %collective-permute-start.9 = (f32[128,1024]{1,0:T(8,128)S(1)}, f32[128,1024]{1,0:T(8,128)S(1)}, u32[]{:S(2)}, u32[]{:S(2)}) collective-permute-start(f32[128,1024]{1,0:T(8,128)S(1)} %get-tuple-element.90), channel_id=1, source_target_pairs={{4,0},{8,4},{12,8},{16,12},{20,16},{24,20},{28,24},{5,1},{9,5},{13... | collective-permute-start | bytes 1572872 | tf_op jit(solution)/shard_map/ppermute | solution.py:589
  84.0 33.7 %inner.3 = (f32[4096,1024]{1,0:T(8,128)}, f32[448,128]{1,0:T(8,128)S(1)}, f32[256,1024]{1,0:T(8,128)S(1)}, f32[256,1024]{1,0:T(8,128)S(1)}) custom-call(f32[4096,1024]{1,0:T(8,128)} %copy-done.7, s32[32,128]{1,0:T(8,128)S(1)} %copy-done.17, s32[32,128]{1,0:T(8,128)S(1)} %copy-done.23, bf16[1024,128]{1,0:T(8,128)(2,1)S(1)} %copy-done.9, ...), custom_call_target="tpu_custom_call" | custom-call | flops 3221225472 | bytes 33554432 | tf_op jit(solution)/shard_map/inner/pallas_call | solution.py:516
  117.7 5.8 %copy-done.2 = f32[4096,1024]{1,0:T(8,128)S(1)} copy-done((f32[4096,1024]{1,0:T(8,128)S(1)}, f32[4096,1024]{1,0:T(8,128)}, u32[]{:S(2)}) %copy-start.2) | copy-done | bytes 16777240
  123.4 1.8 outer.3
  125.3 6.2 %copy-done.3 = f32[4096,1024]{1,0:T(8,128)} copy-done((f32[4096,1024]{1,0:T(8,128)}, f32[4096,1024]{1,0:T(8,128)S(1)}, u32[]{:S(2)}) %copy-start.3) | copy-done | bytes 16777240
  132.8 2.0 collective-permute-start.11
  134.9 1.0 collective-permute-start.12
  135.9 2.2 collective-permute-done.10.refs_1_
  138.1 1.1 collective-permute-done.11.refs_2_
  140.0 1.6 gas.5.refs_0_
  141.6 1.2 collective-permute-start.13
  142.8 2.0 collective-permute-start.14
  145.5 2.2 collective-permute-done.13.refs_1_
  149.9 1.4 state.5
  151.3 1.9 collective-permute-start.16
  153.2 4.5 %collective-permute-start.17 = (f32[128,1024]{1,0:T(8,128)S(1)}, f32[128,1024]{1,0:T(8,128)S(1)}, u32[]{:S(2)}, u32[]{:S(2)}) collective-permute-start(f32[128,1024]{1,0:T(8,128)S(1)} %get-tuple-element.104), channel_id=1, source_target_pairs={{4,0},{8,4},{12,8},{16,12},{20,16},{24,20},{28,24},{5,1},{9,5},{13... | collective-permute-start | bytes 1572872 | tf_op jit(solution)/shard_map/ppermute | solution.py:589
  157.8 33.7 %inner.4 = (f32[4096,1024]{1,0:T(8,128)}, f32[448,128]{1,0:T(8,128)S(1)}, f32[256,1024]{1,0:T(8,128)S(1)}, f32[256,1024]{1,0:T(8,128)S(1)}) custom-call(f32[4096,1024]{1,0:T(8,128)} %copy-done.3, s32[32,128]{1,0:T(8,128)S(1)} %copy-done.18, s32[32,128]{1,0:T(8,128)S(1)} %copy-done.24, bf16[1024,128]{1,0:T(8,128)(2,1)S(1)} %copy-done.9, ...), custom_call_target="tpu_custom_call" | custom-call | flops 3221225472 | bytes 33554432 | tf_op jit(solution)/shard_map/inner/pallas_call | solution.py:516
  191.5 5.8 %copy-done.4 = f32[4096,1024]{1,0:T(8,128)S(1)} copy-done((f32[4096,1024]{1,0:T(8,128)S(1)}, f32[4096,1024]{1,0:T(8,128)}, u32[]{:S(2)}) %copy-start.4) | copy-done | bytes 16777240
  197.2 1.8 outer.4
  199.1 6.2 %copy-done.5 = f32[4096,1024]{1,0:T(8,128)} copy-done((f32[4096,1024]{1,0:T(8,128)}, f32[4096,1024]{1,0:T(8,128)S(1)}, u32[]{:S(2)}) %copy-start.5) | copy-done | bytes 16777240
  205.8 1.1 collective-permute-start.18
  207.0 1.8 collective-permute-start.19
  208.8 1.0 collective-permute-start.20
  209.8 2.1 collective-permute-done.18.refs_1_
  211.9 1.3 collective-permute-done.19.refs_2_
  214.1 1.6 gas.6.refs_0_
  216.6 2.2 collective-permute-start.22
  219.6 2.2 collective-permute-done.21.refs_1_
  223.9 1.4 state.6
  225.2 1.9 collective-permute-start.24
  227.2 4.5 %collective-permute-start.25 = (f32[128,1024]{1,0:T(8,128)S(1)}, f32[128,1024]{1,0:T(8,128)S(1)}, u32[]{:S(2)}, u32[]{:S(2)}) collective-permute-start(f32[128,1024]{1,0:T(8,128)S(1)} %get-tuple-element.118), channel_id=1, source_target_pairs={{4,0},{8,4},{12,8},{16,12},{20,16},{24,20},{28,24},{5,1},{9,5},{13... | collective-permute-start | bytes 1572872 | tf_op jit(solution)/shard_map/ppermute | solution.py:589
  231.7 39.3 %inner.5 = (f32[4096,1024]{1,0:T(8,128)}, f32[448,128]{1,0:T(8,128)S(1)}, f32[256,1024]{1,0:T(8,128)S(1)}, f32[256,1024]{1,0:T(8,128)S(1)}) custom-call(f32[4096,1024]{1,0:T(8,128)} %copy-done.5, s32[32,128]{1,0:T(8,128)S(1)} %copy-done.19, s32[32,128]{1,0:T(8,128)S(1)} %copy-done.25, bf16[1024,128]{1,0:T(8,128)(2,1)S(1)} %copy-done.9, ...), custom_call_target="tpu_custom_call" | custom-call | flops 3221225472 | bytes 33554432 | tf_op jit(solution)/shard_map/inner/pallas_call | solution.py:516
  271.0 5.8 %copy-done = f32[4096,1024]{1,0:T(8,128)S(1)} copy-done((f32[4096,1024]{1,0:T(8,128)S(1)}, f32[4096,1024]{1,0:T(8,128)}, u32[]{:S(2)}) %copy-start) | copy-done | bytes 16777240
  276.8 3.1 outer.5
  280.0 5.8 %copy-done.1 = f32[4096,1024]{1,0:T(8,128)} copy-done((f32[4096,1024]{1,0:T(8,128)}, f32[4096,1024]{1,0:T(8,128)S(1)}, u32[]{:S(2)}) %copy-start.1) | copy-done | bytes 16777240
  286.4 1.3 collective-permute-start.26
  287.7 1.8 collective-permute-start.27
  290.3 2.1 collective-permute-done.26.refs_1_
  292.4 1.3 collective-permute-done.27.refs_2_
  294.8 1.6 gas.7.refs_0_
  297.2 2.2 collective-permute-start.30
  300.2 2.3 collective-permute-done.29.refs_1_
  306.0 19.9 %finish.1 = f32[4096,1024]{1,0:T(8,128)} custom-call(f32[4096,1024]{1,0:T(8,128)} %copy-done.1, bf16[4096,64]{1,0:T(8,128)(2,1)S(1)} %get-tuple-element.124.coef_ref, bf16[64,256]{1,0:T(8,128)(2,1)S(1)} %copy-done.27, bf16[64,1024]{1,0:T(8,128)(2,1)S(1)} %copy-done.12, bf16[64,1024]{1,0:T(8,128)(2,1)S(1)} %copy-done.13, bf16[64,1024]{1,0:T(8,128)(2,1)S(1)} %copy-done.14), custom_call_target="tpu_custom_call" | custom-call | tf_op jit(solution)/shard_map/finish/pallas_call | solution.py:571
  (126 shorter events, 23.4 us)
Async XLA Ops:
  2.9 39.2 %collective-permute-start = (f32[128,1024]{1,0:T(8,128)}, f32[128,1024]{1,0:T(8,128)S(1)}, u32[]{:S(2)}, u32[]{:S(2)}) collective-permute-start(f32[128,1024]{1,0:T(8,128)} %bitcast.1), channel_id=1, source_target_pairs={{0,4},{4,8},{8,12},{12,16},{16,20},{20,24},{24,28},{1,5},{5,9},{9,... | collective-permute-start | bytes 1572872 | tf_op jit(solution)/shard_map/ppermute | solution.py:589
  4.8 37.3 %collective-permute-start.1 = (f32[128,1024]{1,0:T(8,128)}, f32[128,1024]{1,0:T(8,128)S(1)}, u32[]{:S(2)}, u32[]{:S(2)}) collective-permute-start(f32[128,1024]{1,0:T(8,128)} %bitcast.2), channel_id=1, source_target_pairs={{4,0},{8,4},{12,8},{16,12},{20,16},{24,20},{28,24},{5,1},{9,5},{13... | collective-permute-start | bytes 1572872 | tf_op jit(solution)/shard_map/ppermute | solution.py:589
  14.7 27.5 %copy-start.9 = (bf16[1024,128]{1,0:T(8,128)(2,1)S(1)}, bf16[1024,128]{1,0:T(8,128)(2,1)}, u32[]{:S(2)}) copy-start(bf16[1024,128]{1,0:T(8,128)(2,1)} %get-tuple-element.66.sums_ref) | copy-start | bytes 786436
  14.7 27.5 %copy-start.11 = (f32[64,1024]{1,0:T(8,128)S(1)}, f32[64,1024]{1,0:T(8,128)}, u32[]{:S(2)}) copy-start(f32[64,1024]{1,0:T(8,128)} %get-tuple-element.67.stencil_ref) | copy-start | bytes 786436
  14.7 27.5 %copy-start.16 = (s32[32,128]{1,0:T(8,128)S(1)}, s32[32,128]{1,0:T(8,128)}, u32[]{:S(2)}) copy-start(s32[32,128]{1,0:T(8,128)} %get-tuple-element.64.kind_ref.refs_4_) | copy-start | bytes 49156
  14.7 27.5 %copy-start.22 = (s32[32,128]{1,0:T(8,128)S(1)}, s32[32,128]{1,0:T(8,128)}, u32[]{:S(2)}) copy-start(s32[32,128]{1,0:T(8,128)} %get-tuple-element.65.code_ref.refs_5_) | copy-start | bytes 49156
  14.7 60.6 %copy-start.12 = (bf16[64,1024]{1,0:T(8,128)(2,1)S(1)}, bf16[64,1024]{1,0:T(8,128)(2,1)}, u32[]{:S(2)}) copy-start(bf16[64,1024]{1,0:T(8,128)(2,1)} %get-tuple-element.81.refs_10_.refs_2_.target_ref) | copy-start | bytes 393220
  14.7 60.6 %copy-start.13 = (bf16[64,1024]{1,0:T(8,128)(2,1)S(1)}, bf16[64,1024]{1,0:T(8,128)(2,1)}, u32[]{:S(2)}) copy-start(bf16[64,1024]{1,0:T(8,128)(2,1)} %get-tuple-element.82.refs_11_.refs_3_.factor_ref) | copy-start | bytes 393220
  14.7 60.6 %copy-start.14 = (bf16[64,1024]{1,0:T(8,128)(2,1)S(1)}, bf16[64,1024]{1,0:T(8,128)(2,1)}, u32[]{:S(2)}) copy-start(bf16[64,1024]{1,0:T(8,128)(2,1)} %get-tuple-element.83.refs_12_.refs_4_.wall_ref) | copy-start | bytes 393220
  14.7 60.6 %copy-start.17 = (s32[32,128]{1,0:T(8,128)S(1)}, s32[32,128]{1,0:T(8,128)}, u32[]{:S(2)}) copy-start(s32[32,128]{1,0:T(8,128)} %get-tuple-element.64.kind_ref.refs_4_) | copy-start | bytes 49156
  14.7 60.6 %copy-start.23 = (s32[32,128]{1,0:T(8,128)S(1)}, s32[32,128]{1,0:T(8,128)}, u32[]{:S(2)}) copy-start(s32[32,128]{1,0:T(8,128)} %get-tuple-element.65.code_ref.refs_5_) | copy-start | bytes 49156
  14.7 60.6 %copy-start.27 = (bf16[64,256]{1,0:T(8,128)(2,1)S(1)}, bf16[64,256]{1,0:T(8,128)(2,1)}, u32[]{:S(2)}) copy-start(bf16[64,256]{1,0:T(8,128)(2,1)} %get-tuple-element.80.refs_9_.refs_1_.spread_ref) | copy-start | bytes 98308
  14.7 60.6 %copy-start.28 = (f32[32,128]{1,0:T(8,128)S(1)}, f32[32,128]{1,0:T(8,128)}, u32[]{:S(2)}) copy-start(f32[32,128]{1,0:T(8,128)} %get-tuple-element.77.refs_6_) | copy-start | bytes 49156
  42.2 5.8 %copy-start.6 = (f32[4096,1024]{1,0:T(8,128)S(1)}, f32[4096,1024]{1,0:T(8,128)}, u32[]{:S(2)}) copy-start(f32[4096,1024]{1,0:T(8,128)} %get-tuple-element.68.flat_ref) | copy-start | bytes 50331652
  50.0 6.2 %copy-start.7 = (f32[4096,1024]{1,0:T(8,128)}, f32[4096,1024]{1,0:T(8,128)S(1)}, u32[]{:S(2)}) copy-start(f32[4096,1024]{1,0:T(8,128)S(1)} %get-tuple-element.72.flat_ref) | copy-start | bytes 50331652
  56.8 6.5 %collective-permute-start.2 = (f32[112,128]{1,0:T(8,128)S(1)}, f32[112,128]{1,0:T(8,128)S(1)}, u32[]{:S(2)}, u32[]{:S(2)}) collective-permute-start(f32[112,128]{1,0:T(8,128)S(1)} %get-tuple-element.74), channel_id=1, source_target_pairs={{0,1},{1,2},{2,3},{3,0},{4,5},{5,6},{6,7},{7,4},{8,9},{9,10},{10,1... | collective-permute-start | bytes 172040 | tf_op jit(solution)/shard_map/ppermute | solution.py:594
  58.4 6.4 %collective-permute-start.3 = (f32[112,128]{1,0:T(8,128)S(1)}, f32[112,128]{1,0:T(8,128)S(1)}, u32[]{:S(2)}, u32[]{:S(2)}) collective-permute-start(f32[112,128]{1,0:T(8,128)S(1)} %get-tuple-element.75), channel_id=1, source_target_pairs={{0,2},{1,3},{2,0},{3,1},{4,6},{5,7},{6,4},{7,5},{8,10},{9,11},{10,... | collective-permute-start | bytes 172040 | tf_op jit(solution)/shard_map/ppermute | solution.py:594
  61.0 4.3 %collective-permute-start.4 = (f32[112,128]{1,0:T(8,128)S(1)}, f32[112,128]{1,0:T(8,128)S(1)}, u32[]{:S(2)}, u32[]{:S(2)}) collective-permute-start(f32[112,128]{1,0:T(8,128)S(1)} %get-tuple-element.76), channel_id=1, source_target_pairs={{0,3},{1,0},{2,1},{3,2},{4,7},{5,4},{6,5},{7,6},{8,11},{9,8},{10,9... | collective-permute-start | bytes 172040 | tf_op jit(solution)/shard_map/ppermute | solution.py:594
  63.3 1.9 copy-start.40
  67.4 6.1 %collective-permute-start.5 = (f32[80,128]{1,0:T(8,128)}, f32[80,128]{1,0:T(8,128)S(1)}, u32[]{:S(2)}, u32[]{:S(2)}) collective-permute-start(f32[80,128]{1,0:T(8,128)} %gas.4.refs_0_), channel_id=1, source_target_pairs={{0,1},{1,2},{2,3},{3,0},{4,5},{5,6},{6,7},{7,4},{8,9},{9,10},{10,1... | collective-permute-start | bytes 122888 | tf_op jit(solution)/shard_map/ppermute | solution.py:594
  68.0 6.1 %collective-permute-start.6 = (f32[80,128]{1,0:T(8,128)}, f32[80,128]{1,0:T(8,128)S(1)}, u32[]{:S(2)}, u32[]{:S(2)}) collective-permute-start(f32[80,128]{1,0:T(8,128)} %gas.4.refs_0_), channel_id=1, source_target_pairs={{0,2},{1,3},{2,0},{3,1},{4,6},{5,7},{6,4},{7,5},{8,10},{9,11},{10,... | collective-permute-start | bytes 122888 | tf_op jit(solution)/shard_map/ppermute | solution.py:594
  71.0 4.2 %collective-permute-start.7 = (f32[80,128]{1,0:T(8,128)}, f32[80,128]{1,0:T(8,128)S(1)}, u32[]{:S(2)}, u32[]{:S(2)}) collective-permute-start(f32[80,128]{1,0:T(8,128)} %gas.4.refs_0_), channel_id=1, source_target_pairs={{0,3},{1,0},{2,1},{3,2},{4,7},{5,4},{6,5},{7,6},{8,11},{9,8},{10,9... | collective-permute-start | bytes 122888 | tf_op jit(solution)/shard_map/ppermute | solution.py:594
  77.5 40.2 %collective-permute-start.8 = (f32[128,1024]{1,0:T(8,128)S(1)}, f32[128,1024]{1,0:T(8,128)S(1)}, u32[]{:S(2)}, u32[]{:S(2)}) collective-permute-start(f32[128,1024]{1,0:T(8,128)S(1)} %get-tuple-element.89), channel_id=1, source_target_pairs={{0,4},{4,8},{8,12},{12,16},{16,20},{20,24},{24,28},{1,5},{5,9},{9,... | collective-permute-start | bytes 1572872 | tf_op jit(solution)/shard_map/ppermute | solution.py:589
  79.4 38.3 %collective-permute-start.9 = (f32[128,1024]{1,0:T(8,128)S(1)}, f32[128,1024]{1,0:T(8,128)S(1)}, u32[]{:S(2)}, u32[]{:S(2)}) collective-permute-start(f32[128,1024]{1,0:T(8,128)S(1)} %get-tuple-element.90), channel_id=1, source_target_pairs={{4,0},{8,4},{12,8},{16,12},{20,16},{24,20},{28,24},{5,1},{9,5},{13... | collective-permute-start | bytes 1572872 | tf_op jit(solution)/shard_map/ppermute | solution.py:589
  83.9 65.2 %copy-start.18 = (s32[32,128]{1,0:T(8,128)S(1)}, s32[32,128]{1,0:T(8,128)}, u32[]{:S(2)}) copy-start(s32[32,128]{1,0:T(8,128)} %get-tuple-element.64.kind_ref.refs_4_) | copy-start | bytes 49156
  84.0 65.1 %copy-start.24 = (s32[32,128]{1,0:T(8,128)S(1)}, s32[32,128]{1,0:T(8,128)}, u32[]{:S(2)}) copy-start(s32[32,128]{1,0:T(8,128)} %get-tuple-element.65.code_ref.refs_5_) | copy-start | bytes 49156
  84.0 65.1 %copy-start.29 = (f32[32,128]{1,0:T(8,128)S(1)}, f32[32,128]{1,0:T(8,128)}, u32[]{:S(2)}) copy-start(f32[32,128]{1,0:T(8,128)} %get-tuple-element.77.refs_6_) | copy-start | bytes 49156
  117.7 5.8 %copy-start.2 = (f32[4096,1024]{1,0:T(8,128)S(1)}, f32[4096,1024]{1,0:T(8,128)}, u32[]{:S(2)}) copy-start(f32[4096,1024]{1,0:T(8,128)} %get-tuple-element.85.flat_ref) | copy-start | bytes 50331652
  125.3 6.2 %copy-start.3 = (f32[4096,1024]{1,0:T(8,128)}, f32[4096,1024]{1,0:T(8,128)S(1)}, u32[]{:S(2)}) copy-start(f32[4096,1024]{1,0:T(8,128)S(1)} %get-tuple-element.91.flat_ref) | copy-start | bytes 50331652
  132.1 6.1 %collective-permute-start.10 = (f32[112,128]{1,0:T(8,128)S(1)}, f32[112,128]{1,0:T(8,128)S(1)}, u32[]{:S(2)}, u32[]{:S(2)}) collective-permute-start(f32[112,128]{1,0:T(8,128)S(1)} %get-tuple-element.93), channel_id=1, source_target_pairs={{0,1},{1,2},{2,3},{3,0},{4,5},{5,6},{6,7},{7,4},{8,9},{9,10},{10,1... | collective-permute-start | bytes 172040 | tf_op jit(solution)/shard_map/ppermute | solution.py:594
  132.8 6.4 %collective-permute-start.11 = (f32[112,128]{1,0:T(8,128)S(1)}, f32[112,128]{1,0:T(8,128)S(1)}, u32[]{:S(2)}, u32[]{:S(2)}) collective-permute-start(f32[112,128]{1,0:T(8,128)S(1)} %get-tuple-element.94), channel_id=1, source_target_pairs={{0,2},{1,3},{2,0},{3,1},{4,6},{5,7},{6,4},{7,5},{8,10},{9,11},{10,... | collective-permute-start | bytes 172040 | tf_op jit(solution)/shard_map/ppermute | solution.py:594
  134.9 4.6 %collective-permute-start.12 = (f32[112,128]{1,0:T(8,128)S(1)}, f32[112,128]{1,0:T(8,128)S(1)}, u32[]{:S(2)}, u32[]{:S(2)}) collective-permute-start(f32[112,128]{1,0:T(8,128)S(1)} %get-tuple-element.95), channel_id=1, source_target_pairs={{0,3},{1,0},{2,1},{3,2},{4,7},{5,4},{6,5},{7,6},{8,11},{9,8},{10,9... | collective-permute-start | bytes 172040 | tf_op jit(solution)/shard_map/ppermute | solution.py:594
  138.1 1.3 copy-start.41
  141.6 6.0 %collective-permute-start.13 = (f32[80,128]{1,0:T(8,128)}, f32[80,128]{1,0:T(8,128)S(1)}, u32[]{:S(2)}, u32[]{:S(2)}) collective-permute-start(f32[80,128]{1,0:T(8,128)} %gas.5.refs_0_), channel_id=1, source_target_pairs={{0,1},{1,2},{2,3},{3,0},{4,5},{5,6},{6,7},{7,4},{8,9},{9,10},{10,1... | collective-permute-start | bytes 122888 | tf_op jit(solution)/shard_map/ppermute | solution.py:594
  142.8 5.7 %collective-permute-start.14 = (f32[80,128]{1,0:T(8,128)}, f32[80,128]{1,0:T(8,128)S(1)}, u32[]{:S(2)}, u32[]{:S(2)}) collective-permute-start(f32[80,128]{1,0:T(8,128)} %gas.5.refs_0_), channel_id=1, source_target_pairs={{0,2},{1,3},{2,0},{3,1},{4,6},{5,7},{6,4},{7,5},{8,10},{9,11},{10,... | collective-permute-start | bytes 122888 | tf_op jit(solution)/shard_map/ppermute | solution.py:594
  144.9 4.2 %collective-permute-start.15 = (f32[80,128]{1,0:T(8,128)}, f32[80,128]{1,0:T(8,128)S(1)}, u32[]{:S(2)}, u32[]{:S(2)}) collective-permute-start(f32[80,128]{1,0:T(8,128)} %gas.5.refs_0_), channel_id=1, source_target_pairs={{0,3},{1,0},{2,1},{3,2},{4,7},{5,4},{6,5},{7,6},{8,11},{9,8},{10,9... | collective-permute-start | bytes 122888 | tf_op jit(solution)/shard_map/ppermute | solution.py:594
  151.3 40.2 %collective-permute-start.16 = (f32[128,1024]{1,0:T(8,128)S(1)}, f32[128,1024]{1,0:T(8,128)S(1)}, u32[]{:S(2)}, u32[]{:S(2)}) collective-permute-start(f32[128,1024]{1,0:T(8,128)S(1)} %get-tuple-element.103), channel_id=1, source_target_pairs={{0,4},{4,8},{8,12},{12,16},{16,20},{20,24},{24,28},{1,5},{5,9},{9,... | collective-permute-start | bytes 1572872 | tf_op jit(solution)/shard_map/ppermute | solution.py:589
  153.2 38.3 %collective-permute-start.17 = (f32[128,1024]{1,0:T(8,128)S(1)}, f32[128,1024]{1,0:T(8,128)S(1)}, u32[]{:S(2)}, u32[]{:S(2)}) collective-permute-start(f32[128,1024]{1,0:T(8,128)S(1)} %get-tuple-element.104), channel_id=1, source_target_pairs={{4,0},{8,4},{12,8},{16,12},{20,16},{24,20},{28,24},{5,1},{9,5},{13... | collective-permute-start | bytes 1572872 | tf_op jit(solution)/shard_map/ppermute | solution.py:589
  157.7 65.3 %copy-start.19 = (s32[32,128]{1,0:T(8,128)S(1)}, s32[32,128]{1,0:T(8,128)}, u32[]{:S(2)}) copy-start(s32[32,128]{1,0:T(8,128)} %get-tuple-element.64.kind_ref.refs_4_) | copy-start | bytes 49156
  157.7 65.3 %copy-start.25 = (s32[32,128]{1,0:T(8,128)S(1)}, s32[32,128]{1,0:T(8,128)}, u32[]{:S(2)}) copy-start(s32[32,128]{1,0:T(8,128)} %get-tuple-element.65.code_ref.refs_5_) | copy-start | bytes 49156
  157.8 65.3 %copy-start.30 = (f32[32,128]{1,0:T(8,128)S(1)}, f32[32,128]{1,0:T(8,128)}, u32[]{:S(2)}) copy-start(f32[32,128]{1,0:T(8,128)} %get-tuple-element.77.refs_6_) | copy-start | bytes 49156
  191.5 5.8 %copy-start.4 = (f32[4096,1024]{1,0:T(8,128)S(1)}, f32[4096,1024]{1,0:T(8,128)}, u32[]{:S(2)}) copy-start(f32[4096,1024]{1,0:T(8,128)} %get-tuple-element.99.flat_ref) | copy-start | bytes 50331652
  199.1 6.2 %copy-start.5 = (f32[4096,1024]{1,0:T(8,128)}, f32[4096,1024]{1,0:T(8,128)S(1)}, u32[]{:S(2)}) copy-start(f32[4096,1024]{1,0:T(8,128)S(1)} %get-tuple-element.105.flat_ref) | copy-start | bytes 50331652
  205.8 6.0 %collective-permute-start.18 = (f32[112,128]{1,0:T(8,128)S(1)}, f32[112,128]{1,0:T(8,128)S(1)}, u32[]{:S(2)}, u32[]{:S(2)}) collective-permute-start(f32[112,128]{1,0:T(8,128)S(1)} %get-tuple-element.107), channel_id=1, source_target_pairs={{0,1},{1,2},{2,3},{3,0},{4,5},{5,6},{6,7},{7,4},{8,9},{9,10},{10,1... | collective-permute-start | bytes 172040 | tf_op jit(solution)/shard_map/ppermute | solution.py:594
  207.0 6.2 %collective-permute-start.19 = (f32[112,128]{1,0:T(8,128)S(1)}, f32[112,128]{1,0:T(8,128)S(1)}, u32[]{:S(2)}, u32[]{:S(2)}) collective-permute-start(f32[112,128]{1,0:T(8,128)S(1)} %get-tuple-element.108), channel_id=1, source_target_pairs={{0,2},{1,3},{2,0},{3,1},{4,6},{5,7},{6,4},{7,5},{8,10},{9,11},{10,... | collective-permute-start | bytes 172040 | tf_op jit(solution)/shard_map/ppermute | solution.py:594
  208.8 4.7 %collective-permute-start.20 = (f32[112,128]{1,0:T(8,128)S(1)}, f32[112,128]{1,0:T(8,128)S(1)}, u32[]{:S(2)}, u32[]{:S(2)}) collective-permute-start(f32[112,128]{1,0:T(8,128)S(1)} %get-tuple-element.109), channel_id=1, source_target_pairs={{0,3},{1,0},{2,1},{3,2},{4,7},{5,4},{6,5},{7,6},{8,11},{9,8},{10,9... | collective-permute-start | bytes 172040 | tf_op jit(solution)/shard_map/ppermute | solution.py:594
  211.9 1.7 copy-start.42
  215.7 6.1 %collective-permute-start.21 = (f32[80,128]{1,0:T(8,128)}, f32[80,128]{1,0:T(8,128)S(1)}, u32[]{:S(2)}, u32[]{:S(2)}) collective-permute-start(f32[80,128]{1,0:T(8,128)} %gas.6.refs_0_), channel_id=1, source_target_pairs={{0,1},{1,2},{2,3},{3,0},{4,5},{5,6},{6,7},{7,4},{8,9},{9,10},{10,1... | collective-permute-start | bytes 122888 | tf_op jit(solution)/shard_map/ppermute | solution.py:594
  216.6 6.0 %collective-permute-start.22 = (f32[80,128]{1,0:T(8,128)}, f32[80,128]{1,0:T(8,128)S(1)}, u32[]{:S(2)}, u32[]{:S(2)}) collective-permute-start(f32[80,128]{1,0:T(8,128)} %gas.6.refs_0_), channel_id=1, source_target_pairs={{0,2},{1,3},{2,0},{3,1},{4,6},{5,7},{6,4},{7,5},{8,10},{9,11},{10,... | collective-permute-start | bytes 122888 | tf_op jit(solution)/shard_map/ppermute | solution.py:594
  218.8 4.3 %collective-permute-start.23 = (f32[80,128]{1,0:T(8,128)}, f32[80,128]{1,0:T(8,128)S(1)}, u32[]{:S(2)}, u32[]{:S(2)}) collective-permute-start(f32[80,128]{1,0:T(8,128)} %gas.6.refs_0_), channel_id=1, source_target_pairs={{0,3},{1,0},{2,1},{3,2},{4,7},{5,4},{6,5},{7,6},{8,11},{9,8},{10,9... | collective-permute-start | bytes 122888 | tf_op jit(solution)/shard_map/ppermute | solution.py:594
  225.2 45.8 %collective-permute-start.24 = (f32[128,1024]{1,0:T(8,128)S(1)}, f32[128,1024]{1,0:T(8,128)S(1)}, u32[]{:S(2)}, u32[]{:S(2)}) collective-permute-start(f32[128,1024]{1,0:T(8,128)S(1)} %get-tuple-element.117), channel_id=1, source_target_pairs={{0,4},{4,8},{8,12},{12,16},{16,20},{20,24},{24,28},{1,5},{5,9},{9,... | collective-permute-start | bytes 1572872 | tf_op jit(solution)/shard_map/ppermute | solution.py:589
  227.2 43.9 %collective-permute-start.25 = (f32[128,1024]{1,0:T(8,128)S(1)}, f32[128,1024]{1,0:T(8,128)S(1)}, u32[]{:S(2)}, u32[]{:S(2)}) collective-permute-start(f32[128,1024]{1,0:T(8,128)S(1)} %get-tuple-element.118), channel_id=1, source_target_pairs={{4,0},{8,4},{12,8},{16,12},{20,16},{24,20},{28,24},{5,1},{9,5},{13... | collective-permute-start | bytes 1572872 | tf_op jit(solution)/shard_map/ppermute | solution.py:589
  231.7 71.9 %copy-start.20 = (s32[32,128]{1,0:T(8,128)S(1)}, s32[32,128]{1,0:T(8,128)}, u32[]{:S(2)}) copy-start(s32[32,128]{1,0:T(8,128)} %get-tuple-element.64.kind_ref.refs_4_) | copy-start | bytes 49156
  231.7 71.9 %copy-start.26 = (s32[32,128]{1,0:T(8,128)S(1)}, s32[32,128]{1,0:T(8,128)}, u32[]{:S(2)}) copy-start(s32[32,128]{1,0:T(8,128)} %get-tuple-element.65.code_ref.refs_5_) | copy-start | bytes 49156
  231.7 71.9 %copy-start.31 = (f32[32,128]{1,0:T(8,128)S(1)}, f32[32,128]{1,0:T(8,128)}, u32[]{:S(2)}) copy-start(f32[32,128]{1,0:T(8,128)} %get-tuple-element.77.refs_6_) | copy-start | bytes 49156
  271.0 5.8 %copy-start = (f32[4096,1024]{1,0:T(8,128)S(1)}, f32[4096,1024]{1,0:T(8,128)}, u32[]{:S(2)}) copy-start(f32[4096,1024]{1,0:T(8,128)} %get-tuple-element.113.flat_ref) | copy-start | bytes 50331652
  280.0 5.8 %copy-start.1 = (f32[4096,1024]{1,0:T(8,128)}, f32[4096,1024]{1,0:T(8,128)S(1)}, u32[]{:S(2)}) copy-start(f32[4096,1024]{1,0:T(8,128)S(1)} %get-tuple-element.119.flat_ref) | copy-start | bytes 50331652
  286.4 6.0 %collective-permute-start.26 = (f32[112,128]{1,0:T(8,128)S(1)}, f32[112,128]{1,0:T(8,128)S(1)}, u32[]{:S(2)}, u32[]{:S(2)}) collective-permute-start(f32[112,128]{1,0:T(8,128)S(1)} %get-tuple-element.121), channel_id=1, source_target_pairs={{0,1},{1,2},{2,3},{3,0},{4,5},{5,6},{6,7},{7,4},{8,9},{9,10},{10,1... | collective-permute-start | bytes 172040 | tf_op jit(solution)/shard_map/ppermute | solution.py:594
  287.7 6.0 %collective-permute-start.27 = (f32[112,128]{1,0:T(8,128)S(1)}, f32[112,128]{1,0:T(8,128)S(1)}, u32[]{:S(2)}, u32[]{:S(2)}) collective-permute-start(f32[112,128]{1,0:T(8,128)S(1)} %get-tuple-element.122), channel_id=1, source_target_pairs={{0,2},{1,3},{2,0},{3,1},{4,6},{5,7},{6,4},{7,5},{8,10},{9,11},{10,... | collective-permute-start | bytes 172040 | tf_op jit(solution)/shard_map/ppermute | solution.py:594
  289.5 4.7 %collective-permute-start.28 = (f32[112,128]{1,0:T(8,128)S(1)}, f32[112,128]{1,0:T(8,128)S(1)}, u32[]{:S(2)}, u32[]{:S(2)}) collective-permute-start(f32[112,128]{1,0:T(8,128)S(1)} %get-tuple-element.123), channel_id=1, source_target_pairs={{0,3},{1,0},{2,1},{3,2},{4,7},{5,4},{6,5},{7,6},{8,11},{9,8},{10,9... | collective-permute-start | bytes 172040 | tf_op jit(solution)/shard_map/ppermute | solution.py:594
  292.4 1.8 copy-start.43
  296.4 6.1 %collective-permute-start.29 = (f32[80,128]{1,0:T(8,128)}, f32[80,128]{1,0:T(8,128)S(1)}, u32[]{:S(2)}, u32[]{:S(2)}) collective-permute-start(f32[80,128]{1,0:T(8,128)} %gas.7.refs_0_), channel_id=1, source_target_pairs={{0,1},{1,2},{2,3},{3,0},{4,5},{5,6},{6,7},{7,4},{8,9},{9,10},{10,1... | collective-permute-start | bytes 122888 | tf_op jit(solution)/shard_map/ppermute | solution.py:594
  297.2 6.0 %collective-permute-start.30 = (f32[80,128]{1,0:T(8,128)}, f32[80,128]{1,0:T(8,128)S(1)}, u32[]{:S(2)}, u32[]{:S(2)}) collective-permute-start(f32[80,128]{1,0:T(8,128)} %gas.7.refs_0_), channel_id=1, source_target_pairs={{0,2},{1,3},{2,0},{3,1},{4,6},{5,7},{6,4},{7,5},{8,10},{9,11},{10,... | collective-permute-start | bytes 122888 | tf_op jit(solution)/shard_map/ppermute | solution.py:594
  299.4 4.3 %collective-permute-start.31 = (f32[80,128]{1,0:T(8,128)}, f32[80,128]{1,0:T(8,128)S(1)}, u32[]{:S(2)}, u32[]{:S(2)}) collective-permute-start(f32[80,128]{1,0:T(8,128)} %gas.7.refs_0_), channel_id=1, source_target_pairs={{0,3},{1,0},{2,1},{3,2},{4,7},{5,4},{6,5},{7,6},{8,11},{9,8},{10,9... | collective-permute-start | bytes 122888 | tf_op jit(solution)/shard_map/ppermute | solution.py:594
  (20 other events, 13.9 us)

commit v5 on v4

--- a/solution.py
+++ b/solution.py
@@ -36,8 +36,8 @@
 COEF = 2 * PART
 STRIDE = COEF + 1
 
-VMEM_LIMIT = 44 * 1024 * 1024
-SMALL_LIMIT = 24 * 1024 * 1024
+VMEM_LIMIT = 60 * 1024 * 1024
+SMALL_LIMIT = 52 * 1024 * 1024
 
 
 def setup_kernel(span, kind_in_ref, code_in_ref, temp_in_ref, kind_ref, code_ref, temp_ref, target_ref, factor_ref, wall_ref, sums_ref, stencil_ref, spread_ref,
@@ -339,14 +339,10 @@
 
 def relax_block(spread_ref, tables, coef_ref, even_ref, flat_ref, store):
     even_ref[...] = dot(coef_ref[...], spread_ref[...])
-
-    def lane(l, carry):
-        columns = pl.ds(pl.multiple_of(l * WIDE, WIDE), WIDE)
+    for l in range(flat_ref.shape[1] // WIDE):
+        columns = slice(l * WIDE, (l + 1) * WIDE)
         target, factor, wall = (ref[:, columns] for ref in tables)
         store(l, relaxed(coef_ref[...], even_ref, flat_ref[:, columns], target, factor, wall))
-        return carry
-
-    lax.fori_loop(0, flat_ref.shape[1] // WIDE, lane, 0)
 
 
 PAD = 8
@@ -358,10 +354,12 @@
     span = out_ref.shape[1]
     nothing = jnp.minimum(lax.axis_index("vel"), 0)
     shape = (ncols // 8, 8, LANES)
+    unrolled = rows == BLOCK
 
     def lanes(l, carry):
         for h in range(WIDE // LANES):
-            columns = pl.ds(pl.multiple_of(l * WIDE + h * LANES, LANES), LANES)
+            first = l * WIDE + h * LANES
+            columns = slice(first, first + LANES) if unrolled else pl.ds(pl.multiple_of(first, LANES), LANES)
             x0, x1, x2, vx, y0, y1, y2, _ = (stencil_ref[8 * k:8 * k + 8, columns][None] for k in range(8))
             x_up = jnp.broadcast_to(vx > 0, shape)
             ahead = 1 if h == 0 else -1
@@ -393,10 +391,19 @@
                     half_ref[1, cut, columns] = (value - upper.astype(jnp.float32)).astype(jnp.bfloat16)
         return carry
 
-    lax.fori_loop(0, span // WIDE, lanes, 0)
-    table = dot(half_ref[0], sums_ref[...])
-    if exact:
-        table = table + dot(half_ref[1], sums_ref[...])
+    table = None
+    if unrolled:
+        for l in range(span // WIDE):
+            lanes(l, 0)
+            columns = slice(l * WIDE, (l + 1) * WIDE)
+            for k in range(1 + exact):
+                term = dot(half_ref[k, :, columns], sums_ref[columns, :])
+                table = term if table is None else table + term
+    else:
+        lax.fori_loop(0, span // WIDE, lanes, 0)
+        table = dot(half_ref[0], sums_ref[...])
+        if exact:
+            table = table + dot(half_ref[1], sums_ref[...])
     for g in range(rows * ncols // LANES):
         total = table[g * LANES:(g + 1) * LANES, :].T
         kind = kind_ref[pl.ds(group + g, 1), :]
@@ -440,16 +447,15 @@
 
         if relax:
             def store(l, values):
-                field_ref[here, pl.ds(pl.multiple_of(l * WIDE, WIDE), WIDE)] = values
+                field_ref[here, l * WIDE:(l + 1) * WIDE] = values
 
             relax_block(spread_ref, (target_ref, factor_ref, wall_ref), coef_ref, even_ref, flat_ref, store)
         else:
-            def lane(l, carry):
-                columns = pl.ds(pl.multiple_of(l * WIDE, WIDE), WIDE)
-                field_ref[here, columns] = turned(flat_ref[:, columns], l, span)
-                return carry
-
-            lax.fori_loop(0, span // WIDE, lane, 0)
+            for l in range(span // WIDE):
+                columns = slice(l * WIDE, (l + 1) * WIDE)
+                for start in range(0, block, edge):
+                    field_ref[pl.ds(pl.multiple_of(edge + i * block + start, edge), edge), columns] = turned(
+                        flat_ref[start:start + edge, columns], l, span)
 
     @pl.when(i > 0)
     def _():
@@ -559,7 +565,7 @@
     span = flat_ref.shape[1]
 
     def store(l, values):
-        out_ref[:, pl.ds(pl.multiple_of(l * WIDE, WIDE), WIDE)] = turned(values, l, span, back=True)
+        out_ref[:, l * WIDE:(l + 1) * WIDE] = turned(values, l, span, back=True)
 
     relax_block(spread_ref, (target_ref, factor_ref, wall_ref), coef_ref, even_ref, flat_ref, store)
 

time: 327 us -> 285 us (0.87)
  local copies, waits for them, and re-layouts: 61.9 us -> 21.2 us
    unnamed x105 -> x153, local copies, waits for them, and re-layouts: 59.5 us -> 19.7 us
    pallas_call x4, Pallas kernels: 134 us -> 118 us  [inner(): pl.pallas_call(functools.partial(inner_kernel, relax, exact, blocks, ncol...]
    pallas_call x4, Pallas kernels: 8.8 us -> 20.7 us  [outer(): pl.pallas_call(functools.partial(outer_kernel, relax, exact, ncols, count...]
    pallas_call x4, Pallas kernels: 4.88 us -> 9.64 us  [state(): pl.pallas_call(functools.partial(state_kernel, len(pieces), groups, with_...]
where the time goes in v5:
time: 285 us; the launch traced here: 283 us
  Pallas kernels  174 us (61%)
  starting transfers between devices  58.3 us (20%)
  waiting for transfers between devices  28.6 us (10%)
  local copies, waits for them, and re-layouts  21.2 us (7%)
    pallas_call x4, Pallas kernels, inner(): pl.pallas_call(functools.partial(inner_kernel, relax, exact, blocks, ncol...  118 us
    ppermute x24, starting transfers between devices, swap(): lax.ppermute(slots[k], 'vel', [(i, (i + k) % count) for i in range(count)])  32.5 us
    ppermute x24, waiting for transfers between devices, swap(): lax.ppermute(slots[k], 'vel', [(i, (i + k) % count) for i in range(count)])  28.6 us
    ppermute x8, starting transfers between devices, exchange(): return (lax.ppermute(last, 'space', up), lax.ppermute(first, 'space', down))  25.8 us
    pallas_call x4, Pallas kernels, outer(): pl.pallas_call(functools.partial(outer_kernel, relax, exact, ncols, count...  20.7 us
    unnamed x153, local copies, waits for them, and re-layouts  19.7 us
    pallas_call x1, Pallas kernels, finish(): pl.pallas_call(last_kernel, grid=(cells // block,), out_shape=jax.ShapeDt...  17.5 us
    pallas_call x4, Pallas kernels, state(): pl.pallas_call(functools.partial(state_kernel, len(pieces), groups, with_...  9.64 us
  transfers between devices with their start and end apart: 32, of which 24 were waited for; matrix products, arithmetic and copies ran while one was open for 0% of the time, Pallas kernels for 42%

profile of v5, /device:TPU:4, one launch (start us, length us, event | category | flops | bytes accessed | tf_op | source)
XLA Modules:
  0.0 283.3 jit_solution(14565969095444686657)
XLA Ops:
  0.6 1.3 fusion
  1.9 1.9 collective-permute-start
  3.9 4.5 %collective-permute-start.1 = (f32[128,1024]{1,0:T(8,128)S(1)}, f32[128,1024]{1,0:T(8,128)S(1)}, u32[]{:S(2)}, u32[]{:S(2)}) collective-permute-start(f32[128,1024]{1,0:T(8,128)S(1)} %bitcast.6), channel_id=1, source_target_pairs={{4,0},{8,4},{12,8},{16,12},{20,16},{24,20},{28,24},{5,1},{9,5},{13... | collective-permute-start | bytes 1572872 | tf_op jit(solution)/shard_map/ppermute | solution.py:595
  8.4 1.9 setup.1
  10.4 26.0 %inner_first.1 = (f32[4096,1024]{1,0:T(8,128)}, f32[448,128]{1,0:T(8,128)}, f32[256,1024]{1,0:T(8,128)}, f32[256,1024]{1,0:T(8,128)}) custom-call(f32[4096,1024]{1,0:T(8,128)} %bitcast.4, s32[32,128]{1,0:T(8,128)} %get-tuple-element.64.kind_ref.refs_4_, s32[32,128]{1,0:T(8,128)} %get-tuple-element.65.code_ref.refs_5_, ...), custom_call_target="tpu_custom_call" | custom-call | flops 3221225472 | bytes 33554432 | tf_op jit(solution)/shard_map/inner_first/pallas_call | solution.py:522
  37.4 0.9 copy-done.47
  38.4 5.2 %outer_first.1 = (f32[4096,1024]{1,0:T(8,128)}, f32[128,1024]{1,0:T(8,128)S(1)}, f32[128,1024]{1,0:T(8,128)}, f32[112,128]{1,0:T(8,128)S(1)}, f32[112,128]{1,0:T...) custom-call(f32[4096,1024]{1,0:T(8,128)} %get-tuple-element.68.flat_ref, ...), custom_call_target="tpu_custom_call", output_to_operand_aliasing={{0}: (0, {})} | custom-call | tf_op jit(solution)/shard_map/outer_first/pallas_call | solution.py:547
  45.1 1.6 collective-permute-start.2
  46.6 2.6 collective-permute-start.3
  49.2 1.3 collective-permute-start.4
  50.6 1.0 collective-permute-done.2.refs_1_
  51.6 1.4 collective-permute-done.3.refs_2_
  54.1 1.6 gas.4.refs_0_
  56.3 3.0 %collective-permute-start.6 = (f32[80,128]{1,0:T(8,128)}, f32[80,128]{1,0:T(8,128)S(1)}, u32[]{:S(2)}, u32[]{:S(2)}) collective-permute-start(f32[80,128]{1,0:T(8,128)} %gas.4.refs_0_), channel_id=1, source_target_pairs={{0,2},{1,3},{2,0},{3,1},{4,6},{5,7},{6,4},{7,5},{8,10},{9,11},{10,... | collective-permute-start | bytes 122888 | tf_op jit(solution)/shard_map/ppermute | solution.py:600
  59.5 2.3 collective-permute-done.5.refs_1_
  62.4 1.1 collective-permute-done.7.refs_3_
  64.4 3.0 %state.4 = (bf16[4096,64]{1,0:T(8,128)(2,1)}, f32[128,1024]{1,0:T(8,128)S(1)}, f32[128,1024]{1,0:T(8,128)S(1)}) custom-call(f32[80,128]{1,0:T(8,128)S(1)} %copy-done.48, f32[80,128]{1,0:T(8,128)S(1)} %collective-permute-done.5.refs_1_, f32[80,128]{1,0:T(8,128)S(1)} %collective-permute-done.6.refs_2_, f32[80,128]{1,0:T(8,128)S(1)} %collective-permute-done.7.refs_3_, ...), custom_call_target="tpu_custom_call" | custom-call | tf_op jit(solution)/shard_map/state/pallas_call | solution.py:312
  67.3 1.9 collective-permute-start.8
  69.2 4.5 %collective-permute-start.9 = (f32[128,1024]{1,0:T(8,128)S(1)}, f32[128,1024]{1,0:T(8,128)S(1)}, u32[]{:S(2)}, u32[]{:S(2)}) collective-permute-start(f32[128,1024]{1,0:T(8,128)S(1)} %get-tuple-element.90), channel_id=1, source_target_pairs={{4,0},{8,4},{12,8},{16,12},{20,16},{24,20},{28,24},{5,1},{9,5},{13... | collective-permute-start | bytes 1572872 | tf_op jit(solution)/shard_map/ppermute | solution.py:595
  73.9 29.5 %inner.3 = (f32[4096,1024]{1,0:T(8,128)}, f32[448,128]{1,0:T(8,128)}, f32[256,1024]{1,0:T(8,128)}, f32[256,1024]{1,0:T(8,128)}) custom-call(f32[4096,1024]{1,0:T(8,128)} %get-tuple-element.72.flat_ref, s32[32,128]{1,0:T(8,128)} %get-tuple-element.64.kind_ref.refs_4_, s32[32,128]{1,0:T(8,128)} %get-tuple-element.65.code_ref.refs_5_, ...), custom_call_target="tpu_custom_call" | custom-call | flops 3221225472 | bytes 33554432 | tf_op jit(solution)/shard_map/inner/pallas_call | solution.py:522
  104.4 0.9 copy-done.45
  105.3 5.0 %outer.3 = (f32[4096,1024]{1,0:T(8,128)}, f32[128,1024]{1,0:T(8,128)S(1)}, f32[128,1024]{1,0:T(8,128)}, f32[112,128]{1,0:T(8,128)S(1)}, f32[112,128]{1,0:T(8,128...) custom-call(f32[4096,1024]{1,0:T(8,128)} %get-tuple-element.85.flat_ref, ...), custom_call_target="tpu_custom_call", output_to_operand_aliasing={{0}: (0, {})} | custom-call | tf_op jit(solution)/shard_map/outer/pallas_call | solution.py:547
  111.8 0.8 collective-permute-start.10
  112.6 2.0 collective-permute-start.11
  114.6 1.0 collective-permute-start.12
  115.6 2.2 collective-permute-done.10.refs_1_
  117.9 1.1 collective-permute-done.11.refs_2_
  119.8 1.6 gas.5.refs_0_
  121.4 1.2 collective-permute-start.13
  122.6 2.0 collective-permute-start.14
  125.2 2.2 collective-permute-done.13.refs_1_
  127.4 0.9 collective-permute-done.14.refs_2_
  129.6 3.0 %state.5 = (bf16[4096,64]{1,0:T(8,128)(2,1)}, f32[128,1024]{1,0:T(8,128)S(1)}, f32[128,1024]{1,0:T(8,128)S(1)}) custom-call(f32[80,128]{1,0:T(8,128)S(1)} %copy-done.49, f32[80,128]{1,0:T(8,128)S(1)} %collective-permute-done.13.refs_1_, f32[80,128]{1,0:T(8,128)S(1)} %collective-permute-done.14.refs_2_, f32[80,128]{1,0:T(8,128)S(1)} %collective-permute-done.15.refs_3_, ...), custom_call_target="tpu_custom_call" | custom-call | tf_op jit(solution)/shard_map/state/pallas_call | solution.py:312
  132.6 1.9 collective-permute-start.16
  134.5 4.5 %collective-permute-start.17 = (f32[128,1024]{1,0:T(8,128)S(1)}, f32[128,1024]{1,0:T(8,128)S(1)}, u32[]{:S(2)}, u32[]{:S(2)}) collective-permute-start(f32[128,1024]{1,0:T(8,128)S(1)} %get-tuple-element.104), channel_id=1, source_target_pairs={{4,0},{8,4},{12,8},{16,12},{20,16},{24,20},{28,24},{5,1},{9,5},{13... | collective-permute-start | bytes 1572872 | tf_op jit(solution)/shard_map/ppermute | solution.py:595
  139.1 29.6 %inner.4 = (f32[4096,1024]{1,0:T(8,128)}, f32[448,128]{1,0:T(8,128)}, f32[256,1024]{1,0:T(8,128)}, f32[256,1024]{1,0:T(8,128)}) custom-call(f32[4096,1024]{1,0:T(8,128)} %get-tuple-element.91.flat_ref, s32[32,128]{1,0:T(8,128)} %get-tuple-element.64.kind_ref.refs_4_, s32[32,128]{1,0:T(8,128)} %get-tuple-element.65.code_ref.refs_5_, ...), custom_call_target="tpu_custom_call" | custom-call | flops 3221225472 | bytes 33554432 | tf_op jit(solution)/shard_map/inner/pallas_call | solution.py:522
  169.8 0.9 copy-done.46
  170.7 5.0 %outer.4 = (f32[4096,1024]{1,0:T(8,128)}, f32[128,1024]{1,0:T(8,128)S(1)}, f32[128,1024]{1,0:T(8,128)}, f32[112,128]{1,0:T(8,128)S(1)}, f32[112,128]{1,0:T(8,128...) custom-call(f32[4096,1024]{1,0:T(8,128)} %get-tuple-element.99.flat_ref, ...), custom_call_target="tpu_custom_call", output_to_operand_aliasing={{0}: (0, {})} | custom-call | tf_op jit(solution)/shard_map/outer/pallas_call | solution.py:547
  177.2 1.2 collective-permute-start.18
  178.4 1.8 collective-permute-start.19
  180.2 0.9 collective-permute-start.20
  181.1 2.1 collective-permute-done.18.refs_1_
  183.2 1.3 collective-permute-done.19.refs_2_
  185.5 1.6 gas.6.refs_0_
  187.1 0.9 collective-permute-start.21
  187.9 2.2 collective-permute-start.22
  190.1 0.8 collective-permute-start.23
  190.9 2.3 collective-permute-done.21.refs_1_
  195.2 3.0 %state.6 = (bf16[4096,64]{1,0:T(8,128)(2,1)}, f32[128,1024]{1,0:T(8,128)S(1)}, f32[128,1024]{1,0:T(8,128)S(1)}) custom-call(f32[80,128]{1,0:T(8,128)S(1)} %copy-done.50, f32[80,128]{1,0:T(8,128)S(1)} %collective-permute-done.21.refs_1_, f32[80,128]{1,0:T(8,128)S(1)} %collective-permute-done.22.refs_2_, f32[80,128]{1,0:T(8,128)S(1)} %collective-permute-done.23.refs_3_, ...), custom_call_target="tpu_custom_call" | custom-call | tf_op jit(solution)/shard_map/state/pallas_call | solution.py:312
  198.1 1.9 collective-permute-start.24
  200.1 4.5 %collective-permute-start.25 = (f32[128,1024]{1,0:T(8,128)S(1)}, f32[128,1024]{1,0:T(8,128)S(1)}, u32[]{:S(2)}, u32[]{:S(2)}) collective-permute-start(f32[128,1024]{1,0:T(8,128)S(1)} %get-tuple-element.118), channel_id=1, source_target_pairs={{4,0},{8,4},{12,8},{16,12},{20,16},{24,20},{28,24},{5,1},{9,5},{13... | collective-permute-start | bytes 1572872 | tf_op jit(solution)/shard_map/ppermute | solution.py:595
  204.6 32.6 %inner.5 = (f32[4096,1024]{1,0:T(8,128)}, f32[448,128]{1,0:T(8,128)}, f32[256,1024]{1,0:T(8,128)}, f32[256,1024]{1,0:T(8,128)}) custom-call(f32[4096,1024]{1,0:T(8,128)} %get-tuple-element.105.flat_ref, s32[32,128]{1,0:T(8,128)} %get-tuple-element.64.kind_ref.refs_4_, s32[32,128]{1,0:T(8,128)} %get-tuple-element.65.code_ref.refs_5_, ...), custom_call_target="tpu_custom_call" | custom-call | flops 3221225472 | bytes 33554432 | tf_op jit(solution)/shard_map/inner/pallas_call | solution.py:522
  238.3 0.9 copy-done.44
  239.2 5.4 %outer.5 = (f32[4096,1024]{1,0:T(8,128)}, f32[128,1024]{1,0:T(8,128)}, f32[128,1024]{1,0:T(8,128)}, f32[112,128]{1,0:T(8,128)S(1)}, f32[112,128]{1,0:T(8,128)S(1...) custom-call(f32[4096,1024]{1,0:T(8,128)} %get-tuple-element.113.flat_ref, ...), custom_call_target="tpu_custom_call", output_to_operand_aliasing={{0}: (0, {})} | custom-call | tf_op jit(solution)/shard_map/outer/pallas_call | solution.py:547
  245.3 1.3 collective-permute-start.26
  246.6 1.8 collective-permute-start.27
  249.2 2.1 collective-permute-done.26.refs_1_
  251.3 1.3 collective-permute-done.27.refs_2_
  253.7 1.6 gas.7.refs_0_
  256.1 2.2 collective-permute-start.30
  258.2 0.9 collective-permute-start.31
  259.1 2.3 collective-permute-done.29.refs_1_
  264.1 1.0 copy-done.40
  265.9 17.5 %finish.1 = f32[4096,1024]{1,0:T(8,128)} custom-call(f32[4096,1024]{1,0:T(8,128)} %get-tuple-element.119.flat_ref, bf16[4096,64]{1,0:T(8,128)(2,1)} %copy-done.40, bf16[64,256]{1,0:T(8,128)(2,1)} %get-tuple-element.80.refs_9_.refs_1_.spread_ref, bf16[64,1024]{1,0:T(8,128)(2,1)} %get-tuple-element.81.refs_10_.refs_2_.target_ref, ...), custom_call_target="tpu_custom_call" | custom-call | tf_op jit(solution)/shard_map/finish/pallas_call | solution.py:577
  (174 shorter events, 23.9 us)
Async XLA Ops:
  1.9 34.5 %collective-permute-start = (f32[128,1024]{1,0:T(8,128)S(1)}, f32[128,1024]{1,0:T(8,128)S(1)}, u32[]{:S(2)}, u32[]{:S(2)}) collective-permute-start(f32[128,1024]{1,0:T(8,128)S(1)} %bitcast.7), channel_id=1, source_target_pairs={{0,4},{4,8},{8,12},{12,16},{16,20},{20,24},{24,28},{1,5},{5,9},{9,... | collective-permute-start | bytes 1572872 | tf_op jit(solution)/shard_map/ppermute | solution.py:595
  3.9 32.6 %collective-permute-start.1 = (f32[128,1024]{1,0:T(8,128)S(1)}, f32[128,1024]{1,0:T(8,128)S(1)}, u32[]{:S(2)}, u32[]{:S(2)}) collective-permute-start(f32[128,1024]{1,0:T(8,128)S(1)} %bitcast.6), channel_id=1, source_target_pairs={{4,0},{8,4},{12,8},{16,12},{20,16},{24,20},{28,24},{5,1},{9,5},{13... | collective-permute-start | bytes 1572872 | tf_op jit(solution)/shard_map/ppermute | solution.py:595
  10.4 53.2 %copy-start.8 = (bf16[64,1024]{1,0:T(8,128)(2,1)S(1)}, bf16[64,1024]{1,0:T(8,128)(2,1)}, u32[]{:S(2)}) copy-start(bf16[64,1024]{1,0:T(8,128)(2,1)} %get-tuple-element.81.refs_10_.refs_2_.target_ref) | copy-start | bytes 393220
  10.4 53.2 %copy-start.11 = (bf16[64,1024]{1,0:T(8,128)(2,1)S(1)}, bf16[64,1024]{1,0:T(8,128)(2,1)}, u32[]{:S(2)}) copy-start(bf16[64,1024]{1,0:T(8,128)(2,1)} %get-tuple-element.82.refs_11_.refs_3_.factor_ref) | copy-start | bytes 393220
  10.4 53.2 %copy-start.14 = (bf16[64,1024]{1,0:T(8,128)(2,1)S(1)}, bf16[64,1024]{1,0:T(8,128)(2,1)}, u32[]{:S(2)}) copy-start(bf16[64,1024]{1,0:T(8,128)(2,1)} %get-tuple-element.83.refs_12_.refs_4_.wall_ref) | copy-start | bytes 393220
  38.4 66.0 %copy-start.1 = (bf16[1024,128]{1,0:T(8,128)(2,1)S(1)}, bf16[1024,128]{1,0:T(8,128)(2,1)}, u32[]{:S(2)}) copy-start(bf16[1024,128]{1,0:T(8,128)(2,1)} %get-tuple-element.66.sums_ref) | copy-start | bytes 786436
  38.4 66.0 %copy-start.5 = (f32[64,1024]{1,0:T(8,128)S(1)}, f32[64,1024]{1,0:T(8,128)}, u32[]{:S(2)}) copy-start(f32[64,1024]{1,0:T(8,128)} %get-tuple-element.67.stencil_ref) | copy-start | bytes 786436
  38.4 66.0 %copy-start.19 = (s32[32,128]{1,0:T(8,128)S(1)}, s32[32,128]{1,0:T(8,128)}, u32[]{:S(2)}) copy-start(s32[32,128]{1,0:T(8,128)} %get-tuple-element.64.kind_ref.refs_4_) | copy-start | bytes 49156
  38.4 66.0 %copy-start.27 = (s32[32,128]{1,0:T(8,128)S(1)}, s32[32,128]{1,0:T(8,128)}, u32[]{:S(2)}) copy-start(s32[32,128]{1,0:T(8,128)} %get-tuple-element.65.code_ref.refs_5_) | copy-start | bytes 49156
  45.1 6.5 %collective-permute-start.2 = (f32[112,128]{1,0:T(8,128)S(1)}, f32[112,128]{1,0:T(8,128)S(1)}, u32[]{:S(2)}, u32[]{:S(2)}) collective-permute-start(f32[112,128]{1,0:T(8,128)S(1)} %get-tuple-element.74), channel_id=1, source_target_pairs={{0,1},{1,2},{2,3},{3,0},{4,5},{5,6},{6,7},{7,4},{8,9},{9,10},{10,1... | collective-permute-start | bytes 172040 | tf_op jit(solution)/shard_map/ppermute | solution.py:600
  46.6 6.4 %collective-permute-start.3 = (f32[112,128]{1,0:T(8,128)S(1)}, f32[112,128]{1,0:T(8,128)S(1)}, u32[]{:S(2)}, u32[]{:S(2)}) collective-permute-start(f32[112,128]{1,0:T(8,128)S(1)} %get-tuple-element.75), channel_id=1, source_target_pairs={{0,2},{1,3},{2,0},{3,1},{4,6},{5,7},{6,4},{7,5},{8,10},{9,11},{10,... | collective-permute-start | bytes 172040 | tf_op jit(solution)/shard_map/ppermute | solution.py:600
  49.2 4.3 %collective-permute-start.4 = (f32[112,128]{1,0:T(8,128)S(1)}, f32[112,128]{1,0:T(8,128)S(1)}, u32[]{:S(2)}, u32[]{:S(2)}) collective-permute-start(f32[112,128]{1,0:T(8,128)S(1)} %get-tuple-element.76), channel_id=1, source_target_pairs={{0,3},{1,0},{2,1},{3,2},{4,7},{5,4},{6,5},{7,6},{8,11},{9,8},{10,9... | collective-permute-start | bytes 172040 | tf_op jit(solution)/shard_map/ppermute | solution.py:600
  55.7 6.1 %collective-permute-start.5 = (f32[80,128]{1,0:T(8,128)}, f32[80,128]{1,0:T(8,128)S(1)}, u32[]{:S(2)}, u32[]{:S(2)}) collective-permute-start(f32[80,128]{1,0:T(8,128)} %gas.4.refs_0_), channel_id=1, source_target_pairs={{0,1},{1,2},{2,3},{3,0},{4,5},{5,6},{6,7},{7,4},{8,9},{9,10},{10,1... | collective-permute-start | bytes 122888 | tf_op jit(solution)/shard_map/ppermute | solution.py:600
  56.3 6.1 %collective-permute-start.6 = (f32[80,128]{1,0:T(8,128)}, f32[80,128]{1,0:T(8,128)S(1)}, u32[]{:S(2)}, u32[]{:S(2)}) collective-permute-start(f32[80,128]{1,0:T(8,128)} %gas.4.refs_0_), channel_id=1, source_target_pairs={{0,2},{1,3},{2,0},{3,1},{4,6},{5,7},{6,4},{7,5},{8,10},{9,11},{10,... | collective-permute-start | bytes 122888 | tf_op jit(solution)/shard_map/ppermute | solution.py:600
  59.3 4.2 %collective-permute-start.7 = (f32[80,128]{1,0:T(8,128)}, f32[80,128]{1,0:T(8,128)S(1)}, u32[]{:S(2)}, u32[]{:S(2)}) collective-permute-start(f32[80,128]{1,0:T(8,128)} %gas.4.refs_0_), channel_id=1, source_target_pairs={{0,3},{1,0},{2,1},{3,2},{4,7},{5,4},{6,5},{7,6},{8,11},{9,8},{10,9... | collective-permute-start | bytes 122888 | tf_op jit(solution)/shard_map/ppermute | solution.py:600
  67.3 36.1 %collective-permute-start.8 = (f32[128,1024]{1,0:T(8,128)S(1)}, f32[128,1024]{1,0:T(8,128)S(1)}, u32[]{:S(2)}, u32[]{:S(2)}) collective-permute-start(f32[128,1024]{1,0:T(8,128)S(1)} %get-tuple-element.89), channel_id=1, source_target_pairs={{0,4},{4,8},{8,12},{12,16},{16,20},{20,24},{24,28},{1,5},{5,9},{9,... | collective-permute-start | bytes 1572872 | tf_op jit(solution)/shard_map/ppermute | solution.py:595
  69.2 34.2 %collective-permute-start.9 = (f32[128,1024]{1,0:T(8,128)S(1)}, f32[128,1024]{1,0:T(8,128)S(1)}, u32[]{:S(2)}, u32[]{:S(2)}) collective-permute-start(f32[128,1024]{1,0:T(8,128)S(1)} %get-tuple-element.90), channel_id=1, source_target_pairs={{4,0},{8,4},{12,8},{16,12},{20,16},{24,20},{28,24},{5,1},{9,5},{13... | collective-permute-start | bytes 1572872 | tf_op jit(solution)/shard_map/ppermute | solution.py:595
  73.8 55.0 %copy-start.9 = (bf16[64,1024]{1,0:T(8,128)(2,1)S(1)}, bf16[64,1024]{1,0:T(8,128)(2,1)}, u32[]{:S(2)}) copy-start(bf16[64,1024]{1,0:T(8,128)(2,1)} %get-tuple-element.81.refs_10_.refs_2_.target_ref) | copy-start | bytes 393220
  73.8 55.0 %copy-start.12 = (bf16[64,1024]{1,0:T(8,128)(2,1)S(1)}, bf16[64,1024]{1,0:T(8,128)(2,1)}, u32[]{:S(2)}) copy-start(bf16[64,1024]{1,0:T(8,128)(2,1)} %get-tuple-element.82.refs_11_.refs_3_.factor_ref) | copy-start | bytes 393220
  73.8 55.0 %copy-start.15 = (bf16[64,1024]{1,0:T(8,128)(2,1)S(1)}, bf16[64,1024]{1,0:T(8,128)(2,1)}, u32[]{:S(2)}) copy-start(bf16[64,1024]{1,0:T(8,128)(2,1)} %get-tuple-element.83.refs_12_.refs_4_.wall_ref) | copy-start | bytes 393220
  73.8 55.0 %copy-start.20 = (s32[32,128]{1,0:T(8,128)S(1)}, s32[32,128]{1,0:T(8,128)}, u32[]{:S(2)}) copy-start(s32[32,128]{1,0:T(8,128)} %get-tuple-element.64.kind_ref.refs_4_) | copy-start | bytes 49156
  73.8 55.0 %copy-start.28 = (s32[32,128]{1,0:T(8,128)S(1)}, s32[32,128]{1,0:T(8,128)}, u32[]{:S(2)}) copy-start(s32[32,128]{1,0:T(8,128)} %get-tuple-element.65.code_ref.refs_5_) | copy-start | bytes 49156
  73.8 55.0 %copy-start.34 = (bf16[64,256]{1,0:T(8,128)(2,1)S(1)}, bf16[64,256]{1,0:T(8,128)(2,1)}, u32[]{:S(2)}) copy-start(bf16[64,256]{1,0:T(8,128)(2,1)} %get-tuple-element.80.refs_9_.refs_1_.spread_ref) | copy-start | bytes 98308
  73.8 55.0 %copy-start.37 = (f32[32,128]{1,0:T(8,128)S(1)}, f32[32,128]{1,0:T(8,128)}, u32[]{:S(2)}) copy-start(f32[32,128]{1,0:T(8,128)} %get-tuple-element.77.refs_6_) | copy-start | bytes 49156
  105.3 64.5 %copy-start.2 = (bf16[1024,128]{1,0:T(8,128)(2,1)S(1)}, bf16[1024,128]{1,0:T(8,128)(2,1)}, u32[]{:S(2)}) copy-start(bf16[1024,128]{1,0:T(8,128)(2,1)} %get-tuple-element.66.sums_ref) | copy-start | bytes 786436
  105.3 64.5 %copy-start.6 = (f32[64,1024]{1,0:T(8,128)S(1)}, f32[64,1024]{1,0:T(8,128)}, u32[]{:S(2)}) copy-start(f32[64,1024]{1,0:T(8,128)} %get-tuple-element.67.stencil_ref) | copy-start | bytes 786436
  105.3 64.5 %copy-start.21 = (s32[32,128]{1,0:T(8,128)S(1)}, s32[32,128]{1,0:T(8,128)}, u32[]{:S(2)}) copy-start(s32[32,128]{1,0:T(8,128)} %get-tuple-element.64.kind_ref.refs_4_) | copy-start | bytes 49156
  105.3 64.5 %copy-start.29 = (s32[32,128]{1,0:T(8,128)S(1)}, s32[32,128]{1,0:T(8,128)}, u32[]{:S(2)}) copy-start(s32[32,128]{1,0:T(8,128)} %get-tuple-element.65.code_ref.refs_5_) | copy-start | bytes 49156
  111.8 6.1 %collective-permute-start.10 = (f32[112,128]{1,0:T(8,128)S(1)}, f32[112,128]{1,0:T(8,128)S(1)}, u32[]{:S(2)}, u32[]{:S(2)}) collective-permute-start(f32[112,128]{1,0:T(8,128)S(1)} %get-tuple-element.93), channel_id=1, source_target_pairs={{0,1},{1,2},{2,3},{3,0},{4,5},{5,6},{6,7},{7,4},{8,9},{9,10},{10,1... | collective-permute-start | bytes 172040 | tf_op jit(solution)/shard_map/ppermute | solution.py:600
  112.6 6.4 %collective-permute-start.11 = (f32[112,128]{1,0:T(8,128)S(1)}, f32[112,128]{1,0:T(8,128)S(1)}, u32[]{:S(2)}, u32[]{:S(2)}) collective-permute-start(f32[112,128]{1,0:T(8,128)S(1)} %get-tuple-element.94), channel_id=1, source_target_pairs={{0,2},{1,3},{2,0},{3,1},{4,6},{5,7},{6,4},{7,5},{8,10},{9,11},{10,... | collective-permute-start | bytes 172040 | tf_op jit(solution)/shard_map/ppermute | solution.py:600
  114.6 4.6 %collective-permute-start.12 = (f32[112,128]{1,0:T(8,128)S(1)}, f32[112,128]{1,0:T(8,128)S(1)}, u32[]{:S(2)}, u32[]{:S(2)}) collective-permute-start(f32[112,128]{1,0:T(8,128)S(1)} %get-tuple-element.95), channel_id=1, source_target_pairs={{0,3},{1,0},{2,1},{3,2},{4,7},{5,4},{6,5},{7,6},{8,11},{9,8},{10,9... | collective-permute-start | bytes 172040 | tf_op jit(solution)/shard_map/ppermute | solution.py:600
  121.4 6.0 %collective-permute-start.13 = (f32[80,128]{1,0:T(8,128)}, f32[80,128]{1,0:T(8,128)S(1)}, u32[]{:S(2)}, u32[]{:S(2)}) collective-permute-start(f32[80,128]{1,0:T(8,128)} %gas.5.refs_0_), channel_id=1, source_target_pairs={{0,1},{1,2},{2,3},{3,0},{4,5},{5,6},{6,7},{7,4},{8,9},{9,10},{10,1... | collective-permute-start | bytes 122888 | tf_op jit(solution)/shard_map/ppermute | solution.py:600
  122.6 5.7 %collective-permute-start.14 = (f32[80,128]{1,0:T(8,128)}, f32[80,128]{1,0:T(8,128)S(1)}, u32[]{:S(2)}, u32[]{:S(2)}) collective-permute-start(f32[80,128]{1,0:T(8,128)} %gas.5.refs_0_), channel_id=1, source_target_pairs={{0,2},{1,3},{2,0},{3,1},{4,6},{5,7},{6,4},{7,5},{8,10},{9,11},{10,... | collective-permute-start | bytes 122888 | tf_op jit(solution)/shard_map/ppermute | solution.py:600
  124.6 4.2 %collective-permute-start.15 = (f32[80,128]{1,0:T(8,128)}, f32[80,128]{1,0:T(8,128)S(1)}, u32[]{:S(2)}, u32[]{:S(2)}) collective-permute-start(f32[80,128]{1,0:T(8,128)} %gas.5.refs_0_), channel_id=1, source_target_pairs={{0,3},{1,0},{2,1},{3,2},{4,7},{5,4},{6,5},{7,6},{8,11},{9,8},{10,9... | collective-permute-start | bytes 122888 | tf_op jit(solution)/shard_map/ppermute | solution.py:600
  132.6 36.2 %collective-permute-start.16 = (f32[128,1024]{1,0:T(8,128)S(1)}, f32[128,1024]{1,0:T(8,128)S(1)}, u32[]{:S(2)}, u32[]{:S(2)}) collective-permute-start(f32[128,1024]{1,0:T(8,128)S(1)} %get-tuple-element.103), channel_id=1, source_target_pairs={{0,4},{4,8},{8,12},{12,16},{16,20},{20,24},{24,28},{1,5},{5,9},{9,... | collective-permute-start | bytes 1572872 | tf_op jit(solution)/shard_map/ppermute | solution.py:595
  134.5 34.3 %collective-permute-start.17 = (f32[128,1024]{1,0:T(8,128)S(1)}, f32[128,1024]{1,0:T(8,128)S(1)}, u32[]{:S(2)}, u32[]{:S(2)}) collective-permute-start(f32[128,1024]{1,0:T(8,128)S(1)} %get-tuple-element.104), channel_id=1, source_target_pairs={{4,0},{8,4},{12,8},{16,12},{20,16},{24,20},{28,24},{5,1},{9,5},{13... | collective-permute-start | bytes 1572872 | tf_op jit(solution)/shard_map/ppermute | solution.py:595
  139.1 55.3 %copy-start.10 = (bf16[64,1024]{1,0:T(8,128)(2,1)S(1)}, bf16[64,1024]{1,0:T(8,128)(2,1)}, u32[]{:S(2)}) copy-start(bf16[64,1024]{1,0:T(8,128)(2,1)} %get-tuple-element.81.refs_10_.refs_2_.target_ref) | copy-start | bytes 393220
  139.1 55.3 %copy-start.13 = (bf16[64,1024]{1,0:T(8,128)(2,1)S(1)}, bf16[64,1024]{1,0:T(8,128)(2,1)}, u32[]{:S(2)}) copy-start(bf16[64,1024]{1,0:T(8,128)(2,1)} %get-tuple-element.82.refs_11_.refs_3_.factor_ref) | copy-start | bytes 393220
  139.1 55.3 %copy-start.16 = (bf16[64,1024]{1,0:T(8,128)(2,1)S(1)}, bf16[64,1024]{1,0:T(8,128)(2,1)}, u32[]{:S(2)}) copy-start(bf16[64,1024]{1,0:T(8,128)(2,1)} %get-tuple-element.83.refs_12_.refs_4_.wall_ref) | copy-start | bytes 393220
  139.1 55.3 %copy-start.22 = (s32[32,128]{1,0:T(8,128)S(1)}, s32[32,128]{1,0:T(8,128)}, u32[]{:S(2)}) copy-start(s32[32,128]{1,0:T(8,128)} %get-tuple-element.64.kind_ref.refs_4_) | copy-start | bytes 49156
  139.1 55.3 %copy-start.30 = (s32[32,128]{1,0:T(8,128)S(1)}, s32[32,128]{1,0:T(8,128)}, u32[]{:S(2)}) copy-start(s32[32,128]{1,0:T(8,128)} %get-tuple-element.65.code_ref.refs_5_) | copy-start | bytes 49156
  139.1 55.3 %copy-start.35 = (bf16[64,256]{1,0:T(8,128)(2,1)S(1)}, bf16[64,256]{1,0:T(8,128)(2,1)}, u32[]{:S(2)}) copy-start(bf16[64,256]{1,0:T(8,128)(2,1)} %get-tuple-element.80.refs_9_.refs_1_.spread_ref) | copy-start | bytes 98308
  139.1 55.3 %copy-start.38 = (f32[32,128]{1,0:T(8,128)S(1)}, f32[32,128]{1,0:T(8,128)}, u32[]{:S(2)}) copy-start(f32[32,128]{1,0:T(8,128)} %get-tuple-element.77.refs_6_) | copy-start | bytes 49156
  170.7 67.5 %copy-start.3 = (bf16[1024,128]{1,0:T(8,128)(2,1)S(1)}, bf16[1024,128]{1,0:T(8,128)(2,1)}, u32[]{:S(2)}) copy-start(bf16[1024,128]{1,0:T(8,128)(2,1)} %get-tuple-element.66.sums_ref) | copy-start | bytes 786436
  170.7 67.5 %copy-start.7 = (f32[64,1024]{1,0:T(8,128)S(1)}, f32[64,1024]{1,0:T(8,128)}, u32[]{:S(2)}) copy-start(f32[64,1024]{1,0:T(8,128)} %get-tuple-element.67.stencil_ref) | copy-start | bytes 786436
  170.7 67.5 %copy-start.23 = (s32[32,128]{1,0:T(8,128)S(1)}, s32[32,128]{1,0:T(8,128)}, u32[]{:S(2)}) copy-start(s32[32,128]{1,0:T(8,128)} %get-tuple-element.64.kind_ref.refs_4_) | copy-start | bytes 49156
  170.7 67.5 %copy-start.31 = (s32[32,128]{1,0:T(8,128)S(1)}, s32[32,128]{1,0:T(8,128)}, u32[]{:S(2)}) copy-start(s32[32,128]{1,0:T(8,128)} %get-tuple-element.65.code_ref.refs_5_) | copy-start | bytes 49156
  177.2 6.0 %collective-permute-start.18 = (f32[112,128]{1,0:T(8,128)S(1)}, f32[112,128]{1,0:T(8,128)S(1)}, u32[]{:S(2)}, u32[]{:S(2)}) collective-permute-start(f32[112,128]{1,0:T(8,128)S(1)} %get-tuple-element.107), channel_id=1, source_target_pairs={{0,1},{1,2},{2,3},{3,0},{4,5},{5,6},{6,7},{7,4},{8,9},{9,10},{10,1... | collective-permute-start | bytes 172040 | tf_op jit(solution)/shard_map/ppermute | solution.py:600
  178.4 6.1 %collective-permute-start.19 = (f32[112,128]{1,0:T(8,128)S(1)}, f32[112,128]{1,0:T(8,128)S(1)}, u32[]{:S(2)}, u32[]{:S(2)}) collective-permute-start(f32[112,128]{1,0:T(8,128)S(1)} %get-tuple-element.108), channel_id=1, source_target_pairs={{0,2},{1,3},{2,0},{3,1},{4,6},{5,7},{6,4},{7,5},{8,10},{9,11},{10,... | collective-permute-start | bytes 172040 | tf_op jit(solution)/shard_map/ppermute | solution.py:600
  180.2 4.7 %collective-permute-start.20 = (f32[112,128]{1,0:T(8,128)S(1)}, f32[112,128]{1,0:T(8,128)S(1)}, u32[]{:S(2)}, u32[]{:S(2)}) collective-permute-start(f32[112,128]{1,0:T(8,128)S(1)} %get-tuple-element.109), channel_id=1, source_target_pairs={{0,3},{1,0},{2,1},{3,2},{4,7},{5,4},{6,5},{7,6},{8,11},{9,8},{10,9... | collective-permute-start | bytes 172040 | tf_op jit(solution)/shard_map/ppermute | solution.py:600
  187.1 6.1 %collective-permute-start.21 = (f32[80,128]{1,0:T(8,128)}, f32[80,128]{1,0:T(8,128)S(1)}, u32[]{:S(2)}, u32[]{:S(2)}) collective-permute-start(f32[80,128]{1,0:T(8,128)} %gas.6.refs_0_), channel_id=1, source_target_pairs={{0,1},{1,2},{2,3},{3,0},{4,5},{5,6},{6,7},{7,4},{8,9},{9,10},{10,1... | collective-permute-start | bytes 122888 | tf_op jit(solution)/shard_map/ppermute | solution.py:600
  187.9 6.0 %collective-permute-start.22 = (f32[80,128]{1,0:T(8,128)}, f32[80,128]{1,0:T(8,128)S(1)}, u32[]{:S(2)}, u32[]{:S(2)}) collective-permute-start(f32[80,128]{1,0:T(8,128)} %gas.6.refs_0_), channel_id=1, source_target_pairs={{0,2},{1,3},{2,0},{3,1},{4,6},{5,7},{6,4},{7,5},{8,10},{9,11},{10,... | collective-permute-start | bytes 122888 | tf_op jit(solution)/shard_map/ppermute | solution.py:600
  190.1 4.3 %collective-permute-start.23 = (f32[80,128]{1,0:T(8,128)}, f32[80,128]{1,0:T(8,128)S(1)}, u32[]{:S(2)}, u32[]{:S(2)}) collective-permute-start(f32[80,128]{1,0:T(8,128)} %gas.6.refs_0_), channel_id=1, source_target_pairs={{0,3},{1,0},{2,1},{3,2},{4,7},{5,4},{6,5},{7,6},{8,11},{9,8},{10,9... | collective-permute-start | bytes 122888 | tf_op jit(solution)/shard_map/ppermute | solution.py:600
  198.1 39.1 %collective-permute-start.24 = (f32[128,1024]{1,0:T(8,128)S(1)}, f32[128,1024]{1,0:T(8,128)S(1)}, u32[]{:S(2)}, u32[]{:S(2)}) collective-permute-start(f32[128,1024]{1,0:T(8,128)S(1)} %get-tuple-element.117), channel_id=1, source_target_pairs={{0,4},{4,8},{8,12},{12,16},{16,20},{20,24},{24,28},{1,5},{5,9},{9,... | collective-permute-start | bytes 1572872 | tf_op jit(solution)/shard_map/ppermute | solution.py:595
  200.1 37.2 %collective-permute-start.25 = (f32[128,1024]{1,0:T(8,128)S(1)}, f32[128,1024]{1,0:T(8,128)S(1)}, u32[]{:S(2)}, u32[]{:S(2)}) collective-permute-start(f32[128,1024]{1,0:T(8,128)S(1)} %get-tuple-element.118), channel_id=1, source_target_pairs={{4,0},{8,4},{12,8},{16,12},{20,16},{24,20},{28,24},{5,1},{9,5},{13... | collective-permute-start | bytes 1572872 | tf_op jit(solution)/shard_map/ppermute | solution.py:595
  204.6 57.9 %copy-start.24 = (s32[32,128]{1,0:T(8,128)S(1)}, s32[32,128]{1,0:T(8,128)}, u32[]{:S(2)}) copy-start(s32[32,128]{1,0:T(8,128)} %get-tuple-element.64.kind_ref.refs_4_) | copy-start | bytes 49156
  204.6 57.9 %copy-start.32 = (s32[32,128]{1,0:T(8,128)S(1)}, s32[32,128]{1,0:T(8,128)}, u32[]{:S(2)}) copy-start(s32[32,128]{1,0:T(8,128)} %get-tuple-element.65.code_ref.refs_5_) | copy-start | bytes 49156
  204.6 57.9 %copy-start.39 = (f32[32,128]{1,0:T(8,128)S(1)}, f32[32,128]{1,0:T(8,128)}, u32[]{:S(2)}) copy-start(f32[32,128]{1,0:T(8,128)} %get-tuple-element.77.refs_6_) | copy-start | bytes 49156
  245.3 6.0 %collective-permute-start.26 = (f32[112,128]{1,0:T(8,128)S(1)}, f32[112,128]{1,0:T(8,128)S(1)}, u32[]{:S(2)}, u32[]{:S(2)}) collective-permute-start(f32[112,128]{1,0:T(8,128)S(1)} %get-tuple-element.121), channel_id=1, source_target_pairs={{0,1},{1,2},{2,3},{3,0},{4,5},{5,6},{6,7},{7,4},{8,9},{9,10},{10,1... | collective-permute-start | bytes 172040 | tf_op jit(solution)/shard_map/ppermute | solution.py:600
  246.6 5.9 %collective-permute-start.27 = (f32[112,128]{1,0:T(8,128)S(1)}, f32[112,128]{1,0:T(8,128)S(1)}, u32[]{:S(2)}, u32[]{:S(2)}) collective-permute-start(f32[112,128]{1,0:T(8,128)S(1)} %get-tuple-element.122), channel_id=1, source_target_pairs={{0,2},{1,3},{2,0},{3,1},{4,6},{5,7},{6,4},{7,5},{8,10},{9,11},{10,... | collective-permute-start | bytes 172040 | tf_op jit(solution)/shard_map/ppermute | solution.py:600
  248.4 4.7 %collective-permute-start.28 = (f32[112,128]{1,0:T(8,128)S(1)}, f32[112,128]{1,0:T(8,128)S(1)}, u32[]{:S(2)}, u32[]{:S(2)}) collective-permute-start(f32[112,128]{1,0:T(8,128)S(1)} %get-tuple-element.123), channel_id=1, source_target_pairs={{0,3},{1,0},{2,1},{3,2},{4,7},{5,4},{6,5},{7,6},{8,11},{9,8},{10,9... | collective-permute-start | bytes 172040 | tf_op jit(solution)/shard_map/ppermute | solution.py:600
  255.3 6.1 %collective-permute-start.29 = (f32[80,128]{1,0:T(8,128)}, f32[80,128]{1,0:T(8,128)S(1)}, u32[]{:S(2)}, u32[]{:S(2)}) collective-permute-start(f32[80,128]{1,0:T(8,128)} %gas.7.refs_0_), channel_id=1, source_target_pairs={{0,1},{1,2},{2,3},{3,0},{4,5},{5,6},{6,7},{7,4},{8,9},{9,10},{10,1... | collective-permute-start | bytes 122888 | tf_op jit(solution)/shard_map/ppermute | solution.py:600
  256.1 6.0 %collective-permute-start.30 = (f32[80,128]{1,0:T(8,128)}, f32[80,128]{1,0:T(8,128)S(1)}, u32[]{:S(2)}, u32[]{:S(2)}) collective-permute-start(f32[80,128]{1,0:T(8,128)} %gas.7.refs_0_), channel_id=1, source_target_pairs={{0,2},{1,3},{2,0},{3,1},{4,6},{5,7},{6,4},{7,5},{8,10},{9,11},{10,... | collective-permute-start | bytes 122888 | tf_op jit(solution)/shard_map/ppermute | solution.py:600
  258.2 4.3 %collective-permute-start.31 = (f32[80,128]{1,0:T(8,128)}, f32[80,128]{1,0:T(8,128)S(1)}, u32[]{:S(2)}, u32[]{:S(2)}) collective-permute-start(f32[80,128]{1,0:T(8,128)} %gas.7.refs_0_), channel_id=1, source_target_pairs={{0,3},{1,0},{2,1},{3,2},{4,7},{5,4},{6,5},{7,6},{8,11},{9,8},{10,9... | collective-permute-start | bytes 122888 | tf_op jit(solution)/shard_map/ppermute | solution.py:600
  (44 other events, 352.5 us)

commit v6 on v5

--- a/solution.py
+++ b/solution.py
@@ -36,8 +36,8 @@
 COEF = 2 * PART
 STRIDE = COEF + 1
 
-VMEM_LIMIT = 60 * 1024 * 1024
-SMALL_LIMIT = 52 * 1024 * 1024
+VMEM_LIMIT = 50 * 1024 * 1024
+SMALL_LIMIT = 24 * 1024 * 1024
 
 
 def setup_kernel(span, kind_in_ref, code_in_ref, temp_in_ref, kind_ref, code_ref, temp_ref, target_ref, factor_ref, wall_ref, sums_ref, stencil_ref, spread_ref,
@@ -337,12 +337,24 @@
     return jnp.concatenate(parts, axis=1)
 
 
-def relax_block(spread_ref, tables, coef_ref, even_ref, flat_ref, store):
-    even_ref[...] = dot(coef_ref[...], spread_ref[...])
-    for l in range(flat_ref.shape[1] // WIDE):
-        columns = slice(l * WIDE, (l + 1) * WIDE)
-        target, factor, wall = (ref[:, columns] for ref in tables)
-        store(l, relaxed(coef_ref[...], even_ref, flat_ref[:, columns], target, factor, wall))
+CELLS = 512
+
+
+def relax_tiles(cells, spread_ref, tables, coef_ref, even_ref, flat_ref, store):
+    target_ref, factor_ref, wall_ref = tables
+    span = flat_ref.shape[1]
+
+    def block(b, carry):
+        start = pl.multiple_of(b * CELLS, CELLS)
+        coef = coef_ref[pl.ds(start, CELLS), :]
+        even_ref[...] = dot(coef, spread_ref[...])
+        for l in range(span // WIDE):
+            columns = slice(l * WIDE, (l + 1) * WIDE)
+            store(start, l, relaxed(coef, even_ref, flat_ref[pl.ds(start, CELLS), columns],
+                                    target_ref[:, columns], factor_ref[:, columns], wall_ref[:, columns]))
+        return carry
+
+    lax.fori_loop(0, cells // CELLS, block, 0)
 
 
 PAD = 8
@@ -352,7 +364,7 @@
 def transport(exact, rows, field_ref, base, ncols, group, kind_ref, code_ref, sums_ref, stencil_ref,
               out_ref, parts_ref, strip_ref, half_ref):
     span = out_ref.shape[1]
-    nothing = jnp.minimum(lax.axis_index("vel"), 0)
+    nothing = jnp.minimum(pl.program_id(0) if rows == BLOCK else lax.axis_index("vel"), 0)
     shape = (ncols // 8, 8, LANES)
     unrolled = rows == BLOCK
 
@@ -425,9 +437,21 @@
 END = 2
 
 
+def patch(i, blocks, flat_ref, first_ref, last_ref):
+    edge = first_ref.shape[0]
+
+    @pl.when(i == 0)
+    def _():
+        flat_ref[:edge, :] = first_ref[...]
+
+    @pl.when(i == blocks - 1)
+    def _():
+        flat_ref[flat_ref.shape[0] - edge:, :] = last_ref[...]
+
+
 def inner_kernel(relax, exact, blocks, ncols, flat_ref, kind_ref, code_ref, sums_ref, stencil_ref, *refs):
     if relax:
-        coef_ref, spread_ref, target_ref, factor_ref, wall_ref, *refs = refs
+        coef_ref, spread_ref, target_ref, factor_ref, wall_ref, first_ref, last_ref, *refs = refs
     out_ref, parts_ref, head_ref, tail_ref, field_ref, even_ref, strip_ref, half_ref = refs
     i = pl.program_id(0)
     block = BLOCK * ncols
@@ -443,13 +467,13 @@
 
     @pl.when(i < blocks)
     def _():
-        here = pl.ds(pl.multiple_of(edge + i * block, edge), block)
-
         if relax:
-            def store(l, values):
-                field_ref[here, l * WIDE:(l + 1) * WIDE] = values
-
-            relax_block(spread_ref, (target_ref, factor_ref, wall_ref), coef_ref, even_ref, flat_ref, store)
+            def store(start, l, values):
+                cells = pl.ds(pl.multiple_of(edge + i * block + start, edge), CELLS)
+                field_ref[cells, l * WIDE:(l + 1) * WIDE] = values
+
+            patch(i, blocks, flat_ref, first_ref, last_ref)
+            relax_tiles(block, spread_ref, (target_ref, factor_ref, wall_ref), coef_ref, even_ref, flat_ref, store)
         else:
             for l in range(span // WIDE):
                 columns = slice(l * WIDE, (l + 1) * WIDE)
@@ -470,10 +494,10 @@
         tail_ref[...] = field_ref[last - size:last, :]
 
 
-def outer_kernel(relax, exact, ncols, count, flat_ref, given_ref, head_ref, tail_ref, low_ref, high_ref,
-                 kind_ref, code_ref, sums_ref, stencil_ref, out_ref, first_ref, last_ref, *refs):
+def outer_kernel(relax, exact, ncols, count, given_ref, head_ref, tail_ref, low_ref, high_ref,
+                 kind_ref, code_ref, sums_ref, stencil_ref, first_ref, last_ref, *refs):
     slot_refs = refs[:count]
-    parts_ref, field_ref, strip_ref, half_ref, done_ref = refs[count:]
+    parts_ref, field_ref, strip_ref, half_ref = refs[count:]
     edge = END * ncols
     size = head_ref.shape[0]
     span = first_ref.shape[1]
@@ -491,23 +515,17 @@
     field_ref[edge:edge + size, :] = head_ref[...]
     field_ref[edge + size:edge + 2 * size, :] = tail_ref[...]
     halo(high_ref, edge + 2 * size)
-    copies = []
-    for k, (ref, base, group, start) in enumerate((
-            (first_ref, 0, 0, 0), (last_ref, edge + size, groups - edge // LANES, out_ref.shape[0] - edge))):
+    for ref, base, group in ((first_ref, 0, 0), (last_ref, edge + size, groups - edge // LANES)):
         transport(exact, END, field_ref, base, ncols, group, kind_ref, code_ref,
                   sums_ref, stencil_ref, ref, parts_ref, strip_ref, half_ref)
-        copies.append(pltpu.make_async_copy(ref, out_ref.at[pl.ds(start, edge), :], done_ref.at[k]))
-        copies[-1].start()
     me = lax.axis_index("vel")
     rows = slot_refs[0].shape[0]
     for away, ref in enumerate(slot_refs):
         owner = lax.rem(me + away, count)
         ref[...] = parts_ref[pl.ds(pl.multiple_of(owner * rows, 4), rows), :]
-    for copy in copies:
-        copy.wait()
-
-
-def inner(relax, exact, flat, coef, kind, code, spread, tables, sums, stencil, ncols):
+
+
+def inner(relax, exact, flat, first, last, coef, kind, code, spread, tables, sums, stencil, ncols):
     cells, span = flat.shape
     block = BLOCK * ncols
     blocks = cells // block
@@ -517,8 +535,8 @@
     operands = [flat, kind, code, sums, stencil]
     in_specs = [pl.BlockSpec((block, span), lambda i: (jnp.minimum(i, blocks - 1), 0))] + [whole] * 4
     if relax:
-        operands += [coef, spread, *tables]
-        in_specs += [pl.BlockSpec((block, COEF), lambda i: (jnp.minimum(i, blocks - 1), 0))] + [whole] * 4
+        operands += [coef, spread, *tables, first, last]
+        in_specs += [pl.BlockSpec((block, COEF), lambda i: (jnp.minimum(i, blocks - 1), 0))] + [whole] * 6
     return pl.pallas_call(
         functools.partial(inner_kernel, relax, exact, blocks, ncols),
         grid=(blocks + 1,),
@@ -537,55 +555,56 @@
     )(*operands)
 
 
-def outer(relax, exact, flat, parts, head, tail, low, high, kind, code, sums, stencil, ncols):
-    cells, span = flat.shape
+def outer(relax, exact, parts, head, tail, low, high, kind, code, sums, stencil, ncols):
+    span = head.shape[1]
     edge = END * ncols
     count = lax.axis_size("vel")
     whole = pl.BlockSpec(memory_space=pltpu.VMEM)
     slot = jax.ShapeDtypeStruct((parts.shape[0] // count, LANES), jnp.float32)
     rim = jax.ShapeDtypeStruct((edge, span), jnp.float32)
-    flat, first, last, *slots = pl.pallas_call(
+    first, last, *slots = pl.pallas_call(
         functools.partial(outer_kernel, relax, exact, ncols, count),
-        out_shape=(jax.ShapeDtypeStruct((cells, span), jnp.float32), rim, rim) + (slot,) * count,
-        in_specs=[pl.BlockSpec(memory_space=pl.ANY)] + [whole] * 9,
-        out_specs=(pl.BlockSpec(memory_space=pl.ANY),) + (whole,) * (count + 2),
+        out_shape=(rim, rim) + (slot,) * count,
+        in_specs=[whole] * 9,
+        out_specs=(whole,) * (count + 2),
         scratch_shapes=[pltpu.VMEM(parts.shape, jnp.float32),
                         pltpu.VMEM((6 * edge, span), jnp.float32),
                         pltpu.VMEM((WIDE // LANES * BLOCK, ncols + 2 * PAD, LANES), jnp.float32),
-                        pltpu.VMEM((1 + exact, edge, span), jnp.bfloat16),
-                        pltpu.SemaphoreType.DMA((2,))],
-        input_output_aliases={0: 0},
+                        pltpu.VMEM((1 + exact, edge, span), jnp.bfloat16)],
         compiler_params=pltpu.CompilerParams(vmem_limit_bytes=SMALL_LIMIT),
         name="outer" if relax else "outer_first",
-    )(flat, parts, head, tail, low, high, kind, code, sums, stencil)
-    return flat, first, last, slots
-
-
-def last_kernel(flat_ref, coef_ref, spread_ref, target_ref, factor_ref, wall_ref, out_ref, even_ref):
+    )(parts, head, tail, low, high, kind, code, sums, stencil)
+    return first, last, slots
+
+
+def last_kernel(blocks, flat_ref, coef_ref, spread_ref, target_ref, factor_ref, wall_ref, first_ref, last_ref,
+                out_ref, even_ref):
     span = flat_ref.shape[1]
 
-    def store(l, values):
-        out_ref[:, l * WIDE:(l + 1) * WIDE] = turned(values, l, span, back=True)
-
-    relax_block(spread_ref, (target_ref, factor_ref, wall_ref), coef_ref, even_ref, flat_ref, store)
-
-
-def finish(flat, coef, spread, tables, ncols):
+    def store(start, l, values):
+        out_ref[pl.ds(start, CELLS), l * WIDE:(l + 1) * WIDE] = turned(values, l, span, back=True)
+
+    patch(pl.program_id(0), blocks, flat_ref, first_ref, last_ref)
+    relax_tiles(flat_ref.shape[0], spread_ref, (target_ref, factor_ref, wall_ref), coef_ref, even_ref,
+                flat_ref, store)
+
+
+def finish(flat, first, last, coef, spread, tables, ncols):
     cells, span = flat.shape
     block = 8 * ncols
     whole = pl.BlockSpec(memory_space=pltpu.VMEM)
     return pl.pallas_call(
-        last_kernel,
+        functools.partial(last_kernel, cells // block),
         grid=(cells // block,),
         out_shape=jax.ShapeDtypeStruct((cells, span), jnp.float32),
         in_specs=[pl.BlockSpec((block, span), lambda i: (i, 0)),
                   pl.BlockSpec((block, COEF), lambda i: (i, 0)),
-                  whole, whole, whole, whole],
+                  whole, whole, whole, whole, whole, whole],
         out_specs=pl.BlockSpec((block, span), lambda i: (i, 0)),
         scratch_shapes=[pltpu.VMEM((block, 2 * LANES), jnp.float32)],
         compiler_params=pltpu.CompilerParams(vmem_limit_bytes=VMEM_LIMIT),
         name="finish",
-    )(flat, coef, spread, *tables)
+    )(flat, coef, spread, *tables, first, last)
 
 
 def exchange(first, last):
@@ -608,19 +627,19 @@
     kind, code, temp, target, factor, wall, sums, stencil, spread = setup(span, cell_kind, normal_code, wall_temp)
     tables = (target, factor, wall)
     edge = 2 * ncols
-    coef = None
+    coef = first = last = None
     low, high = flat[:edge], flat[cells - edge:]
     for step in range(STEPS):
         final = step == STEPS - 1
         low, high = exchange(low, high)
-        flat, parts, head, tail = inner(step > 0, final, flat, coef, kind, code, spread, tables, sums, stencil, ncols)
-        flat, first, last, slots = outer(step > 0, final, flat, parts, head, tail, low, high, kind, code, sums, stencil, ncols)
+        flat, parts, head, tail = inner(step > 0, final, flat, first, last, coef, kind, code, spread, tables, sums, stencil, ncols)
+        first, last, slots = outer(step > 0, final, parts, head, tail, low, high, kind, code, sums, stencil, ncols)
         own = gas(swap(slots), kind, code, temp)
         coef, *others = state(not final, swap([own] * len(slots)), kind, code, temp, first, last, spread, tables)
         if not final:
             low, high = others
     flux = others[0]
-    current = finish(flat, coef, spread, tables, ncols)
+    current = finish(flat, first, last, coef, spread, tables, ncols)
     columns = ncols // lax.axis_size("vel")
     own_flux = lax.dynamic_slice_in_dim(flux.reshape(nrows, ncols), lax.axis_index("vel") * columns, columns, 1)
     return current.reshape(nrows, ncols, span), own_flux

time: 285 us -> 253 us (0.89)
  Pallas kernels: 174 us -> 143 us
    pallas_call x4, Pallas kernels: 20.7 us -> 7.4 us  [outer(): pl.pallas_call(functools.partial(outer_kernel, relax, exact, ncols, count...]
    pallas_call x4, Pallas kernels: 118 us -> 105 us  [inner(): pl.pallas_call(functools.partial(inner_kernel, relax, exact, blocks, ncol...]
    pallas_call x4, Pallas kernels: 9.64 us -> 4.89 us  [state(): pl.pallas_call(functools.partial(state_kernel, len(pieces), groups, with_...]
    unnamed x153 -> x97, local copies, waits for them, and re-layouts: 19.7 us -> 18.6 us
  transfers between devices with their start and end apart: 32 -> 32, of which waited for: 24 -> 24; matrix products, arithmetic and copies ran while one was open for 0% -> 0% of each run, Pallas kernels for 42% -> 43%
where the time goes in v6:
time: 253 us; the launch traced here: 251 us
  Pallas kernels  143 us (57%)
  starting transfers between devices  58.5 us (23%)
  waiting for transfers between devices  28.5 us (11%)
  local copies, waits for them, and re-layouts  20.1 us (8%)
    pallas_call x4, Pallas kernels, inner(): pl.pallas_call(functools.partial(inner_kernel, relax, exact, blocks, ncol...  105 us
    ppermute x24, starting transfers between devices, swap(): lax.ppermute(slots[k], 'vel', [(i, (i + k) % count) for i in range(count)])  32.5 us
    ppermute x24, waiting for transfers between devices, swap(): lax.ppermute(slots[k], 'vel', [(i, (i + k) % count) for i in range(count)])  28.5 us
    ppermute x8, starting transfers between devices, exchange(): return (lax.ppermute(last, 'space', up), lax.ppermute(first, 'space', down))  26 us
    unnamed x97, local copies, waits for them, and re-layouts  18.6 us
    pallas_call x1, Pallas kernels, finish(): pl.pallas_call(functools.partial(last_kernel, cells // block), grid=(cell...  17.2 us
    pallas_call x4, Pallas kernels, outer(): pl.pallas_call(functools.partial(outer_kernel, relax, exact, ncols, count...  7.4 us
    pallas_call x4, Pallas kernels, gas(): pl.pallas_call(functools.partial(gas_kernel, len(parts), size), out_shape...  6.37 us
  transfers between devices with their start and end apart: 32, of which 24 were waited for; matrix products, arithmetic and copies ran while one was open for 0% of the time, Pallas kernels for 43%

profile of v6, /device:TPU:4, one launch (start us, length us, event | category | flops | bytes accessed | tf_op | source)
XLA Modules:
  0.0 251.3 jit_solution(14784163195628010816)
XLA Ops:
  0.6 1.3 fusion
  1.9 1.9 collective-permute-start
  3.9 4.5 %collective-permute-start.1 = (f32[128,1024]{1,0:T(8,128)S(1)}, f32[128,1024]{1,0:T(8,128)S(1)}, u32[]{:S(2)}, u32[]{:S(2)}) collective-permute-start(f32[128,1024]{1,0:T(8,128)S(1)} %bitcast.6), channel_id=1, source_target_pairs={{4,0},{8,4},{12,8},{16,12},{20,16},{24,20},{28,24},{5,1},{9,5},{13... | collective-permute-start | bytes 1572872 | tf_op jit(solution)/shard_map/ppermute | solution.py:614
  8.4 1.9 setup.1
  10.3 0.9 copy-done
  11.3 0.9 copy-done.2
  13.7 22.8 %inner_first.1 = (f32[4096,1024]{1,0:T(8,128)}, f32[448,128]{1,0:T(8,128)S(1)}, f32[256,1024]{1,0:T(8,128)S(1)}, f32[256,1024]{1,0:T(8,128)S(1)}) custom-call(f32[4096,1024]{1,0:T(8,128)} %bitcast.4, s32[32,128]{1,0:T(8,128)S(1)} %copy-done.7, s32[32,128]{1,0:T(8,128)S(1)} %copy-done.12, bf16[1024,128]{1,0:T(8,128)(2,1)S(1)} %copy-done, f32[64,1024]{1,0:T(8,128)S(1)} %copy-done.2), custom_call_target="tpu_custom_call" | custom-call | flops 3221225472 | bytes 33554432 | tf_op jit(solution)/shard_map/inner_first/pallas_call | solution.py:540
  36.6 1.9 outer_first.1
  39.1 1.6 collective-permute-start.2
  40.7 2.6 %collective-permute-start.3 = (f32[112,128]{1,0:T(8,128)S(1)}, f32[112,128]{1,0:T(8,128)S(1)}, u32[]{:S(2)}, u32[]{:S(2)}) collective-permute-start(f32[112,128]{1,0:T(8,128)S(1)} %get-tuple-element.72), channel_id=1, source_target_pairs={{0,2},{1,3},{2,0},{3,1},{4,6},{5,7},{6,4},{7,5},{8,10},{9,11},{10,... | collective-permute-start | bytes 172040 | tf_op jit(solution)/shard_map/ppermute | solution.py:619
  43.3 1.3 collective-permute-start.4
  44.6 1.0 collective-permute-done.2.refs_1_
  45.6 1.4 collective-permute-done.3.refs_2_
  48.1 1.6 gas.4.refs_0_
  50.3 3.0 %collective-permute-start.6 = (f32[80,128]{1,0:T(8,128)}, f32[80,128]{1,0:T(8,128)S(1)}, u32[]{:S(2)}, u32[]{:S(2)}) collective-permute-start(f32[80,128]{1,0:T(8,128)} %gas.4.refs_0_), channel_id=1, source_target_pairs={{0,2},{1,3},{2,0},{3,1},{4,6},{5,7},{6,4},{7,5},{8,10},{9,11},{10,... | collective-permute-start | bytes 122888 | tf_op jit(solution)/shard_map/ppermute | solution.py:619
  53.6 2.3 collective-permute-done.5.refs_1_
  56.5 1.1 collective-permute-done.7.refs_3_
  58.4 1.4 state.4
  59.8 1.0 copy-done.22
  60.8 1.9 collective-permute-start.8
  62.7 4.5 %collective-permute-start.9 = (f32[128,1024]{1,0:T(8,128)S(1)}, f32[128,1024]{1,0:T(8,128)S(1)}, u32[]{:S(2)}, u32[]{:S(2)}) collective-permute-start(f32[128,1024]{1,0:T(8,128)S(1)} %get-tuple-element.87), channel_id=1, source_target_pairs={{4,0},{8,4},{12,8},{16,12},{20,16},{24,20},{28,24},{5,1},{9,5},{13... | collective-permute-start | bytes 1572872 | tf_op jit(solution)/shard_map/ppermute | solution.py:614
  67.2 26.5 %inner.3 = (f32[4096,1024]{1,0:T(8,128)}, f32[448,128]{1,0:T(8,128)S(1)}, f32[256,1024]{1,0:T(8,128)S(1)}, f32[256,1024]{1,0:T(8,128)}) custom-call(f32[4096,1024]{1,0:T(8,128)} %get-tuple-element.66.flat_ref, s32[32,128]{1,0:T(8,128)S(1)} %copy-done.8, s32[32,128]{1,0:T(8,128)S(1)} %copy-done.13, bf16[1024,128]{1,0:T(8,128)(2,1)S(1)} %copy-done.1, ...), custom_call_target="tpu_custom_call" | custom-call | flops 3221225472 | bytes 33554432 | tf_op jit(solution)/shard_map/inner/pallas_call | solution.py:540
  93.7 1.2 copy-done.26
  95.0 1.7 outer.3
  98.1 2.0 collective-permute-start.11
  100.1 1.1 collective-permute-start.12
  101.2 2.2 collective-permute-done.10.refs_1_
  103.4 1.1 collective-permute-done.11.refs_2_
  105.3 1.6 gas.5.refs_0_
  106.9 1.2 collective-permute-start.13
  108.1 2.0 collective-permute-start.14
  110.7 2.2 collective-permute-done.13.refs_1_
  115.1 1.4 state.5
  116.5 1.0 copy-done.23
  117.5 1.9 collective-permute-start.16
  119.4 4.7 %collective-permute-start.17 = (f32[128,1024]{1,0:T(8,128)S(1)}, f32[128,1024]{1,0:T(8,128)S(1)}, u32[]{:S(2)}, u32[]{:S(2)}) collective-permute-start(f32[128,1024]{1,0:T(8,128)S(1)} %get-tuple-element.100), channel_id=1, source_target_pairs={{4,0},{8,4},{12,8},{16,12},{20,16},{24,20},{28,24},{5,1},{9,5},{13... | collective-permute-start | bytes 1572872 | tf_op jit(solution)/shard_map/ppermute | solution.py:614
  124.1 26.5 %inner.4 = (f32[4096,1024]{1,0:T(8,128)}, f32[448,128]{1,0:T(8,128)S(1)}, f32[256,1024]{1,0:T(8,128)S(1)}, f32[256,1024]{1,0:T(8,128)}) custom-call(f32[4096,1024]{1,0:T(8,128)} %get-tuple-element.82.flat_ref, s32[32,128]{1,0:T(8,128)S(1)} %copy-done.9, s32[32,128]{1,0:T(8,128)S(1)} %copy-done.14, bf16[1024,128]{1,0:T(8,128)(2,1)S(1)} %copy-done.1, ...), custom_call_target="tpu_custom_call" | custom-call | flops 3221225472 | bytes 33554432 | tf_op jit(solution)/shard_map/inner/pallas_call | solution.py:540
  150.7 1.2 copy-done.27
  151.9 1.7 outer.4
  154.3 1.1 collective-permute-start.18
  155.4 1.8 collective-permute-start.19
  157.2 1.0 collective-permute-start.20
  158.2 2.1 collective-permute-done.18.refs_1_
  160.3 1.3 collective-permute-done.19.refs_2_
  162.5 1.6 gas.6.refs_0_
  164.1 0.9 collective-permute-start.21
  165.1 2.2 collective-permute-start.22
  168.0 2.2 collective-permute-done.21.refs_1_
  172.3 1.4 state.6
  173.6 1.0 copy-done.24
  174.6 1.9 collective-permute-start.24
  176.5 4.5 %collective-permute-start.25 = (f32[128,1024]{1,0:T(8,128)S(1)}, f32[128,1024]{1,0:T(8,128)S(1)}, u32[]{:S(2)}, u32[]{:S(2)}) collective-permute-start(f32[128,1024]{1,0:T(8,128)S(1)} %get-tuple-element.113), channel_id=1, source_target_pairs={{4,0},{8,4},{12,8},{16,12},{20,16},{24,20},{28,24},{5,1},{9,5},{13... | collective-permute-start | bytes 1572872 | tf_op jit(solution)/shard_map/ppermute | solution.py:614
  181.1 29.5 %inner.5 = (f32[4096,1024]{1,0:T(8,128)}, f32[448,128]{1,0:T(8,128)S(1)}, f32[256,1024]{1,0:T(8,128)S(1)}, f32[256,1024]{1,0:T(8,128)}) custom-call(f32[4096,1024]{1,0:T(8,128)} %get-tuple-element.95.flat_ref, s32[32,128]{1,0:T(8,128)S(1)} %copy-done.10, s32[32,128]{1,0:T(8,128)S(1)} %copy-done.15, bf16[1024,128]{1,0:T(8,128)(2,1)S(1)} %copy-done.1, ...), custom_call_target="tpu_custom_call" | custom-call | flops 3221225472 | bytes 33554432 | tf_op jit(solution)/shard_map/inner/pallas_call | solution.py:540
  210.6 1.2 copy-done.25
  211.8 2.0 outer.5
  214.5 1.3 collective-permute-start.26
  215.8 1.8 collective-permute-start.27
  218.4 2.1 collective-permute-done.26.refs_1_
  220.5 1.3 collective-permute-done.27.refs_2_
  222.9 1.6 gas.7.refs_0_
  225.3 2.2 collective-permute-start.30
  227.4 0.9 collective-permute-start.31
  228.3 2.3 collective-permute-done.29.refs_1_
  234.1 17.2 %finish.1 = f32[4096,1024]{1,0:T(8,128)} custom-call(f32[4096,1024]{1,0:T(8,128)} %get-tuple-element.108.flat_ref, bf16[4096,64]{1,0:T(8,128)(2,1)S(1)} %get-tuple-element.118.coef_ref, bf16[64,256]{1,0:T(8,128)(2,1)S(1)} %copy-done.17, bf16[64,1024]{1,0:T(8,128)(2,1)S(1)} %copy-done.4, bf16[64,1024]{1,0:T(8,128)(2,1)S(1)} %copy-done.5, ...), custom_call_target="tpu_custom_call" | custom-call | tf_op jit(solution)/shard_map/finish/pallas_call | solution.py:596
  (118 shorter events, 21.5 us)
Async XLA Ops:
  1.9 34.6 %collective-permute-start = (f32[128,1024]{1,0:T(8,128)S(1)}, f32[128,1024]{1,0:T(8,128)S(1)}, u32[]{:S(2)}, u32[]{:S(2)}) collective-permute-start(f32[128,1024]{1,0:T(8,128)S(1)} %bitcast.7), channel_id=1, source_target_pairs={{0,4},{4,8},{8,12},{12,16},{16,20},{20,24},{24,28},{1,5},{5,9},{9,... | collective-permute-start | bytes 1572872 | tf_op jit(solution)/shard_map/ppermute | solution.py:614
  3.9 32.7 %collective-permute-start.1 = (f32[128,1024]{1,0:T(8,128)S(1)}, f32[128,1024]{1,0:T(8,128)S(1)}, u32[]{:S(2)}, u32[]{:S(2)}) collective-permute-start(f32[128,1024]{1,0:T(8,128)S(1)} %bitcast.6), channel_id=1, source_target_pairs={{4,0},{8,4},{12,8},{16,12},{20,16},{24,20},{28,24},{5,1},{9,5},{13... | collective-permute-start | bytes 1572872 | tf_op jit(solution)/shard_map/ppermute | solution.py:614
  10.3 1.0 copy-start
  11.3 0.9 copy-start.2
  13.6 43.9 %copy-start.4 = (bf16[64,1024]{1,0:T(8,128)(2,1)S(1)}, bf16[64,1024]{1,0:T(8,128)(2,1)}, u32[]{:S(2)}) copy-start(bf16[64,1024]{1,0:T(8,128)(2,1)} %get-tuple-element.78.refs_10_.refs_2_.target_ref) | copy-start | bytes 393220
  13.6 43.9 %copy-start.5 = (bf16[64,1024]{1,0:T(8,128)(2,1)S(1)}, bf16[64,1024]{1,0:T(8,128)(2,1)}, u32[]{:S(2)}) copy-start(bf16[64,1024]{1,0:T(8,128)(2,1)} %get-tuple-element.79.refs_11_.refs_3_.factor_ref) | copy-start | bytes 393220
  13.7 43.9 %copy-start.6 = (bf16[64,1024]{1,0:T(8,128)(2,1)S(1)}, bf16[64,1024]{1,0:T(8,128)(2,1)}, u32[]{:S(2)}) copy-start(bf16[64,1024]{1,0:T(8,128)(2,1)} %get-tuple-element.80.refs_12_.refs_4_.wall_ref) | copy-start | bytes 393220
  13.7 43.9 %copy-start.8 = (s32[32,128]{1,0:T(8,128)S(1)}, s32[32,128]{1,0:T(8,128)}, u32[]{:S(2)}) copy-start(s32[32,128]{1,0:T(8,128)} %get-tuple-element.62.kind_ref.refs_4_) | copy-start | bytes 49156
  13.7 43.9 %copy-start.13 = (s32[32,128]{1,0:T(8,128)S(1)}, s32[32,128]{1,0:T(8,128)}, u32[]{:S(2)}) copy-start(s32[32,128]{1,0:T(8,128)} %get-tuple-element.63.code_ref.refs_5_) | copy-start | bytes 49156
  13.7 43.9 %copy-start.17 = (bf16[64,256]{1,0:T(8,128)(2,1)S(1)}, bf16[64,256]{1,0:T(8,128)(2,1)}, u32[]{:S(2)}) copy-start(bf16[64,256]{1,0:T(8,128)(2,1)} %get-tuple-element.77.refs_9_.refs_1_.spread_ref) | copy-start | bytes 98308
  13.7 43.9 %copy-start.18 = (f32[32,128]{1,0:T(8,128)S(1)}, f32[32,128]{1,0:T(8,128)}, u32[]{:S(2)}) copy-start(f32[32,128]{1,0:T(8,128)} %get-tuple-element.74.refs_6_) | copy-start | bytes 49156
  13.7 53.5 %copy-start.1 = (bf16[1024,128]{1,0:T(8,128)(2,1)S(1)}, bf16[1024,128]{1,0:T(8,128)(2,1)}, u32[]{:S(2)}) copy-start(bf16[1024,128]{1,0:T(8,128)(2,1)} %get-tuple-element.64.sums_ref) | copy-start | bytes 786436
  13.7 53.5 %copy-start.3 = (f32[64,1024]{1,0:T(8,128)S(1)}, f32[64,1024]{1,0:T(8,128)}, u32[]{:S(2)}) copy-start(f32[64,1024]{1,0:T(8,128)} %get-tuple-element.65.stencil_ref) | copy-start | bytes 786436
  36.5 77.8 %copy-start.9 = (s32[32,128]{1,0:T(8,128)S(1)}, s32[32,128]{1,0:T(8,128)}, u32[]{:S(2)}) copy-start(s32[32,128]{1,0:T(8,128)} %get-tuple-element.62.kind_ref.refs_4_) | copy-start | bytes 49156
  36.5 77.8 %copy-start.14 = (s32[32,128]{1,0:T(8,128)S(1)}, s32[32,128]{1,0:T(8,128)}, u32[]{:S(2)}) copy-start(s32[32,128]{1,0:T(8,128)} %get-tuple-element.63.code_ref.refs_5_) | copy-start | bytes 49156
  36.5 77.8 %copy-start.19 = (f32[32,128]{1,0:T(8,128)S(1)}, f32[32,128]{1,0:T(8,128)}, u32[]{:S(2)}) copy-start(f32[32,128]{1,0:T(8,128)} %get-tuple-element.74.refs_6_) | copy-start | bytes 49156
  39.1 6.5 %collective-permute-start.2 = (f32[112,128]{1,0:T(8,128)S(1)}, f32[112,128]{1,0:T(8,128)S(1)}, u32[]{:S(2)}, u32[]{:S(2)}) collective-permute-start(f32[112,128]{1,0:T(8,128)S(1)} %get-tuple-element.71), channel_id=1, source_target_pairs={{0,1},{1,2},{2,3},{3,0},{4,5},{5,6},{6,7},{7,4},{8,9},{9,10},{10,1... | collective-permute-start | bytes 172040 | tf_op jit(solution)/shard_map/ppermute | solution.py:619
  40.7 6.4 %collective-permute-start.3 = (f32[112,128]{1,0:T(8,128)S(1)}, f32[112,128]{1,0:T(8,128)S(1)}, u32[]{:S(2)}, u32[]{:S(2)}) collective-permute-start(f32[112,128]{1,0:T(8,128)S(1)} %get-tuple-element.72), channel_id=1, source_target_pairs={{0,2},{1,3},{2,0},{3,1},{4,6},{5,7},{6,4},{7,5},{8,10},{9,11},{10,... | collective-permute-start | bytes 172040 | tf_op jit(solution)/shard_map/ppermute | solution.py:619
  43.3 4.3 %collective-permute-start.4 = (f32[112,128]{1,0:T(8,128)S(1)}, f32[112,128]{1,0:T(8,128)S(1)}, u32[]{:S(2)}, u32[]{:S(2)}) collective-permute-start(f32[112,128]{1,0:T(8,128)S(1)} %get-tuple-element.73), channel_id=1, source_target_pairs={{0,3},{1,0},{2,1},{3,2},{4,7},{5,4},{6,5},{7,6},{8,11},{9,8},{10,9... | collective-permute-start | bytes 172040 | tf_op jit(solution)/shard_map/ppermute | solution.py:619
  45.6 1.9 copy-start.36
  49.7 6.1 %collective-permute-start.5 = (f32[80,128]{1,0:T(8,128)}, f32[80,128]{1,0:T(8,128)S(1)}, u32[]{:S(2)}, u32[]{:S(2)}) collective-permute-start(f32[80,128]{1,0:T(8,128)} %gas.4.refs_0_), channel_id=1, source_target_pairs={{0,1},{1,2},{2,3},{3,0},{4,5},{5,6},{6,7},{7,4},{8,9},{9,10},{10,1... | collective-permute-start | bytes 122888 | tf_op jit(solution)/shard_map/ppermute | solution.py:619
  50.3 6.1 %collective-permute-start.6 = (f32[80,128]{1,0:T(8,128)}, f32[80,128]{1,0:T(8,128)S(1)}, u32[]{:S(2)}, u32[]{:S(2)}) collective-permute-start(f32[80,128]{1,0:T(8,128)} %gas.4.refs_0_), channel_id=1, source_target_pairs={{0,2},{1,3},{2,0},{3,1},{4,6},{5,7},{6,4},{7,5},{8,10},{9,11},{10,... | collective-permute-start | bytes 122888 | tf_op jit(solution)/shard_map/ppermute | solution.py:619
  53.4 4.2 %collective-permute-start.7 = (f32[80,128]{1,0:T(8,128)}, f32[80,128]{1,0:T(8,128)S(1)}, u32[]{:S(2)}, u32[]{:S(2)}) collective-permute-start(f32[80,128]{1,0:T(8,128)} %gas.4.refs_0_), channel_id=1, source_target_pairs={{0,3},{1,0},{2,1},{3,2},{4,7},{5,4},{6,5},{7,6},{8,11},{9,8},{10,9... | collective-permute-start | bytes 122888 | tf_op jit(solution)/shard_map/ppermute | solution.py:619
  57.6 0.8 copy-start.28
  59.8 1.0 copy-start.22
  60.8 33.0 %collective-permute-start.8 = (f32[128,1024]{1,0:T(8,128)S(1)}, f32[128,1024]{1,0:T(8,128)S(1)}, u32[]{:S(2)}, u32[]{:S(2)}) collective-permute-start(f32[128,1024]{1,0:T(8,128)S(1)} %get-tuple-element.86), channel_id=1, source_target_pairs={{0,4},{4,8},{8,12},{12,16},{16,20},{20,24},{24,28},{1,5},{5,9},{9,... | collective-permute-start | bytes 1572872 | tf_op jit(solution)/shard_map/ppermute | solution.py:614
  62.7 31.1 %collective-permute-start.9 = (f32[128,1024]{1,0:T(8,128)S(1)}, f32[128,1024]{1,0:T(8,128)S(1)}, u32[]{:S(2)}, u32[]{:S(2)}) collective-permute-start(f32[128,1024]{1,0:T(8,128)S(1)} %get-tuple-element.87), channel_id=1, source_target_pairs={{4,0},{8,4},{12,8},{16,12},{20,16},{24,20},{28,24},{5,1},{9,5},{13... | collective-permute-start | bytes 1572872 | tf_op jit(solution)/shard_map/ppermute | solution.py:614
  93.7 77.8 %copy-start.10 = (s32[32,128]{1,0:T(8,128)S(1)}, s32[32,128]{1,0:T(8,128)}, u32[]{:S(2)}) copy-start(s32[32,128]{1,0:T(8,128)} %get-tuple-element.62.kind_ref.refs_4_) | copy-start | bytes 49156
  93.7 77.8 %copy-start.15 = (s32[32,128]{1,0:T(8,128)S(1)}, s32[32,128]{1,0:T(8,128)}, u32[]{:S(2)}) copy-start(s32[32,128]{1,0:T(8,128)} %get-tuple-element.63.code_ref.refs_5_) | copy-start | bytes 49156
  93.7 77.8 %copy-start.20 = (f32[32,128]{1,0:T(8,128)S(1)}, f32[32,128]{1,0:T(8,128)}, u32[]{:S(2)}) copy-start(f32[32,128]{1,0:T(8,128)} %get-tuple-element.74.refs_6_) | copy-start | bytes 49156
  93.7 1.2 copy-start.26
  97.3 6.1 %collective-permute-start.10 = (f32[112,128]{1,0:T(8,128)S(1)}, f32[112,128]{1,0:T(8,128)S(1)}, u32[]{:S(2)}, u32[]{:S(2)}) collective-permute-start(f32[112,128]{1,0:T(8,128)S(1)} %get-tuple-element.89), channel_id=1, source_target_pairs={{0,1},{1,2},{2,3},{3,0},{4,5},{5,6},{6,7},{7,4},{8,9},{9,10},{10,1... | collective-permute-start | bytes 172040 | tf_op jit(solution)/shard_map/ppermute | solution.py:619
  98.1 6.4 %collective-permute-start.11 = (f32[112,128]{1,0:T(8,128)S(1)}, f32[112,128]{1,0:T(8,128)S(1)}, u32[]{:S(2)}, u32[]{:S(2)}) collective-permute-start(f32[112,128]{1,0:T(8,128)S(1)} %get-tuple-element.90), channel_id=1, source_target_pairs={{0,2},{1,3},{2,0},{3,1},{4,6},{5,7},{6,4},{7,5},{8,10},{9,11},{10,... | collective-permute-start | bytes 172040 | tf_op jit(solution)/shard_map/ppermute | solution.py:619
  100.1 4.6 %collective-permute-start.12 = (f32[112,128]{1,0:T(8,128)S(1)}, f32[112,128]{1,0:T(8,128)S(1)}, u32[]{:S(2)}, u32[]{:S(2)}) collective-permute-start(f32[112,128]{1,0:T(8,128)S(1)} %get-tuple-element.91), channel_id=1, source_target_pairs={{0,3},{1,0},{2,1},{3,2},{4,7},{5,4},{6,5},{7,6},{8,11},{9,8},{10,9... | collective-permute-start | bytes 172040 | tf_op jit(solution)/shard_map/ppermute | solution.py:619
  103.4 1.3 copy-start.37
  106.9 6.0 %collective-permute-start.13 = (f32[80,128]{1,0:T(8,128)}, f32[80,128]{1,0:T(8,128)S(1)}, u32[]{:S(2)}, u32[]{:S(2)}) collective-permute-start(f32[80,128]{1,0:T(8,128)} %gas.5.refs_0_), channel_id=1, source_target_pairs={{0,1},{1,2},{2,3},{3,0},{4,5},{5,6},{6,7},{7,4},{8,9},{9,10},{10,1... | collective-permute-start | bytes 122888 | tf_op jit(solution)/shard_map/ppermute | solution.py:619
  108.1 5.7 %collective-permute-start.14 = (f32[80,128]{1,0:T(8,128)}, f32[80,128]{1,0:T(8,128)S(1)}, u32[]{:S(2)}, u32[]{:S(2)}) collective-permute-start(f32[80,128]{1,0:T(8,128)} %gas.5.refs_0_), channel_id=1, source_target_pairs={{0,2},{1,3},{2,0},{3,1},{4,6},{5,7},{6,4},{7,5},{8,10},{9,11},{10,... | collective-permute-start | bytes 122888 | tf_op jit(solution)/shard_map/ppermute | solution.py:619
  110.1 4.2 %collective-permute-start.15 = (f32[80,128]{1,0:T(8,128)}, f32[80,128]{1,0:T(8,128)S(1)}, u32[]{:S(2)}, u32[]{:S(2)}) collective-permute-start(f32[80,128]{1,0:T(8,128)} %gas.5.refs_0_), channel_id=1, source_target_pairs={{0,3},{1,0},{2,1},{3,2},{4,7},{5,4},{6,5},{7,6},{8,11},{9,8},{10,9... | collective-permute-start | bytes 122888 | tf_op jit(solution)/shard_map/ppermute | solution.py:619
  116.5 1.0 copy-start.23
  117.5 33.2 %collective-permute-start.16 = (f32[128,1024]{1,0:T(8,128)S(1)}, f32[128,1024]{1,0:T(8,128)S(1)}, u32[]{:S(2)}, u32[]{:S(2)}) collective-permute-start(f32[128,1024]{1,0:T(8,128)S(1)} %get-tuple-element.99), channel_id=1, source_target_pairs={{0,4},{4,8},{8,12},{12,16},{16,20},{20,24},{24,28},{1,5},{5,9},{9,... | collective-permute-start | bytes 1572872 | tf_op jit(solution)/shard_map/ppermute | solution.py:614
  119.4 31.3 %collective-permute-start.17 = (f32[128,1024]{1,0:T(8,128)S(1)}, f32[128,1024]{1,0:T(8,128)S(1)}, u32[]{:S(2)}, u32[]{:S(2)}) collective-permute-start(f32[128,1024]{1,0:T(8,128)S(1)} %get-tuple-element.100), channel_id=1, source_target_pairs={{4,0},{8,4},{12,8},{16,12},{20,16},{24,20},{28,24},{5,1},{9,5},{13... | collective-permute-start | bytes 1572872 | tf_op jit(solution)/shard_map/ppermute | solution.py:614
  150.6 81.0 %copy-start.11 = (s32[32,128]{1,0:T(8,128)S(1)}, s32[32,128]{1,0:T(8,128)}, u32[]{:S(2)}) copy-start(s32[32,128]{1,0:T(8,128)} %get-tuple-element.62.kind_ref.refs_4_) | copy-start | bytes 49156
  150.6 81.0 %copy-start.16 = (s32[32,128]{1,0:T(8,128)S(1)}, s32[32,128]{1,0:T(8,128)}, u32[]{:S(2)}) copy-start(s32[32,128]{1,0:T(8,128)} %get-tuple-element.63.code_ref.refs_5_) | copy-start | bytes 49156
  150.7 81.0 %copy-start.21 = (f32[32,128]{1,0:T(8,128)S(1)}, f32[32,128]{1,0:T(8,128)}, u32[]{:S(2)}) copy-start(f32[32,128]{1,0:T(8,128)} %get-tuple-element.74.refs_6_) | copy-start | bytes 49156
  150.7 1.2 copy-start.27
  154.3 6.0 %collective-permute-start.18 = (f32[112,128]{1,0:T(8,128)S(1)}, f32[112,128]{1,0:T(8,128)S(1)}, u32[]{:S(2)}, u32[]{:S(2)}) collective-permute-start(f32[112,128]{1,0:T(8,128)S(1)} %get-tuple-element.102), channel_id=1, source_target_pairs={{0,1},{1,2},{2,3},{3,0},{4,5},{5,6},{6,7},{7,4},{8,9},{9,10},{10,1... | collective-permute-start | bytes 172040 | tf_op jit(solution)/shard_map/ppermute | solution.py:619
  155.4 6.2 %collective-permute-start.19 = (f32[112,128]{1,0:T(8,128)S(1)}, f32[112,128]{1,0:T(8,128)S(1)}, u32[]{:S(2)}, u32[]{:S(2)}) collective-permute-start(f32[112,128]{1,0:T(8,128)S(1)} %get-tuple-element.103), channel_id=1, source_target_pairs={{0,2},{1,3},{2,0},{3,1},{4,6},{5,7},{6,4},{7,5},{8,10},{9,11},{10,... | collective-permute-start | bytes 172040 | tf_op jit(solution)/shard_map/ppermute | solution.py:619
  157.2 4.7 %collective-permute-start.20 = (f32[112,128]{1,0:T(8,128)S(1)}, f32[112,128]{1,0:T(8,128)S(1)}, u32[]{:S(2)}, u32[]{:S(2)}) collective-permute-start(f32[112,128]{1,0:T(8,128)S(1)} %get-tuple-element.104), channel_id=1, source_target_pairs={{0,3},{1,0},{2,1},{3,2},{4,7},{5,4},{6,5},{7,6},{8,11},{9,8},{10,9... | collective-permute-start | bytes 172040 | tf_op jit(solution)/shard_map/ppermute | solution.py:619
  160.3 1.6 copy-start.38
  164.1 6.1 %collective-permute-start.21 = (f32[80,128]{1,0:T(8,128)}, f32[80,128]{1,0:T(8,128)S(1)}, u32[]{:S(2)}, u32[]{:S(2)}) collective-permute-start(f32[80,128]{1,0:T(8,128)} %gas.6.refs_0_), channel_id=1, source_target_pairs={{0,1},{1,2},{2,3},{3,0},{4,5},{5,6},{6,7},{7,4},{8,9},{9,10},{10,1... | collective-permute-start | bytes 122888 | tf_op jit(solution)/shard_map/ppermute | solution.py:619
  165.1 6.0 %collective-permute-start.22 = (f32[80,128]{1,0:T(8,128)}, f32[80,128]{1,0:T(8,128)S(1)}, u32[]{:S(2)}, u32[]{:S(2)}) collective-permute-start(f32[80,128]{1,0:T(8,128)} %gas.6.refs_0_), channel_id=1, source_target_pairs={{0,2},{1,3},{2,0},{3,1},{4,6},{5,7},{6,4},{7,5},{8,10},{9,11},{10,... | collective-permute-start | bytes 122888 | tf_op jit(solution)/shard_map/ppermute | solution.py:619
  167.2 4.3 %collective-permute-start.23 = (f32[80,128]{1,0:T(8,128)}, f32[80,128]{1,0:T(8,128)S(1)}, u32[]{:S(2)}, u32[]{:S(2)}) collective-permute-start(f32[80,128]{1,0:T(8,128)} %gas.6.refs_0_), channel_id=1, source_target_pairs={{0,3},{1,0},{2,1},{3,2},{4,7},{5,4},{6,5},{7,6},{8,11},{9,8},{10,9... | collective-permute-start | bytes 122888 | tf_op jit(solution)/shard_map/ppermute | solution.py:619
  173.6 1.0 copy-start.24
  174.6 36.0 %collective-permute-start.24 = (f32[128,1024]{1,0:T(8,128)S(1)}, f32[128,1024]{1,0:T(8,128)S(1)}, u32[]{:S(2)}, u32[]{:S(2)}) collective-permute-start(f32[128,1024]{1,0:T(8,128)S(1)} %get-tuple-element.112), channel_id=1, source_target_pairs={{0,4},{4,8},{8,12},{12,16},{16,20},{20,24},{24,28},{1,5},{5,9},{9,... | collective-permute-start | bytes 1572872 | tf_op jit(solution)/shard_map/ppermute | solution.py:614
  176.5 34.1 %collective-permute-start.25 = (f32[128,1024]{1,0:T(8,128)S(1)}, f32[128,1024]{1,0:T(8,128)S(1)}, u32[]{:S(2)}, u32[]{:S(2)}) collective-permute-start(f32[128,1024]{1,0:T(8,128)S(1)} %get-tuple-element.113), channel_id=1, source_target_pairs={{4,0},{8,4},{12,8},{16,12},{20,16},{24,20},{28,24},{5,1},{9,5},{13... | collective-permute-start | bytes 1572872 | tf_op jit(solution)/shard_map/ppermute | solution.py:614
  210.6 1.2 copy-start.25
  214.5 6.0 %collective-permute-start.26 = (f32[112,128]{1,0:T(8,128)S(1)}, f32[112,128]{1,0:T(8,128)S(1)}, u32[]{:S(2)}, u32[]{:S(2)}) collective-permute-start(f32[112,128]{1,0:T(8,128)S(1)} %get-tuple-element.115), channel_id=1, source_target_pairs={{0,1},{1,2},{2,3},{3,0},{4,5},{5,6},{6,7},{7,4},{8,9},{9,10},{10,1... | collective-permute-start | bytes 172040 | tf_op jit(solution)/shard_map/ppermute | solution.py:619
  215.8 6.0 %collective-permute-start.27 = (f32[112,128]{1,0:T(8,128)S(1)}, f32[112,128]{1,0:T(8,128)S(1)}, u32[]{:S(2)}, u32[]{:S(2)}) collective-permute-start(f32[112,128]{1,0:T(8,128)S(1)} %get-tuple-element.116), channel_id=1, source_target_pairs={{0,2},{1,3},{2,0},{3,1},{4,6},{5,7},{6,4},{7,5},{8,10},{9,11},{10,... | collective-permute-start | bytes 172040 | tf_op jit(solution)/shard_map/ppermute | solution.py:619
  217.6 4.7 %collective-permute-start.28 = (f32[112,128]{1,0:T(8,128)S(1)}, f32[112,128]{1,0:T(8,128)S(1)}, u32[]{:S(2)}, u32[]{:S(2)}) collective-permute-start(f32[112,128]{1,0:T(8,128)S(1)} %get-tuple-element.117), channel_id=1, source_target_pairs={{0,3},{1,0},{2,1},{3,2},{4,7},{5,4},{6,5},{7,6},{8,11},{9,8},{10,9... | collective-permute-start | bytes 172040 | tf_op jit(solution)/shard_map/ppermute | solution.py:619
  220.5 1.8 copy-start.39
  224.5 6.1 %collective-permute-start.29 = (f32[80,128]{1,0:T(8,128)}, f32[80,128]{1,0:T(8,128)S(1)}, u32[]{:S(2)}, u32[]{:S(2)}) collective-permute-start(f32[80,128]{1,0:T(8,128)} %gas.7.refs_0_), channel_id=1, source_target_pairs={{0,1},{1,2},{2,3},{3,0},{4,5},{5,6},{6,7},{7,4},{8,9},{9,10},{10,1... | collective-permute-start | bytes 122888 | tf_op jit(solution)/shard_map/ppermute | solution.py:619
  225.3 6.0 %collective-permute-start.30 = (f32[80,128]{1,0:T(8,128)}, f32[80,128]{1,0:T(8,128)S(1)}, u32[]{:S(2)}, u32[]{:S(2)}) collective-permute-start(f32[80,128]{1,0:T(8,128)} %gas.7.refs_0_), channel_id=1, source_target_pairs={{0,2},{1,3},{2,0},{3,1},{4,6},{5,7},{6,4},{7,5},{8,10},{9,11},{10,... | collective-permute-start | bytes 122888 | tf_op jit(solution)/shard_map/ppermute | solution.py:619
  227.4 4.3 %collective-permute-start.31 = (f32[80,128]{1,0:T(8,128)}, f32[80,128]{1,0:T(8,128)S(1)}, u32[]{:S(2)}, u32[]{:S(2)}) collective-permute-start(f32[80,128]{1,0:T(8,128)} %gas.7.refs_0_), channel_id=1, source_target_pairs={{0,3},{1,0},{2,1},{3,2},{4,7},{5,4},{6,5},{7,6},{8,11},{9,8},{10,9... | collective-permute-start | bytes 122888 | tf_op jit(solution)/shard_map/ppermute | solution.py:619
  231.7 0.8 copy-start.31
  (16 other events, 10.4 us)
